TPU v7x, 128 devices: a whole 4x4x4 slice. The times are simulated.
128 devices in a mesh: context: 16 (over y, x), tensor: 8 (over z, core).
Axes of the slice: x: 4, y: 4, z: 4, core: 2. Of those that a mesh axis runs over, the one named last changes fastest.
Arguments:
- seq_inputs: bfloat16 [2, 8192, 8192], P(None, 'context', 'tensor'), may hold values from -6 to 6
- b_proj: bfloat16 [2, 8192, 2048], P(None, 'context', 'tensor'), may hold values from -1.796875 to 1.796875
- c_proj: bfloat16 [2, 8192, 2048], P(None, 'context', 'tensor'), may hold values from -1.796875 to 1.796875
- dt_raw: float32 [2, 128, 8192], P(None, 'tensor', 'context'), may hold values from -3 to 3
- dt_bias: float32 [128], P('tensor'), may hold values from -4 to -2
- a_log: float32 [128], P('tensor'), may hold values from -11 to 0
- d_skip: float32 [128], P('tensor'), may hold values from 0.5 to 1.5
- out_grad: bfloat16 [2, 8192, 8192], P(None, 'context', 'tensor'), may hold values from -6 to 6
- log_ratio: float32 [2, 8192], P(None, ('context', 'tensor')), may hold values from -0.15 to 0.15
- lengths: int32 [2], replicated, may hold values from 4096 to 8192, as said below
Outputs:
- grad_inputs: bfloat16 [2, 8192, 8192], P(None, 'context', 'tensor')
- grad_b: bfloat16 [2, 8192, 2048], P(None, 'context', 'tensor')
- grad_c: bfloat16 [2, 8192, 2048], P(None, 'context', 'tensor')
- grad_dt: float32 [2, 128, 8192], P(None, 'tensor', 'context')
- grad_a_log: float32 [128], P('tensor')
- grad_dt_bias: float32 [128], P('tensor')
- grad_skip: float32 [128], P('tensor')
Inputs may be any that keep to these rules, and one draw needn't show every extreme that they name: One of the two lengths is 8192, the other at least 4096.
All inputs are finite; a program needn't handle non-finite values.
Results may differ from a plain program's by a relative error of at most 0.0075.
Values sent between devices are 32-bit elements; how exact they have to be, the bound alone decides.
No kernel may reach another device: no remote copies, remote signals or barrier semaphores. Data moves between devices by JAX's collectives and lax.ppermute only.
A program may use at most 256 MiB of HBM per device.

v0:
```python
import jax
import jax.numpy as jnp
from jax import lax
from jax.sharding import PartitionSpec as P

HP = 64
NS = 256
QB = 256


BETA = 0.5
HIGH = lax.Precision.HIGHEST


def carried_in(value, axis, join, neutral):
    count, mine = (lax.axis_size(axis), lax.axis_index(axis))
    pieces = jax.tree.map(lambda part: lax.all_gather(part, axis), value)
    total = jax.tree.map(
        lambda part, zero: jnp.full_like(part, 0) + jnp.asarray(zero, part.dtype), value, neutral
    )

    def turn(position, total):
        longer = join(total, jax.tree.map(lambda part: part[position], pieces))
        return jax.tree.map(lambda new, old: jnp.where(position < mine, new, old), longer, total)

    return lax.fori_loop(0, count - 1, turn, total)


def shifted(block, axis, distance):
    devices = range(lax.axis_size(axis))
    route = [(i - distance, i) for i in devices if i - distance in devices]
    return lax.ppermute(block, axis, route)


def to_heads(values, num_groups):
    seq_count, tok_rows, head_count = values.shape
    shaped = values.reshape(seq_count, tok_rows, num_groups, head_count // num_groups)
    return jnp.transpose(shaped, (0, 2, 3, 1))


def from_heads(values):
    return jnp.transpose(values, (0, 3, 1, 2))[..., None]


def block_step(decay_rates, skip_gain, carry_state, inputs):
    x_block, b_block, c_block, step_block = inputs
    seq_count, tok_rows, row_width = x_block.shape
    num_groups = b_block.shape[-1] // NS
    per_group = decay_rates.shape[0] // num_groups
    x_five = x_block.reshape(seq_count, tok_rows, num_groups, per_group, HP)
    b_four = b_block.reshape(seq_count, tok_rows, num_groups, NS)
    c_four = c_block.reshape(seq_count, tok_rows, num_groups, NS)
    running = jnp.cumsum(to_heads(step_block * decay_rates, num_groups), axis=-1)
    step_heads = to_heads(step_block, num_groups)
    causal = jnp.arange(tok_rows)[:, None] >= jnp.arange(tok_rows)[None, :]
    spread = jnp.where(causal, running[..., :, None] - running[..., None, :], -jnp.inf)
    gram_block = jnp.einsum(
        "sqgn,skgn->sgqk",
        c_four.astype(jnp.bfloat16),
        b_four.astype(jnp.bfloat16),
        preferred_element_type=jnp.float32,
    )
    weights = (gram_block[:, :, None] * jnp.exp(spread) * step_heads[..., None, :]).astype(
        jnp.bfloat16
    )
    intra_out = jnp.einsum(
        "sgjqk,skgjp->sqgjp",
        weights,
        x_five.astype(jnp.bfloat16),
        preferred_element_type=jnp.float32,
    )
    carried = jnp.einsum("sqgn,sgjpn->sqgjp", c_four, carry_state, precision=HIGH) * from_heads(
        jnp.exp(running)
    )
    outputs = intra_out + carried + skip_gain.reshape(num_groups, per_group, 1) * x_five
    tail_decay = jnp.exp(running[..., -1:] - running) * step_heads
    fresh_state = jnp.einsum(
        "sqgjp,sqgn->sgjpn", x_five * from_heads(tail_decay), b_four, precision=HIGH
    )
    carry_state = jnp.exp(running[..., -1])[..., None, None] * carry_state + fresh_state
    return (carry_state, outputs.reshape(seq_count, tok_rows, row_width))


def scan_blocks(x_in, b_in, c_in, step_raw, bias_in, log_rate, skip_in, init_state):
    step_size = jax.nn.softplus(step_raw + bias_in)
    decay_rates = -jnp.exp(log_rate)
    seq_count, tok_rows, row_width = x_in.shape
    num_blocks = tok_rows // QB

    def to_blocks(array_in):
        return jnp.swapaxes(
            array_in.reshape((seq_count, num_blocks, QB) + array_in.shape[2:]), 0, 1
        )

    def block_fn(carry_state, inputs):
        return block_step(decay_rates, skip_in, carry_state, inputs)

    final_state, outputs = lax.scan(
        jax.checkpoint(block_fn),
        init_state,
        (to_blocks(x_in), to_blocks(b_in), to_blocks(c_in), to_blocks(step_size)),
    )
    return (jnp.swapaxes(outputs, 0, 1).reshape(seq_count, tok_rows, row_width), final_state)


def shard_state(x_in, b_in, step_raw, bias_in, log_rate):
    step_size = jax.nn.softplus(step_raw + bias_in)
    decay_rates = -jnp.exp(log_rate)
    seq_count, tok_rows, row_width = x_in.shape
    num_groups = b_in.shape[-1] // NS
    per_group = decay_rates.shape[0] // num_groups
    running = jnp.cumsum(to_heads(step_size * decay_rates, num_groups), axis=-1)
    tail_decay = jnp.exp(running[..., -1:] - running) * to_heads(step_size, num_groups)
    x_five = x_in.reshape(seq_count, tok_rows, num_groups, per_group, HP)
    b_four = b_in.reshape(seq_count, tok_rows, num_groups, NS)
    fresh_state = jnp.einsum(
        "sqgjp,sqgn->sgjpn", x_five * from_heads(tail_decay), b_four, precision=HIGH
    )
    return (fresh_state, jnp.exp(running[..., -1]))


def on_device(
    seq_inputs, b_proj, c_proj, dt_raw, dt_bias, a_log, d_skip, out_grad, log_ratio, lengths
):
    seq_count, tok_rows, row_width = seq_inputs.shape
    num_groups = b_proj.shape[-1] // NS
    per_group = dt_bias.shape[0] // num_groups
    ratio_rows = log_ratio.shape[1]
    ratio_pos = lax.axis_index(("context", "tensor")) * ratio_rows + jnp.arange(
        ratio_rows, dtype=jnp.int32
    )
    ratio_live = (ratio_pos[None, :] < lengths[:, None]).astype(jnp.float32)
    totals = lax.psum(jnp.sum(ratio_live * log_ratio, axis=1), ("context", "tensor"))
    seq_signs = jnp.where(jnp.arange(2, dtype=jnp.int32) == 0, -1.0, 1.0).astype(jnp.float32)
    margin = -jnp.sum(seq_signs * totals)
    seq_gate = seq_signs * BETA * jax.nn.sigmoid(-BETA * margin)
    token_pos = lax.axis_index("context") * tok_rows + jnp.arange(tok_rows, dtype=jnp.int32)
    live_mask = (token_pos[None, :] < lengths[:, None]).astype(jnp.float32)
    cotangent = seq_gate[:, None, None] * live_mask[:, :, None] * out_grad.astype(jnp.float32)
    x_full = seq_inputs.astype(jnp.float32)
    b_full = b_proj.astype(jnp.float32)
    c_full = c_proj.astype(jnp.float32)
    dt_rows = jnp.swapaxes(dt_raw, 1, 2)
    local_fresh, local_decay = shard_state(x_full, b_full, dt_rows, dt_bias, a_log)

    def chain_state(earlier_part, later_part):
        return (
            later_part[1][..., None, None] * earlier_part[0] + later_part[0],
            earlier_part[1] * later_part[1],
        )

    identity = (jnp.zeros_like(local_fresh), jnp.ones_like(local_decay))
    entering, _ = carried_in((local_fresh, local_decay), "context", chain_state, identity)

    def forward(x_in, b_in, c_in, step_raw, bias_in, log_rate, skip_in):
        return scan_blocks(x_in, b_in, c_in, step_raw, bias_in, log_rate, skip_in, entering)

    step_size = jax.nn.softplus(dt_rows + dt_bias)
    running = jnp.cumsum(to_heads(step_size * -jnp.exp(a_log), num_groups), axis=-1)
    cot_five = cotangent.reshape(seq_count, tok_rows, num_groups, per_group, HP)
    c_four = c_full.reshape(seq_count, tok_rows, num_groups, NS)
    pull_back = jnp.einsum(
        "sqgjp,sqgn->sgjpn", cot_five * from_heads(jnp.exp(running)), c_four, precision=HIGH
    )

    def relay_step(loop_step, leaving_now):
        sending = local_decay[..., None, None] * leaving_now + pull_back
        return shifted(sending, "context", -1)

    leaving = lax.fori_loop(0, lax.axis_size("context") - 1, relay_step, jnp.zeros_like(pull_back))
    _, full_pull = jax.vjp(forward, x_full, b_full, c_full, dt_rows, dt_bias, a_log, d_skip)
    gradients = full_pull((cotangent, leaving))
    bias_total, rate_total, skip_total = lax.psum(
        (gradients[4], gradients[5], gradients[6]), "context"
    )
    return (
        gradients[0].astype(jnp.bfloat16),
        gradients[1].astype(jnp.bfloat16),
        gradients[2].astype(jnp.bfloat16),
        jnp.swapaxes(gradients[3], 1, 2),
        rate_total,
        bias_total,
        skip_total,
    )


def solution(mesh):
    return jax.shard_map(
        on_device,
        mesh=mesh,
        in_specs=(
            P(None, "context", "tensor"),
            P(None, "context", "tensor"),
            P(None, "context", "tensor"),
            P(None, "tensor", "context"),
            P("tensor"),
            P("tensor"),
            P("tensor"),
            P(None, "context", "tensor"),
            P(None, ("context", "tensor")),
            P(),
        ),
        out_specs=(
            P(None, "context", "tensor"),
            P(None, "context", "tensor"),
            P(None, "context", "tensor"),
            P(None, "tensor", "context"),
            P("tensor"),
            P("tensor"),
            P("tensor"),
        ),
        check_vma=False,
    )
```

profile of v0, /device:TPU:0, one launch (start us, length us, event | category | flops | bytes accessed | tf_op | source)
XLA Modules:
  0.0 1244.0 jit_solution(9554491319648042843)
XLA Ops:
  21.0 69.2 %psum.28 = f32[2]{0:T(128)S(1)} all-reduce(f32[2]{0:T(128)S(1)} %fusion.137), channel_id=1, replica_groups=mesh['context'=16,'tensor'=8] {'context','tensor'}, use_global_device_ids=true, to_apply=%region_3.4 | all-reduce | flops 2 | bytes 16 | tf_op jit(solution)/shard_map/psum | solution.py:133
  115.8 21.3 %all-gather = f32[32,1,16,1]{2,3,1,0:T(1,128)S(1)} all-gather(f32[2,1,16,1]{2,3,1,0:T(1,128)S(1)} %copy.289), channel_id=2, replica_groups=mesh['context'=16,'tensor'=8] {'context'}, dimensions={0}, use_global_device_ids=true | all-gather | bytes 2176 | tf_op jit(solution)/shard_map/all_gather | solution.py:17
  144.9 75.6 %all-gather.4.cloned.1.call-done = f32[32,16,64,256]{3,2,1,0:T(8,128)} async-done(((f32[2,16,64,256]{3,2,1,0:T(8,128)}), f32[32,16,64,256]{3,2,1,0:T(8,128)}) %all-gather.4.cloned.1.call-update) | async-done | bytes 33554448 | tf_op jit(solution)/shard_map/all_gather | solution.py:17
  220.5 32.1 %while.65 = (s32[]{:T(128)}, f32[2,1,16,64,256]{4,3,2,1,0:T(8,128)S(1)}, s32[]{:T(128)}, f32[16,2,1,16]{3,1,2,0:T(2,128)S(1)}, f32[16,2,1,16,64,256]{5,4,3,1,2,0:T(8,128)}, /*index=5*/s32[]{:T(128)}, s32[]{:T(128)}) while((s32[]{:T(128)}, f32[2,1,16,64,256]{4,3,2,1,0:T(8,128)S(1)}, s32[]{:T(128)}, f32[16,2,1,16]{3,1,2,0:T(2,128)S(1)}, ...), condition=%wide.region_8.9_spmd.clone, body=%wide.region_7.8_spmd.clone.sunk | while | flops 2097156 | bytes 6291945 | solution.py:26
  252.7 16.1 %while.64 = (s32[]{:T(128)}, f32[2,1,16,64,256]{4,3,2,0,1:T(8,128)S(1)}, f32[2,2,1,16,64,256]{5,4,3,1,2,0:T(8,128)}, f32[2,2,256,16]{2,0,3,1:T(2,128)S(1)}, f32[...) while((s32[]{:T(128)}, ...), condition=%wide.region_12.13_spmd, body=%wide.region_9.12_spmd.sunk | while | flops 1613258880 | bytes 32576208 | solution.py:98
  269.0 725.5 %while.63 = (s32[]{:T(128)}, f32[2,1,16,64,256]{4,3,2,1,0:T(8,128)S(1)}, f32[2,1,16]{2,0,1:T(2,128)S(1)}, f32[2,1,16,64,256]{4,3,2,1,0:T(8,128)}, s32[]{:T(128)}) while((s32[]{:T(128)}, f32[2,1,16,64,256]{4,3,2,1,0:T(8,128)S(1)}, f32[2,1,16]{2,0,1:T(2,128)S(1)}, f32[2,1,16,64,256]{4,3,2,1,0:T(8,128)}, s32[]{:T(128)}) %tuple.181), condition=%wide.region_6.7_spmd, body=%wide.region_5.6_spmd.sunk | while | flops 1048578 | bytes 14680293 | solution.py:170
  273.5 48.2 %collective-permute-done = f32[2,1,16,64,256]{4,3,2,1,0:T(8,128)S(1)} collective-permute-done((f32[2,1,16,64,256]{4,3,2,1,0:T(8,128)}, f32[2,1,16,64,256]{4,3,2,1,0:T(8,128)S(1)}, u32[]{:S(2)}, u32[]{:S(2)}) %collective-permute-start) | collective-permute-done | bytes 2097184 | tf_op jit(solution)/shard_map/while/body/eval_jaxpr/ppermute | solution.py:32
  326.2 47.3 %collective-permute-done = f32[2,1,16,64,256]{4,3,2,1,0:T(8,128)S(1)} collective-permute-done((f32[2,1,16,64,256]{4,3,2,1,0:T(8,128)}, f32[2,1,16,64,256]{4,3,2,1,0:T(8,128)S(1)}, u32[]{:S(2)}, u32[]{:S(2)}) %collective-permute-start) | collective-permute-done | bytes 2097184 | tf_op jit(solution)/shard_map/while/body/eval_jaxpr/ppermute | solution.py:32
  378.0 46.4 %collective-permute-done = f32[2,1,16,64,256]{4,3,2,1,0:T(8,128)S(1)} collective-permute-done((f32[2,1,16,64,256]{4,3,2,1,0:T(8,128)}, f32[2,1,16,64,256]{4,3,2,1,0:T(8,128)S(1)}, u32[]{:S(2)}, u32[]{:S(2)}) %collective-permute-start) | collective-permute-done | bytes 2097184 | tf_op jit(solution)/shard_map/while/body/eval_jaxpr/ppermute | solution.py:32
  428.9 47.2 %collective-permute-done = f32[2,1,16,64,256]{4,3,2,1,0:T(8,128)S(1)} collective-permute-done((f32[2,1,16,64,256]{4,3,2,1,0:T(8,128)}, f32[2,1,16,64,256]{4,3,2,1,0:T(8,128)S(1)}, u32[]{:S(2)}, u32[]{:S(2)}) %collective-permute-start) | collective-permute-done | bytes 2097184 | tf_op jit(solution)/shard_map/while/body/eval_jaxpr/ppermute | solution.py:32
  480.6 46.6 %collective-permute-done = f32[2,1,16,64,256]{4,3,2,1,0:T(8,128)S(1)} collective-permute-done((f32[2,1,16,64,256]{4,3,2,1,0:T(8,128)}, f32[2,1,16,64,256]{4,3,2,1,0:T(8,128)S(1)}, u32[]{:S(2)}, u32[]{:S(2)}) %collective-permute-start) | collective-permute-done | bytes 2097184 | tf_op jit(solution)/shard_map/while/body/eval_jaxpr/ppermute | solution.py:32
  531.7 45.7 %collective-permute-done = f32[2,1,16,64,256]{4,3,2,1,0:T(8,128)S(1)} collective-permute-done((f32[2,1,16,64,256]{4,3,2,1,0:T(8,128)}, f32[2,1,16,64,256]{4,3,2,1,0:T(8,128)S(1)}, u32[]{:S(2)}, u32[]{:S(2)}) %collective-permute-start) | collective-permute-done | bytes 2097184 | tf_op jit(solution)/shard_map/while/body/eval_jaxpr/ppermute | solution.py:32
  582.0 44.8 %collective-permute-done = f32[2,1,16,64,256]{4,3,2,1,0:T(8,128)S(1)} collective-permute-done((f32[2,1,16,64,256]{4,3,2,1,0:T(8,128)}, f32[2,1,16,64,256]{4,3,2,1,0:T(8,128)S(1)}, u32[]{:S(2)}, u32[]{:S(2)}) %collective-permute-start) | collective-permute-done | bytes 2097184 | tf_op jit(solution)/shard_map/while/body/eval_jaxpr/ppermute | solution.py:32
  631.3 43.9 %collective-permute-done = f32[2,1,16,64,256]{4,3,2,1,0:T(8,128)S(1)} collective-permute-done((f32[2,1,16,64,256]{4,3,2,1,0:T(8,128)}, f32[2,1,16,64,256]{4,3,2,1,0:T(8,128)S(1)}, u32[]{:S(2)}, u32[]{:S(2)}) %collective-permute-start) | collective-permute-done | bytes 2097184 | tf_op jit(solution)/shard_map/while/body/eval_jaxpr/ppermute | solution.py:32
  679.6 43.0 %collective-permute-done = f32[2,1,16,64,256]{4,3,2,1,0:T(8,128)S(1)} collective-permute-done((f32[2,1,16,64,256]{4,3,2,1,0:T(8,128)}, f32[2,1,16,64,256]{4,3,2,1,0:T(8,128)S(1)}, u32[]{:S(2)}, u32[]{:S(2)}) %collective-permute-start) | collective-permute-done | bytes 2097184 | tf_op jit(solution)/shard_map/while/body/eval_jaxpr/ppermute | solution.py:32
  727.1 42.0 %collective-permute-done = f32[2,1,16,64,256]{4,3,2,1,0:T(8,128)S(1)} collective-permute-done((f32[2,1,16,64,256]{4,3,2,1,0:T(8,128)}, f32[2,1,16,64,256]{4,3,2,1,0:T(8,128)S(1)}, u32[]{:S(2)}, u32[]{:S(2)}) %collective-permute-start) | collective-permute-done | bytes 2097184 | tf_op jit(solution)/shard_map/while/body/eval_jaxpr/ppermute | solution.py:32
  773.6 41.3 %collective-permute-done = f32[2,1,16,64,256]{4,3,2,1,0:T(8,128)S(1)} collective-permute-done((f32[2,1,16,64,256]{4,3,2,1,0:T(8,128)}, f32[2,1,16,64,256]{4,3,2,1,0:T(8,128)S(1)}, u32[]{:S(2)}, u32[]{:S(2)}) %collective-permute-start) | collective-permute-done | bytes 2097184 | tf_op jit(solution)/shard_map/while/body/eval_jaxpr/ppermute | solution.py:32
  819.4 41.3 %collective-permute-done = f32[2,1,16,64,256]{4,3,2,1,0:T(8,128)S(1)} collective-permute-done((f32[2,1,16,64,256]{4,3,2,1,0:T(8,128)}, f32[2,1,16,64,256]{4,3,2,1,0:T(8,128)S(1)}, u32[]{:S(2)}, u32[]{:S(2)}) %collective-permute-start) | collective-permute-done | bytes 2097184 | tf_op jit(solution)/shard_map/while/body/eval_jaxpr/ppermute | solution.py:32
  865.2 41.3 %collective-permute-done = f32[2,1,16,64,256]{4,3,2,1,0:T(8,128)S(1)} collective-permute-done((f32[2,1,16,64,256]{4,3,2,1,0:T(8,128)}, f32[2,1,16,64,256]{4,3,2,1,0:T(8,128)S(1)}, u32[]{:S(2)}, u32[]{:S(2)}) %collective-permute-start) | collective-permute-done | bytes 2097184 | tf_op jit(solution)/shard_map/while/body/eval_jaxpr/ppermute | solution.py:32
  911.0 41.3 %collective-permute-done = f32[2,1,16,64,256]{4,3,2,1,0:T(8,128)S(1)} collective-permute-done((f32[2,1,16,64,256]{4,3,2,1,0:T(8,128)}, f32[2,1,16,64,256]{4,3,2,1,0:T(8,128)S(1)}, u32[]{:S(2)}, u32[]{:S(2)}) %collective-permute-start) | collective-permute-done | bytes 2097184 | tf_op jit(solution)/shard_map/while/body/eval_jaxpr/ppermute | solution.py:32
  956.8 37.7 %collective-permute-done = f32[2,1,16,64,256]{4,3,2,1,0:T(8,128)S(1)} collective-permute-done((f32[2,1,16,64,256]{4,3,2,1,0:T(8,128)}, f32[2,1,16,64,256]{4,3,2,1,0:T(8,128)S(1)}, u32[]{:S(2)}, u32[]{:S(2)}) %collective-permute-start) | collective-permute-done | bytes 2097184 | tf_op jit(solution)/shard_map/while/body/eval_jaxpr/ppermute | solution.py:32
  998.6 187.6 %while.66 = (s32[]{:T(128)}, f32[16]{0:T(128)}, f32[16]{0:T(128)}, f32[2,1,16,64,256]{4,3,2,0,1:T(8,128)S(1)}, bf16[2,2,256,1024]{2,3,1,0:T(8,128)(2,1)}, /*inde...) while((s32[]{:T(128)}, f32[16]{0:T(128)}, f32[16]{0:T(128)}, ...), condition=%wide.region_29.30_spmd.clone, body=%wide.region_13.29_spmd.clone.sunk | while | flops 8844836864 | bytes 141977136 | solution.py:98
  1046.0 8.4 fusion.204
  1195.7 41.3 %all-reduce.2 = (f32[16]{0:T(128)}, f32[16]{0:T(128)}, f32[16]{0:T(128)}) all-reduce(f32[16]{0:T(128)S(1)} %negate_multiply_fusion, f32[16]{0:T(128)S(1)} %get-tuple-element.872, f32[16]{0:T(128)S(1)} %copy-done.26), channel_id=1, replica_groups=mesh['context'=16,'tensor'=8] {'context'}, use_global_device_ids=true, to_apply=%region_30.31 | all-reduce | flops 48 | bytes 384 | tf_op jit(solution)/shard_map/psum | solution.py:173
  (375 shorter events, 337.0 us)
Async XLA Ops:
  7.2 213.4 %all-gather.4.cloned.1.call-start = ((), (), s32[]{:S(2)}) async-start(), calls=%async_computation | async-start | bytes 35651584 | tf_op jit(solution)/shard_map/all_gather | solution.py:17
  272.3 49.5 %collective-permute-start = (f32[2,1,16,64,256]{4,3,2,1,0:T(8,128)}, f32[2,1,16,64,256]{4,3,2,1,0:T(8,128)S(1)}, u32[]{:S(2)}, u32[]{:S(2)}) collective-permute-start(f32[2,1,16,64,256]{4,3,2,1,0:T(8,128)} %multiply_add_fusion.2), channel_id=1, source_target_pairs={{8,0},{16,8},{24,16},{32,24},{40,32},{48,40},{56,48},{64,56},{72,6... | collective-permute-start | bytes 6291464 | tf_op jit(solution)/shard_map/while/body/eval_jaxpr/ppermute | solution.py:32
  324.9 48.6 %collective-permute-start = (f32[2,1,16,64,256]{4,3,2,1,0:T(8,128)}, f32[2,1,16,64,256]{4,3,2,1,0:T(8,128)S(1)}, u32[]{:S(2)}, u32[]{:S(2)}) collective-permute-start(f32[2,1,16,64,256]{4,3,2,1,0:T(8,128)} %multiply_add_fusion.2), channel_id=1, source_target_pairs={{8,0},{16,8},{24,16},{32,24},{40,32},{48,40},{56,48},{64,56},{72,6... | collective-permute-start | bytes 6291464 | tf_op jit(solution)/shard_map/while/body/eval_jaxpr/ppermute | solution.py:32
  376.7 47.7 %collective-permute-start = (f32[2,1,16,64,256]{4,3,2,1,0:T(8,128)}, f32[2,1,16,64,256]{4,3,2,1,0:T(8,128)S(1)}, u32[]{:S(2)}, u32[]{:S(2)}) collective-permute-start(f32[2,1,16,64,256]{4,3,2,1,0:T(8,128)} %multiply_add_fusion.2), channel_id=1, source_target_pairs={{8,0},{16,8},{24,16},{32,24},{40,32},{48,40},{56,48},{64,56},{72,6... | collective-permute-start | bytes 6291464 | tf_op jit(solution)/shard_map/while/body/eval_jaxpr/ppermute | solution.py:32
  427.6 48.5 %collective-permute-start = (f32[2,1,16,64,256]{4,3,2,1,0:T(8,128)}, f32[2,1,16,64,256]{4,3,2,1,0:T(8,128)S(1)}, u32[]{:S(2)}, u32[]{:S(2)}) collective-permute-start(f32[2,1,16,64,256]{4,3,2,1,0:T(8,128)} %multiply_add_fusion.2), channel_id=1, source_target_pairs={{8,0},{16,8},{24,16},{32,24},{40,32},{48,40},{56,48},{64,56},{72,6... | collective-permute-start | bytes 6291464 | tf_op jit(solution)/shard_map/while/body/eval_jaxpr/ppermute | solution.py:32
  479.3 47.9 %collective-permute-start = (f32[2,1,16,64,256]{4,3,2,1,0:T(8,128)}, f32[2,1,16,64,256]{4,3,2,1,0:T(8,128)S(1)}, u32[]{:S(2)}, u32[]{:S(2)}) collective-permute-start(f32[2,1,16,64,256]{4,3,2,1,0:T(8,128)} %multiply_add_fusion.2), channel_id=1, source_target_pairs={{8,0},{16,8},{24,16},{32,24},{40,32},{48,40},{56,48},{64,56},{72,6... | collective-permute-start | bytes 6291464 | tf_op jit(solution)/shard_map/while/body/eval_jaxpr/ppermute | solution.py:32
  530.5 47.0 %collective-permute-start = (f32[2,1,16,64,256]{4,3,2,1,0:T(8,128)}, f32[2,1,16,64,256]{4,3,2,1,0:T(8,128)S(1)}, u32[]{:S(2)}, u32[]{:S(2)}) collective-permute-start(f32[2,1,16,64,256]{4,3,2,1,0:T(8,128)} %multiply_add_fusion.2), channel_id=1, source_target_pairs={{8,0},{16,8},{24,16},{32,24},{40,32},{48,40},{56,48},{64,56},{72,6... | collective-permute-start | bytes 6291464 | tf_op jit(solution)/shard_map/while/body/eval_jaxpr/ppermute | solution.py:32
  580.7 46.1 %collective-permute-start = (f32[2,1,16,64,256]{4,3,2,1,0:T(8,128)}, f32[2,1,16,64,256]{4,3,2,1,0:T(8,128)S(1)}, u32[]{:S(2)}, u32[]{:S(2)}) collective-permute-start(f32[2,1,16,64,256]{4,3,2,1,0:T(8,128)} %multiply_add_fusion.2), channel_id=1, source_target_pairs={{8,0},{16,8},{24,16},{32,24},{40,32},{48,40},{56,48},{64,56},{72,6... | collective-permute-start | bytes 6291464 | tf_op jit(solution)/shard_map/while/body/eval_jaxpr/ppermute | solution.py:32
  630.0 45.2 %collective-permute-start = (f32[2,1,16,64,256]{4,3,2,1,0:T(8,128)}, f32[2,1,16,64,256]{4,3,2,1,0:T(8,128)S(1)}, u32[]{:S(2)}, u32[]{:S(2)}) collective-permute-start(f32[2,1,16,64,256]{4,3,2,1,0:T(8,128)} %multiply_add_fusion.2), channel_id=1, source_target_pairs={{8,0},{16,8},{24,16},{32,24},{40,32},{48,40},{56,48},{64,56},{72,6... | collective-permute-start | bytes 6291464 | tf_op jit(solution)/shard_map/while/body/eval_jaxpr/ppermute | solution.py:32
  678.3 44.2 %collective-permute-start = (f32[2,1,16,64,256]{4,3,2,1,0:T(8,128)}, f32[2,1,16,64,256]{4,3,2,1,0:T(8,128)S(1)}, u32[]{:S(2)}, u32[]{:S(2)}) collective-permute-start(f32[2,1,16,64,256]{4,3,2,1,0:T(8,128)} %multiply_add_fusion.2), channel_id=1, source_target_pairs={{8,0},{16,8},{24,16},{32,24},{40,32},{48,40},{56,48},{64,56},{72,6... | collective-permute-start | bytes 6291464 | tf_op jit(solution)/shard_map/while/body/eval_jaxpr/ppermute | solution.py:32
  725.8 43.3 %collective-permute-start = (f32[2,1,16,64,256]{4,3,2,1,0:T(8,128)}, f32[2,1,16,64,256]{4,3,2,1,0:T(8,128)S(1)}, u32[]{:S(2)}, u32[]{:S(2)}) collective-permute-start(f32[2,1,16,64,256]{4,3,2,1,0:T(8,128)} %multiply_add_fusion.2), channel_id=1, source_target_pairs={{8,0},{16,8},{24,16},{32,24},{40,32},{48,40},{56,48},{64,56},{72,6... | collective-permute-start | bytes 6291464 | tf_op jit(solution)/shard_map/while/body/eval_jaxpr/ppermute | solution.py:32
  772.3 42.6 %collective-permute-start = (f32[2,1,16,64,256]{4,3,2,1,0:T(8,128)}, f32[2,1,16,64,256]{4,3,2,1,0:T(8,128)S(1)}, u32[]{:S(2)}, u32[]{:S(2)}) collective-permute-start(f32[2,1,16,64,256]{4,3,2,1,0:T(8,128)} %multiply_add_fusion.2), channel_id=1, source_target_pairs={{8,0},{16,8},{24,16},{32,24},{40,32},{48,40},{56,48},{64,56},{72,6... | collective-permute-start | bytes 6291464 | tf_op jit(solution)/shard_map/while/body/eval_jaxpr/ppermute | solution.py:32
  818.1 42.6 %collective-permute-start = (f32[2,1,16,64,256]{4,3,2,1,0:T(8,128)}, f32[2,1,16,64,256]{4,3,2,1,0:T(8,128)S(1)}, u32[]{:S(2)}, u32[]{:S(2)}) collective-permute-start(f32[2,1,16,64,256]{4,3,2,1,0:T(8,128)} %multiply_add_fusion.2), channel_id=1, source_target_pairs={{8,0},{16,8},{24,16},{32,24},{40,32},{48,40},{56,48},{64,56},{72,6... | collective-permute-start | bytes 6291464 | tf_op jit(solution)/shard_map/while/body/eval_jaxpr/ppermute | solution.py:32
  863.9 42.6 %collective-permute-start = (f32[2,1,16,64,256]{4,3,2,1,0:T(8,128)}, f32[2,1,16,64,256]{4,3,2,1,0:T(8,128)S(1)}, u32[]{:S(2)}, u32[]{:S(2)}) collective-permute-start(f32[2,1,16,64,256]{4,3,2,1,0:T(8,128)} %multiply_add_fusion.2), channel_id=1, source_target_pairs={{8,0},{16,8},{24,16},{32,24},{40,32},{48,40},{56,48},{64,56},{72,6... | collective-permute-start | bytes 6291464 | tf_op jit(solution)/shard_map/while/body/eval_jaxpr/ppermute | solution.py:32
  909.7 42.6 %collective-permute-start = (f32[2,1,16,64,256]{4,3,2,1,0:T(8,128)}, f32[2,1,16,64,256]{4,3,2,1,0:T(8,128)S(1)}, u32[]{:S(2)}, u32[]{:S(2)}) collective-permute-start(f32[2,1,16,64,256]{4,3,2,1,0:T(8,128)} %multiply_add_fusion.2), channel_id=1, source_target_pairs={{8,0},{16,8},{24,16},{32,24},{40,32},{48,40},{56,48},{64,56},{72,6... | collective-permute-start | bytes 6291464 | tf_op jit(solution)/shard_map/while/body/eval_jaxpr/ppermute | solution.py:32
  955.5 39.0 %collective-permute-start = (f32[2,1,16,64,256]{4,3,2,1,0:T(8,128)}, f32[2,1,16,64,256]{4,3,2,1,0:T(8,128)S(1)}, u32[]{:S(2)}, u32[]{:S(2)}) collective-permute-start(f32[2,1,16,64,256]{4,3,2,1,0:T(8,128)} %multiply_add_fusion.2), channel_id=1, source_target_pairs={{8,0},{16,8},{24,16},{32,24},{40,32},{48,40},{56,48},{64,56},{72,6... | collective-permute-start | bytes 6291464 | tf_op jit(solution)/shard_map/while/body/eval_jaxpr/ppermute | solution.py:32
  1045.9 8.5 copy-start.21
  1078.4 6.6 copy-start.10
  1078.4 6.7 copy-start.12
  1078.4 6.7 copy-start.29
  1131.3 8.5 copy-start.21
  1163.8 6.6 copy-start.10
  1163.8 6.7 copy-start.12
  1163.8 6.7 copy-start.29
  (44 other events, 110.0 us)
Sparse Core Ops, SparseCore 0:
  20.3 200.2 all-gather.3
where the time goes:
time: 1240 us
  waiting for transfers between devices  734 us (59%)
  other arithmetic  137 us (11%)
  blocking collectives  132 us (11%)
  local copies, waits for them, and re-layouts  99.1 us (8%)
  matrix products  89.5 us (7%)
  starting transfers between devices  19.2 us (2%)
  loops' own time  18.1 us (1%)
  between operations  15.2 us (1%)
    ppermute x15, waiting for transfers between devices, shifted(): return lax.ppermute(block, axis, route)  658 us
    all_gather x1, waiting for transfers between devices, carried_in(): pieces = jax.tree.map(lambda part: lax.all_gather(part, axis), value)  75.6 us
    psum x1, blocking collectives, on_device(): lax.psum(jnp.sum(ratio_live * log_ratio, axis=1), ('context', 'tensor'))  69.2 us
    add x15, other arithmetic, relay_step(): sending = local_decay[..., None, None] * leaving_now + pull_back  48.1 us
    psum x1, blocking collectives, on_device(): lax.psum((gradients[4], gradients[5], gradients[6]), 'context')  41.3 us
    select_n x15, other arithmetic, turn(): jnp.where(position < mine, new, old)  31.6 us
    dot_general x4, matrix products, block_step(): jnp.einsum('sgjqk,skgjp->sqgjp', weights, x_five.astype(jnp.bfloat16), pr...  27.4 us
    dot_general x6, matrix products, block_step(): jnp.einsum('sqgn,sgjpn->sqgjp', c_four, carry_state, precision=HIGH)  27 us
  transfers between devices with their start and end apart: 16, of which 16 were waited for; matrix products, arithmetic and copies ran while one was open for 3% of the time, Pallas kernels for 0%

commit v1 on v0

v1 whole, which is shorter than its diff:
```python
import functools

import jax
import jax.numpy as jnp
from jax import lax
from jax.experimental import pallas as pl
from jax.experimental.pallas import tpu as pltpu
from jax.sharding import PartitionSpec as P

HP = 64
NS = 256
QB = 256
HALF = 128
BETA = 0.5
VMEM = 56 * 1024 * 1024
F32 = jnp.float32
BF16 = jnp.bfloat16
HIGH = lax.Precision.HIGHEST


def dot(lhs, rhs, dims, precision=None):
    return lax.dot_general(
        lhs, rhs, (dims, ((), ())), precision=precision, preferred_element_type=F32
    )


NN = ((1,), (0,))
NT = ((1,), (1,))
TN = ((0,), (0,))


def split3(value):
    top = value.astype(BF16)
    rest = value - top.astype(F32)
    mid = rest.astype(BF16)
    return top, mid, (rest - mid.astype(F32)).astype(BF16)


def spread_matrix(heads):
    row = lax.broadcasted_iota(jnp.int32, (3 * heads, heads * HP), 0)
    lane = lax.broadcasted_iota(jnp.int32, (3 * heads, heads * HP), 1)
    return (lax.rem(row, heads) == lax.div(lane, HP)).astype(BF16)


def spread(values, ones_rows):
    return dot(jnp.concatenate(split3(values), axis=0), ones_rows, TN)


def head_sums(product, ones_rows, heads):
    top = product.astype(BF16)
    low = (product - top.astype(F32)).astype(BF16)
    ones = ones_rows[:heads]
    return dot(ones, top, NT) + dot(ones, low, NT)


def softplus(value):
    return jnp.maximum(value, 0.0) + jnp.log1p(jnp.exp(-jnp.abs(value)))


def upper_ones():
    row = lax.broadcasted_iota(jnp.int32, (QB, QB), 0)
    col = lax.broadcasted_iota(jnp.int32, (QB, QB), 1)
    return (row <= col).astype(F32)


def running_sum(values, ones_upper):
    return dot(values, ones_upper, NN, HIGH)


def live_rows(base, length, count):
    row = lax.broadcasted_iota(jnp.int32, (count, 1), 0)
    return base + row < length


def states_kernel(info, x_ref, g_ref, b_ref, c_ref, dt_ref, bias_ref, alog_ref,
                  out_ref, first_ref, last_ref):
    heads = dt_ref.shape[1]
    seq = pl.program_id(0)
    ones_rows = spread_matrix(heads)
    ones_upper = upper_ones()
    step = softplus(dt_ref[0] + bias_ref[...])
    logs = step * -jnp.exp(alog_ref[...])
    fresh, pulls, ends = [], [], []
    for blk in range(2):
        rows = slice(blk * QB, (blk + 1) * QB)
        cum = running_sum(logs[:, rows], ones_upper)
        cum_last = cum[:, QB - 1 : QB]
        tail = spread(jnp.exp(cum_last - cum) * step[:, rows], ones_rows)
        grow = spread(jnp.exp(cum), ones_rows)
        ends.append(grow[QB - 1 : QB])
        x_tail = (x_ref[0, rows].astype(F32) * tail).astype(BF16)
        fresh.append(dot(b_ref[0, rows], x_tail, TN))
        live = live_rows(info[0] + blk * QB, info[1 + seq], QB)
        g_grow = jnp.where(live, g_ref[0, rows].astype(F32) * grow, 0.0).astype(BF16)
        pulls.append(dot(c_ref[0, rows], g_grow, TN))
    first_ref[0] = fresh[0]
    last_ref[0] = pulls[1]
    pieces, lanes = out_ref.shape[0], out_ref.shape[-1]
    out_ref[:, 0, 0] = (ends[1] * fresh[0] + fresh[1]).reshape(pieces, -1, lanes)
    out_ref[:, 1, 0] = (pulls[0] + ends[0] * pulls[1]).reshape(pieces, -1, lanes)


def chain_kernel(decay_ref, in_ref, out_ref):
    count = in_ref.shape[0]

    @pl.when(pl.program_id(0) == 0)
    def _():
        total = jnp.zeros(in_ref.shape[3:], F32)
        for at in range(count):
            out_ref[at, 0, 0] = total
            total = decay_ref[at] * total + in_ref[at, 0, 0]

    @pl.when(pl.program_id(0) == 1)
    def _():
        total = jnp.zeros(in_ref.shape[3:], F32)
        for at in reversed(range(count)):
            out_ref[at, 0, 0] = total
            total = decay_ref[at] * total + in_ref[at, 0, 0]


def intra_kernel(info, x_ref, g_ref, b_ref, c_ref, dt_ref, bias_ref, alog_ref,
                 dx_ref, db_ref, dc_ref, diff_ref, col_ref, skip_ref,
                 y_sc, d_sc, xs_sc, g_sc):
    heads = dt_ref.shape[1]
    seq, blk = pl.program_id(0), pl.program_id(1)
    ones_rows = spread_matrix(heads)
    step = softplus(dt_ref[0] + bias_ref[...])
    cum = running_sum(step * -jnp.exp(alog_ref[...]), upper_ones())
    cum_t = cum.T
    live = live_rows(info[0] + blk * QB, info[1 + seq], QB)
    x_full = x_ref[0].astype(F32)
    g_full = jnp.where(live, g_ref[0].astype(F32), 0.0)
    g_sc[...] = g_full.astype(BF16)
    step_rows = spread(step, ones_rows)
    xs_full = x_full * step_rows
    xs_sc[...] = xs_full.astype(BF16)
    skip_ref[0, 0] = jnp.sum(x_full * g_full, axis=0, keepdims=True)
    gram = dot(c_ref[0], b_ref[0], NT)
    mid = cum[:, HALF - 1 : HALF]
    early = spread(jnp.exp(mid - cum[:, :HALF]), ones_rows)
    late = spread(jnp.exp(cum[:, HALF:] - mid), ones_rows)
    x_early = (xs_sc[:HALF].astype(F32) * early).astype(BF16)
    g_late = (g_full[HALF:] * late).astype(BF16)
    gram_low = gram[HALF:, :HALF].astype(BF16)
    y_low = dot(gram_low, x_early, NN)
    dx_low = dot(gram_low, g_late, TN)
    dgram_low = dot(g_late, x_early, NT)
    row_low = head_sums(g_late.astype(F32) * y_low, ones_rows, heads)
    col_low = head_sums(x_early.astype(F32) * dx_low, ones_rows, heads)
    causal = (
        lax.broadcasted_iota(jnp.int32, (HALF, HALF), 0)
        >= lax.broadcasted_iota(jnp.int32, (HALF, HALF), 1)
    )
    left = lax.broadcasted_iota(jnp.int32, (HALF, 2 * HP), 1) < HP
    zero = jnp.zeros((HALF, 2 * HP), BF16)
    dgrams = []
    for half in range(2):
        rows = slice(half * HALF, (half + 1) * HALF)
        gram_here = jnp.where(causal, gram[rows, rows], 0.0)
        dgram = jnp.zeros((HALF, HALF), F32)
        for pair in range(heads // 2):
            lanes = slice(pair * 2 * HP, (pair + 1) * 2 * HP)
            xs = xs_sc[rows, lanes]
            gg = g_sc[rows, lanes]
            g_two = jnp.concatenate([jnp.where(left, gg, zero), jnp.where(left, zero, gg)], axis=0)
            x_two = jnp.concatenate([jnp.where(left, xs, zero), jnp.where(left, zero, xs)], axis=0)
            dweights = dot(g_two, xs, NT)
            weights = []
            for one in range(2):
                head = 2 * pair + one
                decay = jnp.exp(
                    jnp.minimum(cum_t[rows, head : head + 1] - cum[head : head + 1, rows], 0.0)
                )
                weights.append((gram_here * decay).astype(BF16))
                dgram = dgram + dweights[one * HALF : (one + 1) * HALF] * decay
            y_sc[rows, lanes] = dot(jnp.concatenate(weights, axis=1), x_two, NN)
            d_sc[rows, lanes] = dot(jnp.concatenate(weights, axis=0), g_two, TN)
        dgrams.append(jnp.where(causal, dgram, 0.0))
    row = head_sums(g_full * y_sc[...], ones_rows, heads)
    col = head_sums(xs_sc[...].astype(F32) * d_sc[...], ones_rows, heads)
    none = jnp.zeros((heads, HALF), F32)
    row = row + jnp.concatenate([none, row_low], axis=1)
    col = col + jnp.concatenate([col_low, none], axis=1)
    diff_ref[0] = row - col
    col_ref[0] = col
    dx_ref[0, :HALF] = step_rows[:HALF] * (d_sc[:HALF] + early * dx_low)
    dx_ref[0, HALF:] = step_rows[HALF:] * d_sc[HALF:]
    dgram = jnp.concatenate(
        [
            jnp.concatenate([dgrams[0], jnp.zeros((HALF, HALF), F32)], axis=1),
            jnp.concatenate([dgram_low, dgrams[1]], axis=1),
        ],
        axis=0,
    ).astype(BF16)
    dc_ref[0] = dot(dgram, b_ref[0], NN)
    db_ref[0] = dot(dgram, c_ref[0], TN)


def final_kernel(info, gate_ref, x_ref, g_ref, b_ref, c_ref, dt_ref, bias_ref, alog_ref, skip_ref,
                 enter_ref, leave_ref, first_ref, last_ref, dxi_ref, dbi_ref, dci_ref,
                 diff_ref, col_ref,
                 dx_ref, db_ref, dc_ref, ddt_ref, par_ref):
    heads = dt_ref.shape[1]
    width = heads * HP
    seq = pl.program_id(0)
    gate = gate_ref[seq]
    ones_rows = spread_matrix(heads)
    ones_upper = upper_ones()
    raw = dt_ref[0] + bias_ref[...]
    step = softplus(raw)
    rate = -jnp.exp(alog_ref[...])
    logs = step * rate
    skip_row = spread(jnp.broadcast_to(skip_ref[...], (heads, 8)), ones_rows)[0:1]
    enter = enter_ref[:, 0, 0].reshape(NS, width)
    leave = leave_ref[:, 0, 0].reshape(NS, width)
    cums = [running_sum(logs[:, b * QB : (b + 1) * QB], ones_upper) for b in range(2)]
    grows = [spread(jnp.exp(cum), ones_rows) for cum in cums]
    ends = [grow[QB - 1 : QB] for grow in grows]
    states = [enter, ends[0] * enter + first_ref[0]]
    dstates = [ends[1] * leave + last_ref[0], leave]
    ga = jnp.zeros((heads, 1), F32)
    gb = jnp.zeros((heads, 1), F32)
    for blk in range(2):
        rows = slice(blk * QB, (blk + 1) * QB)
        cum = cums[blk]
        state = states[blk].astype(BF16)
        dstate = dstates[blk].astype(BF16)
        live = live_rows(info[0] + blk * QB, info[1 + seq], QB)
        g_full = jnp.where(live, g_ref[0, rows].astype(F32), 0.0)
        g_grow = g_full * grows[blk]
        y = dot(c_ref[0, rows], state, NN)
        row = head_sums(g_grow * y, ones_rows, heads)
        dc = dot(g_grow.astype(BF16), state, NT)
        tail = spread(jnp.exp(cum[:, QB - 1 : QB] - cum) * step[:, rows], ones_rows)
        u = tail * dot(b_ref[0, rows], dstate, NN)
        x_full = x_ref[0, rows].astype(F32)
        col = head_sums(x_full * u, ones_rows, heads)
        db = dot((x_full * tail).astype(BF16), dstate, NT)
        dx_ref[0, rows] = (gate * (dxi_ref[0, rows] + u + skip_row * g_full)).astype(BF16)
        dc_ref[0, rows] = (gate * (dci_ref[0, rows] + dc)).astype(BF16)
        db_ref[0, rows] = (gate * (dbi_ref[0, rows] + db)).astype(BF16)
        through = jnp.sum(states[blk] * dstates[blk], axis=0, keepdims=True) * ends[blk]
        through = head_sums(jnp.broadcast_to(through, (8, width)), ones_rows, heads)[:, 0:1]
        both = diff_ref[0, :, rows] + row
        later = dot(both, ones_upper, NT, HIGH)
        earlier = dot(col, ones_upper, NN, HIGH) - col
        dlogs = later + earlier + through
        step_here = step[:, rows]
        dstep = (col_ref[0, :, rows] + col) / step_here + rate * dlogs
        ddt = gate * dstep * jax.nn.sigmoid(raw[:, rows])
        ddt_ref[0, :, rows] = ddt
        gb = gb + jnp.sum(ddt, axis=1, keepdims=True)
        ga = ga + gate * rate * jnp.sum(step_here * dlogs, axis=1, keepdims=True)
    par_ref[0, 0] = jnp.broadcast_to(ga, (heads, 128))
    par_ref[0, 1] = jnp.broadcast_to(gb, (heads, 128))


def on_device(
    seq_inputs, b_proj, c_proj, dt_raw, dt_bias, a_log, d_skip, out_grad, log_ratio, lengths
):
    seqs, toks, width = seq_inputs.shape
    heads = dt_bias.shape[0]
    count = lax.axis_size("context")
    ratio_rows = log_ratio.shape[1]
    ratio_pos = lax.axis_index(("context", "tensor")) * ratio_rows + jnp.arange(
        ratio_rows, dtype=jnp.int32
    )
    ratio_live = (ratio_pos[None, :] < lengths[:, None]).astype(F32)
    totals = lax.psum(jnp.sum(ratio_live * log_ratio, axis=1), ("context", "tensor"))
    signs = jnp.where(jnp.arange(2, dtype=jnp.int32) == 0, -1.0, 1.0).astype(F32)
    margin = -jnp.sum(signs * totals)
    gate = signs * BETA * jax.nn.sigmoid(-BETA * margin)
    info = jnp.concatenate(
        [(lax.axis_index("context") * toks).astype(jnp.int32)[None], lengths]
    )
    bias_col = dt_bias[:, None]
    alog_col = a_log[:, None]
    logs = jnp.sum(
        jax.nn.softplus(dt_raw + dt_bias[None, :, None]) * -jnp.exp(a_log)[None, :, None], axis=2
    )
    decays = jnp.exp(lax.all_gather(logs, "context"))
    decays = jnp.repeat(decays, HP, axis=2)[:, :, None, :]

    smem = pl.BlockSpec(memory_space=pltpu.SMEM)
    params = pltpu.CompilerParams(vmem_limit_bytes=VMEM)
    per_seq = lambda *shape: pl.BlockSpec((1,) + shape, lambda s: (s,) + (0,) * len(shape))
    whole = lambda *shape: pl.BlockSpec(shape, lambda *at: (0,) * len(shape))
    piece = NS // count
    seq_specs = [
        per_seq(toks, width), per_seq(toks, width), per_seq(toks, NS), per_seq(toks, NS),
        per_seq(heads, toks), whole(heads, 1), whole(heads, 1),
    ]
    local, first, last = pl.pallas_call(
        states_kernel,
        grid=(seqs,),
        in_specs=[smem] + seq_specs,
        out_specs=[
            pl.BlockSpec((count, 2, 1, piece, width), lambda s: (0, 0, s, 0, 0)),
            per_seq(NS, width), per_seq(NS, width),
        ],
        out_shape=[
            jax.ShapeDtypeStruct((count, 2, seqs, piece, width), F32),
            jax.ShapeDtypeStruct((seqs, NS, width), F32),
            jax.ShapeDtypeStruct((seqs, NS, width), F32),
        ],
        compiler_params=params,
        name="states",
    )(info, seq_inputs, out_grad, b_proj, c_proj, dt_raw, bias_col, alog_col)

    gathered = lax.all_to_all(local, "context", 0, 0)
    chained = pl.pallas_call(
        chain_kernel,
        grid=(2, seqs),
        in_specs=[
            pl.BlockSpec((count, None, 1, width), lambda k, s: (0, s, 0, 0)),
            pl.BlockSpec((count, 1, 1, piece, width), lambda k, s: (0, k, s, 0, 0)),
        ],
        out_specs=pl.BlockSpec((count, 1, 1, piece, width), lambda k, s: (0, k, s, 0, 0)),
        out_shape=jax.ShapeDtypeStruct((count, 2, seqs, piece, width), F32),
        compiler_params=params,
        name="chain",
    )(decays, gathered)
    entering = lax.all_to_all(chained, "context", 0, 0)

    tok_spec = lambda w: pl.BlockSpec((1, QB, w), lambda s, b: (s, b, 0))
    head_spec = pl.BlockSpec((1, heads, QB), lambda s, b: (s, 0, b))
    blocks = toks // QB
    dxi, dbi, dci, diff, col, skips = pl.pallas_call(
        intra_kernel,
        grid=(seqs, blocks),
        in_specs=[smem, tok_spec(width), tok_spec(width), tok_spec(NS), tok_spec(NS),
                  head_spec, whole(heads, 1), whole(heads, 1)],
        out_specs=[tok_spec(width), tok_spec(NS), tok_spec(NS), head_spec, head_spec,
                   pl.BlockSpec((1, 1, 1, width), lambda s, b: (s, b, 0, 0))],
        out_shape=[
            jax.ShapeDtypeStruct((seqs, toks, width), F32),
            jax.ShapeDtypeStruct((seqs, toks, NS), F32),
            jax.ShapeDtypeStruct((seqs, toks, NS), F32),
            jax.ShapeDtypeStruct((seqs, heads, toks), F32),
            jax.ShapeDtypeStruct((seqs, heads, toks), F32),
            jax.ShapeDtypeStruct((seqs, blocks, 1, width), F32),
        ],
        scratch_shapes=[
            pltpu.VMEM((QB, width), F32), pltpu.VMEM((QB, width), F32),
            pltpu.VMEM((QB, width), BF16), pltpu.VMEM((QB, width), BF16),
        ],
        compiler_params=params,
        name="intra",
    )(info, seq_inputs, out_grad, b_proj, c_proj, dt_raw, bias_col, alog_col)

    state_spec = lambda k: pl.BlockSpec((count, 1, 1, piece, width), lambda s: (0, k, s, 0, 0))
    dx, db, dc, ddt, pars = pl.pallas_call(
        final_kernel,
        grid=(seqs,),
        in_specs=[smem, smem] + seq_specs + [
            whole(heads, 1), state_spec(0), state_spec(1), per_seq(NS, width), per_seq(NS, width),
            per_seq(toks, width), per_seq(toks, NS), per_seq(toks, NS),
            per_seq(heads, toks), per_seq(heads, toks),
        ],
        out_specs=[per_seq(toks, width), per_seq(toks, NS), per_seq(toks, NS),
                   per_seq(heads, toks), per_seq(2, heads, 128)],
        out_shape=[
            jax.ShapeDtypeStruct((seqs, toks, width), BF16),
            jax.ShapeDtypeStruct((seqs, toks, NS), BF16),
            jax.ShapeDtypeStruct((seqs, toks, NS), BF16),
            jax.ShapeDtypeStruct((seqs, heads, toks), F32),
            jax.ShapeDtypeStruct((seqs, 2, heads, 128), F32),
        ],
        compiler_params=params,
        name="final",
    )(info, gate, seq_inputs, out_grad, b_proj, c_proj, dt_raw, bias_col, alog_col,
      d_skip[:, None], entering, entering, first, last, dxi, dbi, dci, diff, col)
    skip_part = jnp.sum(
        gate[:, None] * jnp.sum(skips.reshape(seqs, blocks, heads, HP), axis=(1, 3)), axis=0
    )
    sums = lax.psum(
        jnp.concatenate([jnp.sum(pars[:, :, :, 0], axis=0), skip_part[None]], axis=0), "context"
    )
    return dx, db, dc, ddt, sums[0], sums[1], sums[2]


def solution(mesh):
    return jax.shard_map(
        on_device,
        mesh=mesh,
        in_specs=(
            P(None, "context", "tensor"),
            P(None, "context", "tensor"),
            P(None, "context", "tensor"),
            P(None, "tensor", "context"),
            P("tensor"),
            P("tensor"),
            P("tensor"),
            P(None, "context", "tensor"),
            P(None, ("context", "tensor")),
            P(),
        ),
        out_specs=(
            P(None, "context", "tensor"),
            P(None, "context", "tensor"),
            P(None, "context", "tensor"),
            P(None, "tensor", "context"),
            P("tensor"),
            P("tensor"),
            P("tensor"),
        ),
        check_vma=False,
    )
```

time: 1240 us -> 288 us (0.23)
  waiting for transfers between devices: 734 us -> 0.01 us
  other arithmetic: 137 us -> 4.01 us
  local copies, waits for them, and re-layouts: 99.1 us -> 5.37 us
  matrix products: 89.5 us -> 0 us
  blocking collectives: 132 us -> 220 us
  Pallas kernels: 0 us -> 44.6 us
  loops' own time: 18.1 us -> 0 us
  between operations: 15.2 us -> 1.52 us
    ppermute x15 -> x0, waiting for transfers between devices: 658 us -> none  [shifted(): return lax.ppermute(block, axis, route)]
    dot_general x24 -> x0, matrix products: 89.5 us -> none  [the longest x4 27.4 us: block_step(): jnp.einsum('sgjqk,skgjp->sqgjp', weights, x_five.astype(jnp.bfloat16), pr...]
    all_gather x1 -> x0, waiting for transfers between devices: 75.6 us -> none  [carried_in(): pieces = jax.tree.map(lambda part: lax.all_gather(part, axis), value)]
    all_gather x1, blocking collectives: 21.3 us -> 75.6 us  [on_device(): decays = jnp.exp(lax.all_gather(logs, 'context'))]
    add x16 -> x0, other arithmetic: 48.1 us -> none  [the longest x15 48.1 us: relay_step(): sending = local_decay[..., None, None] * leaving_now + pull_back]
    pallas_call x0 -> x4, Pallas kernels: none -> 44.6 us  [the longest x1 15.6 us: on_device(): pl.pallas_call(intra_kernel, grid=(seqs, blocks), in_specs=[smem, tok_spe...]
    psum x1, blocking collectives: 69.2 us -> 106 us  [on_device(): lax.psum(jnp.sum(ratio_live * log_ratio, axis=1), ('context', 'tensor'))]
    select_n x16 -> x0, other arithmetic: 32.5 us -> none  [the longest x15 31.6 us: turn(): jnp.where(position < mine, new, old)]
  transfers between devices with their start and end apart: 16 -> 2, of which waited for: 16 -> 0; matrix products, arithmetic and copies ran while one was open for 3% -> 1% of each run, Pallas kernels for 0% -> 5%
where the time goes in v1:
time: 288 us; the launch traced here: 287 us
  blocking collectives  220 us (76%)
  Pallas kernels  44.6 us (15%)
  starting transfers between devices  12 us (4%)
  local copies, waits for them, and re-layouts  5.37 us (2%)
  other arithmetic  4.01 us (1%)
    psum x1, blocking collectives, on_device(): lax.psum(jnp.sum(ratio_live * log_ratio, axis=1), ('context', 'tensor'))  106 us
    all_gather x1, blocking collectives, on_device(): decays = jnp.exp(lax.all_gather(logs, 'context'))  75.6 us
    psum x1, blocking collectives, on_device(): lax.psum(jnp.concatenate([jnp.sum(pars[:, :, :, 0], axis=0), skip_part[No...  37.8 us
    pallas_call x1, Pallas kernels, on_device(): pl.pallas_call(intra_kernel, grid=(seqs, blocks), in_specs=[smem, tok_spe...  15.6 us
    pallas_call x1, Pallas kernels, on_device(): pl.pallas_call(final_kernel, grid=(seqs,), in_specs=[smem, smem] + seq_sp...  15.3 us
    pallas_call x1, Pallas kernels, on_device(): pl.pallas_call(states_kernel, grid=(seqs,), in_specs=[smem] + seq_specs,...  8.83 us
    all_to_all x1, starting transfers between devices, on_device(): gathered = lax.all_to_all(local, 'context', 0, 0)  7.31 us
  transfers between devices with their start and end apart: 2, of which 0 were waited for; matrix products, arithmetic and copies ran while one was open for 1% of the time, Pallas kernels for 5%

profile of v1, /device:TPU:0, one launch (start us, length us, event | category | flops | bytes accessed | tf_op | source)
XLA Modules:
  0.0 287.2 jit_solution(5183557408804778092)
XLA Ops:
  0.6 1.3 copy.35.bias_ref
  2.0 1.3 copy.36.alog_ref
  3.3 1.2 pad_add_fusion.info
  4.5 8.8 %states.1 = (f32[16,2,2,16,1024]{4,3,2,1,0:T(8,128)}, f32[2,256,1024]{2,1,0:T(8,128)}, f32[2,256,1024]{2,1,0:T(8,128)}) custom-call(s32[3]{0:T(128)} %pad_add_fusion.info, bf16[2,512,1024]{2,1,0:T(8,128)(2,1)} %x_ref.5, bf16[2,512,1024]{2,1,0:T(8,128)(2,1)} %g_ref.5, bf16[2,512,256]{2,1,0:T(8,128)(2,1)} %b_ref.5, bf16[2,512,256]{2,1,0:T(8,128)(2,1)} %c_ref.5, ...), custom_call_target="tpu_custom_call" | custom-call | tf_op jit(solution)/shard_map/states/pallas_call | solution.py:293
  13.4 7.3 %all-to-all-start = ((f32[16,2,2,16,1024]{4,3,2,1,0:T(8,128)}), f32[16,2,2,16,1024]{4,3,2,1,0:T(8,128)}, u32[]{:S(2)}, u32[]{:S(2)}) async-start(f32[16,2,2,16,1024]{4,3,2,1,0:T(8,128)} %get-tuple-element.21), calls=%async_computation | async-start | bytes 8388608 | tf_op jit(solution)/shard_map/all_to_all | solution.py:310
  20.7 0.2 fusion.1
  20.9 75.6 %all-gather.1 = f32[16,2,16]{2,1,0:T(2,128)S(1)} all-gather(f32[1,2,16]{2,1,0:T(2,128)S(1)} %bitcast.14), channel_id=2, replica_groups=mesh['context'=16,'tensor'=8] {'context'}, dimensions={0}, use_global_device_ids=true | all-gather | bytes 2176 | tf_op jit(solution)/shard_map/all_gather | solution.py:281
  96.6 0.1 broadcast_in_dim.37
  96.7 0.8 broadcast_in_dim_reshape.3.decay_ref
  97.6 4.8 %chain.1 = f32[16,2,2,16,1024]{4,3,2,1,0:T(8,128)} custom-call(f32[16,2,1,1024]{3,2,1,0:T(1,128)} %broadcast_in_dim_reshape.3.decay_ref, f32[16,2,2,16,1024]{4,3,2,1,0:T(8,128)} %all-to-all-done.in_ref), custom_call_target="tpu_custom_call" | custom-call | tf_op jit(solution)/shard_map/chain/pallas_call | solution.py:311
  102.4 4.7 %all-to-all-start.1 = ((f32[16,2,2,16,1024]{4,3,2,1,0:T(8,128)}), f32[16,2,2,16,1024]{4,3,2,1,0:T(8,128)}, u32[]{:S(2)}, u32[]{:S(2)}) async-start(f32[16,2,2,16,1024]{4,3,2,1,0:T(8,128)} %chain.1), calls=%async_computation.1 | async-start | bytes 8388608 | tf_op jit(solution)/shard_map/all_to_all | solution.py:323
  107.1 0.2 fusion.2
  107.3 106.3 %psum.14 = f32[2]{0:T(128)S(1)} all-reduce(f32[2]{0:T(128)S(1)} %fusion.2), channel_id=1, replica_groups=mesh['context'=16,'tensor'=8] {'context','tensor'}, use_global_device_ids=true, to_apply=%region_1.0 | all-reduce | flops 2 | bytes 16 | tf_op jit(solution)/shard_map/psum | solution.py:269
  213.6 15.6 %intra.1 = (f32[2,512,1024]{2,1,0:T(8,128)}, f32[2,512,256]{2,1,0:T(8,128)}, f32[2,512,256]{2,1,0:T(8,128)}, f32[2,16,512]{2,1,0:T(8,128)}, f32[2,16,512]{2,1,0:T(8,128)}, /*index=5*/f32[2,2,1,1024]{3,2,1,0:T(1,128)}) custom-call(s32[3]{0:T(128)} %pad_add_fusion.info, bf16[2,512,1024]{2,1,0:T(8,128)(2,1)} %x_ref.5, bf16[2,512,1024]{2,1,0:T(8,128)(2,1)} %g_ref.5, ...), custom_call_target="tpu_custom_call" | custom-call | tf_op jit(solution)/shard_map/intra/pallas_call | solution.py:328
  229.2 0.6 multiply_reduce_fusion.1
  230.6 0.7 copy.37.skip_ref
  231.3 0.8 reduce_sum.65
  232.1 0.1 reduce_sum.67
  232.2 0.1 multiply_reduce_fusion
  232.3 0.4 copy-done.1
  232.7 15.3 %final.1 = (bf16[2,512,1024]{2,1,0:T(8,128)(2,1)}, bf16[2,512,256]{2,1,0:T(8,128)(2,1)}, bf16[2,512,256]{2,1,0:T(8,128)(2,1)}, f32[2,16,512]{2,1,0:T(8,128)}, f32[2,2,16,128]{3,2,1,0:T(8,128)}) custom-call(s32[3]{0:T(128)} %pad_add_fusion.info, f32[2]{0:T(128)} %copy-done.1, bf16[2,512,1024]{2,1,0:T(8,128)(2,1)} %x_ref.5, bf16[2,512,1024]{2,1,0:T(8,128)(2,1)} %g_ref.5, ...), custom_call_target="tpu_custom_call" | custom-call | tf_op jit(solution)/shard_map/final/pallas_call | solution.py:352
  248.0 0.8 slice_reduce_fusion
  248.9 37.8 %psum.15 = f32[3,16]{1,0:T(4,128)S(1)} all-reduce(f32[3,16]{1,0:T(4,128)S(1)} %pad_maximum_fusion), channel_id=1, replica_groups=mesh['context'=16,'tensor'=8] {'context'}, use_global_device_ids=true, to_apply=%region_8.9 | all-reduce | flops 48 | bytes 384 | tf_op jit(solution)/shard_map/psum | solution.py:376
  286.7 0.5 slice_bitcast_fusion
  (21 shorter events, 0.2 us)
Async XLA Ops:
  13.4 7.4 %copy-start.4 = (f32[16]{0:T(128)S(1)}, f32[16]{0:T(128)}, u32[]{:S(2)}) copy-start(f32[16]{0:T(128)} %param.15) | copy-start | bytes 196
  13.4 7.4 %copy-start = (f32[2,16,512]{2,1,0:T(8,128)S(1)}, f32[2,16,512]{2,1,0:T(8,128)}, u32[]{:S(2)}) copy-start(f32[2,16,512]{2,1,0:T(8,128)} %dt_ref.5) | copy-start | bytes 196612
  13.4 7.4 %copy-start.2 = (f32[16]{0:T(128)S(1)}, f32[16]{0:T(128)}, u32[]{:S(2)}) copy-start(f32[16]{0:T(128)} %param.14) | copy-start | bytes 196
  13.4 84.2 %all-to-all-start = ((f32[16,2,2,16,1024]{4,3,2,1,0:T(8,128)}), f32[16,2,2,16,1024]{4,3,2,1,0:T(8,128)}, u32[]{:S(2)}, u32[]{:S(2)}) async-start(f32[16,2,2,16,1024]{4,3,2,1,0:T(8,128)} %get-tuple-element.21), calls=%async_computation | async-start | bytes 8388608 | tf_op jit(solution)/shard_map/all_to_all | solution.py:310
  102.4 4.7 %copy-start.3 = (f32[2,64]{1,0:T(2,128)S(1)}, f32[2,64]{1,0:T(2,128)}, u32[]{:S(2)}) copy-start(f32[2,64]{1,0:T(2,128)} %param.18) | copy-start | bytes 1540
  102.4 4.7 %copy-start.5 = (s32[2]{0:T(128)S(1)}, s32[2]{0:T(128)}, u32[]{:S(2)}) copy-start(s32[2]{0:T(128)} %param.19) | copy-start | bytes 28
  102.4 129.9 %all-to-all-start.1 = ((f32[16,2,2,16,1024]{4,3,2,1,0:T(8,128)}), f32[16,2,2,16,1024]{4,3,2,1,0:T(8,128)}, u32[]{:S(2)}, u32[]{:S(2)}) async-start(f32[16,2,2,16,1024]{4,3,2,1,0:T(8,128)} %chain.1), calls=%async_computation.1 | async-start | bytes 8388608 | tf_op jit(solution)/shard_map/all_to_all | solution.py:323
  107.1 123.5 %copy-start.6 = (f32[16]{0:T(128)S(1)}, f32[16]{0:T(128)}, u32[]{:S(2)}) copy-start(f32[16]{0:T(128)} %param.16) | copy-start | bytes 196
  232.2 0.5 copy-start.1

commit v2 on v1

v2 whole, which is shorter than its diff:
```python
import jax
import jax.numpy as jnp
from jax import lax
from jax.experimental import pallas as pl
from jax.experimental.pallas import tpu as pltpu
from jax.sharding import PartitionSpec as P

HP = 64
NS = 256
QB = 256
HALF = 128
BETA = 0.5
PAIR = 2 * HP
LANES = 8 * HP
TILE = 8
VMEM = 56 * 1024 * 1024
F32 = jnp.float32
BF16 = jnp.bfloat16
HIGH = lax.Precision.HIGHEST


def dot(lhs, rhs, dims, precision=None):
    return lax.dot_general(
        lhs, rhs, (dims, ((), ())), precision=precision, preferred_element_type=F32
    )


NN = ((1,), (0,))
NT = ((1,), (1,))
TN = ((0,), (0,))


def split3(value):
    top = value.astype(BF16)
    rest = value - top.astype(F32)
    mid = rest.astype(BF16)
    return top, mid, (rest - mid.astype(F32)).astype(BF16)


def spread_matrix(heads):
    row = lax.broadcasted_iota(jnp.int32, (3 * heads, heads * HP), 0)
    lane = lax.broadcasted_iota(jnp.int32, (3 * heads, heads * HP), 1)
    return (lax.rem(row, heads) == lax.div(lane, HP)).astype(BF16)


def spread(values, ones_rows):
    return dot(jnp.concatenate(split3(values), axis=0), ones_rows, TN)


def head_sums(product, ones_rows, heads):
    top = product.astype(BF16)
    low = (product - top.astype(F32)).astype(BF16)
    ones = ones_rows[:heads]
    return dot(ones, top, NT) + dot(ones, low, NT)


def softplus(value):
    return jnp.maximum(value, 0.0) + jnp.log1p(jnp.exp(-jnp.abs(value)))


def upper_ones():
    row = lax.broadcasted_iota(jnp.int32, (QB, QB), 0)
    col = lax.broadcasted_iota(jnp.int32, (QB, QB), 1)
    return (row <= col).astype(F32)


def running_sum(values, ones_upper):
    return dot(values, ones_upper, NN, HIGH)


def live_rows(base, length, count):
    row = lax.broadcasted_iota(jnp.int32, (count, 1), 0)
    return base + row < length


def column(row_ref):
    heads = row_ref.shape[1]
    same = lax.broadcasted_iota(jnp.int32, (heads, heads), 0) == lax.broadcasted_iota(
        jnp.int32, (heads, heads), 1
    )
    return jnp.sum(jnp.where(same, row_ref[...], 0.0), axis=1, keepdims=True)


def token_base(toks):
    return lax.axis_index("context") * toks


def flat(column_values, lanes):
    heads = column_values.shape[0]
    same = lax.broadcasted_iota(jnp.int32, (heads, lanes), 0) == lax.broadcasted_iota(
        jnp.int32, (heads, lanes), 1
    )
    return jnp.sum(jnp.where(same, column_values, 0.0), axis=0, keepdims=True)


def scale_columns(tail, grow):
    rows = jnp.concatenate([tail, grow, jnp.zeros((128 - 2 * tail.shape[0], tail.shape[1]), F32)], axis=0)
    return jnp.concatenate(split3(rows.T), axis=1)


def spread_part(heads, first, lane0, lanes):
    row = lax.rem(lax.broadcasted_iota(jnp.int32, (3 * 128, lanes), 0), 128)
    lane = lax.broadcasted_iota(jnp.int32, (3 * 128, lanes), 1) + lane0
    return (row - first == lax.div(lane, HP)).astype(BF16)


def lane_sums(product, ones_part):
    top = product.astype(BF16)
    low = (product - top.astype(F32)).astype(BF16)
    return dot(top, ones_part, NT) + dot(low, ones_part, NT)


def sum_part(heads, lane0, lanes):
    row = lax.broadcasted_iota(jnp.int32, (128, lanes), 0)
    lane = lax.broadcasted_iota(jnp.int32, (128, lanes), 1) + lane0
    return (row == lax.div(lane, HP)).astype(BF16)


def exact_dot(lhs, rhs, dims):
    top = rhs.astype(BF16)
    low = (rhs - top.astype(F32)).astype(BF16)
    return dot(lhs, top, dims) + dot(lhs, low, dims)


def states_kernel(len_ref, x_ref, g_ref, b_ref, c_ref, dt_ref, bias_ref, alog_ref, ratio_ref,
                  out_ref, first_ref, last_ref, turned_sc, scal_sc, tile_sc):
    heads = dt_ref.shape[1]
    toks = x_ref.shape[1]
    pieces = out_ref.shape[0]
    piece = NS // pieces
    at = pl.program_id(0)
    parts = heads * HP // LANES
    work = 2 * parts

    @pl.when(at < work)
    def _():
        seq, part = lax.div(at, parts), lax.rem(at, parts)

        @pl.when(part == 0)
        def _():
            ones_upper = upper_ones()
            step = softplus(dt_ref[0] + column(bias_ref))
            logs = step * -jnp.exp(column(alog_ref))
            total = jnp.zeros((heads, 1), F32)
            for blk in range(2):
                rows = slice(blk * QB, (blk + 1) * QB)
                cum = running_sum(logs[:, rows], ones_upper)
                last = cum[:, QB - 1 : QB]
                total = total + last
                scal_sc[blk] = scale_columns(jnp.exp(last - cum) * step[:, rows], jnp.exp(cum))
                turned_sc[blk] = b_ref[0, rows].astype(F32).T.astype(BF16)
                turned_sc[2 + blk] = c_ref[0, rows].astype(F32).T.astype(BF16)
            tile_sc[pl.ds(seq, 1)] = flat(jnp.exp(total), 128)

        tail_part = spread_part(heads, 0, part * LANES, LANES)
        grow_part = spread_part(heads, heads, part * LANES, LANES)
        fresh, pulls, ends = [], [], []
        for blk in range(2):
            rows = slice(blk * QB, (blk + 1) * QB)
            tail = dot(scal_sc[blk], tail_part, NN)
            grow = dot(scal_sc[blk], grow_part, NN)
            ends.append(grow[QB - 1 : QB])
            x_tail = (x_ref[0, rows].astype(F32) * tail).astype(BF16)
            fresh.append(dot(turned_sc[blk], x_tail, NN))
            live = live_rows(token_base(toks) + blk * QB, len_ref[seq], QB)
            g_grow = jnp.where(live, g_ref[0, rows].astype(F32) * grow, 0.0).astype(BF16)
            pulls.append(dot(turned_sc[2 + blk], g_grow, NN))
        first_ref[0] = fresh[0]
        last_ref[0] = pulls[1]
        whole = (ends[1] * fresh[0] + fresh[1], pulls[0] + ends[0] * pulls[1])
        for scan in range(2):
            for pair in range(LANES // PAIR):
                row = (scan * (LANES // PAIR) + pair) * piece
                out_ref[:, row : row + piece] = whole[scan][:, pair * PAIR : (pair + 1) * PAIR].reshape(
                    pieces, piece, PAIR
                )

    @pl.when(at == work)
    def _():
        ratio = ratio_ref[...]
        rows = ratio.shape[1]
        first = lax.axis_index(("context", "tensor")) * rows
        place = lax.broadcasted_iota(jnp.int32, ratio.shape, 1) + first
        seq = lax.broadcasted_iota(jnp.int32, ratio.shape, 0)
        length = jnp.where(seq == 0, len_ref[0], len_ref[1])
        totals = jnp.sum(jnp.where(place < length, ratio, 0.0), axis=1, keepdims=True)
        tile_sc[2:4] = jnp.broadcast_to(totals, (2, 128))
        tile_sc[4:] = jnp.zeros((TILE - 4, 128), F32)
        out_ref[:, 0:TILE] = jnp.broadcast_to(tile_sc[...][None], (pieces, TILE, 128))


def chain_kernel(seq, heads, tile_ref, in_ref, out_ref, sums_ref, decay_sc):
    count = in_ref.shape[0]
    piece = NS // count
    part = pl.program_id(0)

    @pl.when(part == 0)
    def _():
        tiles = [tile_ref[at] for at in range(count)]
        sums_ref[...] = sum(tiles[1:], tiles[0])
        decay = jnp.concatenate([tile[seq : seq + 1] for tile in tiles], axis=0)
        columns = jnp.concatenate(split3(decay), axis=1)
        wide = dot(columns, spread_part(heads, 0, 0, heads * HP), NN)
        for pair in range(heads // 2):
            decay_sc[pair] = wide[:, pair * PAIR : (pair + 1) * PAIR]

    pairs = LANES // PAIR
    for pair in range(pairs):
        decay = decay_sc[part * pairs + pair]
        rows = slice(pair * piece, (pair + 1) * piece)
        total = jnp.zeros((piece, PAIR), F32)
        for at in range(count):
            out_ref[at, rows] = total
            total = decay[at : at + 1] * total + in_ref[at, rows]
        rows = slice((pairs + pair) * piece, (pairs + pair + 1) * piece)
        total = jnp.zeros((piece, PAIR), F32)
        for at in reversed(range(count)):
            out_ref[at, rows] = total
            total = decay[at : at + 1] * total + in_ref[at, rows]


def intra_kernel(len_ref, x_ref, g_ref, b_ref, c_ref, dt_ref, bias_ref, alog_ref, gain_ref,
                 dx_ref, db_ref, dc_ref, diff_ref, col_ref, skip_ref, xv_ref, gg_ref, scal_ref,
                 y_sc, d_sc, g_sc):
    heads = dt_ref.shape[1]
    seq, blk = pl.program_id(0), pl.program_id(1)
    ones_rows = spread_matrix(heads)
    step = softplus(dt_ref[0] + column(bias_ref))
    cum = running_sum(step * -jnp.exp(column(alog_ref)), upper_ones())
    cum_t = cum.T
    live = live_rows(token_base(pl.num_programs(1) * QB) + blk * QB, len_ref[seq], QB)
    x_full = x_ref[0].astype(F32)
    g_full = jnp.where(live, g_ref[0].astype(F32), 0.0)
    g_sc[...] = g_full.astype(BF16)
    skip_ref[0, 0] = jnp.sum(x_full * g_full, axis=0, keepdims=True)
    tail = jnp.exp(cum[:, QB - 1 : QB] - cum) * step
    scal_ref[0] = scale_columns(tail, jnp.exp(cum))
    xv_ref[0] = (x_full * spread(tail, ones_rows)).astype(BF16)
    gg_ref[0] = (g_full * spread(jnp.exp(cum), ones_rows)).astype(BF16)
    gram = dot(c_ref[0], b_ref[0], NT)
    causal = (
        lax.broadcasted_iota(jnp.int32, (HALF, HALF), 0)
        >= lax.broadcasted_iota(jnp.int32, (HALF, HALF), 1)
    )
    low, high = slice(0, HALF), slice(HALF, QB)
    tiles = ((low, low), (high, low), (high, high))
    grams = [jnp.where(causal, gram[t, k], 0.0) if t is k else gram[t, k] for t, k in tiles]
    left = lax.broadcasted_iota(jnp.int32, (QB, PAIR), 1) < HP
    zero = jnp.zeros((QB, PAIR), BF16)
    dgrams = [jnp.zeros((HALF, HALF), F32) for _ in tiles]
    for pair in range(heads // 2):
        lanes = slice(pair * PAIR, (pair + 1) * PAIR)
        xx = x_ref[0, :, lanes]
        gg = g_sc[:, lanes]
        gs = [jnp.where(left, gg, zero), jnp.where(left, zero, gg)]
        xs = [jnp.where(left, xx, zero), jnp.where(left, zero, xx)]
        weights = []
        for one in range(2):
            head = 2 * pair + one
            mine = []
            dlow = dot(gs[one], xx[low], NT)
            dhigh = dot(gs[one][high], xx[high], NT)
            dparts = (dlow[low], dlow[high], dhigh)
            for which, (t, k) in enumerate(tiles):
                gap = cum_t[t, head : head + 1] - cum[head : head + 1, k]
                if t is k:
                    gap = jnp.minimum(gap, 0.0)
                decay = jnp.exp(gap) * step[head : head + 1, k]
                mine.append((grams[which] * decay).astype(BF16))
                dgrams[which] = dgrams[which] + dparts[which] * decay
            weights.append(mine)
        (a0, a1, a2), (b0, b1, b2) = weights
        y_sc[low, lanes] = dot(
            jnp.concatenate([a0, b0], axis=1), jnp.concatenate([xs[0][low], xs[1][low]], axis=0), NN
        )
        y_sc[high, lanes] = dot(
            jnp.concatenate([a1, a2, b1, b2], axis=1), jnp.concatenate(xs, axis=0), NN
        )
        d_sc[low, lanes] = dot(
            jnp.concatenate([a0, a1, b0, b1], axis=0), jnp.concatenate(gs, axis=0), TN
        )
        d_sc[high, lanes] = dot(
            jnp.concatenate([a2, b2], axis=0),
            jnp.concatenate([gs[0][high], gs[1][high]], axis=0), TN,
        )
    row = head_sums(g_full * y_sc[...], ones_rows, heads)
    col = head_sums(x_full * d_sc[...], ones_rows, heads)
    diff_ref[0] = row - col
    col_ref[0] = col
    gain = spread(jnp.broadcast_to(column(gain_ref), (heads, 8)), ones_rows)[0:1]
    dx_ref[0] = d_sc[...] + gain * g_full
    dgram = jnp.concatenate(
        [
            jnp.concatenate(
                [jnp.where(causal, dgrams[0], 0.0), jnp.zeros((HALF, HALF), F32)], axis=1
            ),
            jnp.concatenate([dgrams[1], jnp.where(causal, dgrams[2], 0.0)], axis=1),
        ],
        axis=0,
    ).astype(BF16)
    dc_ref[0] = dot(dgram, b_ref[0], NN)
    db_ref[0] = dot(dgram, c_ref[0], TN)


def final_kernel(seq, refs, len_ref, gate_ref, x_ref, g_ref, b_ref, c_ref, dt_ref, bias_ref,
                 alog_ref, ends_ref, first_ref, last_ref, scal_ref, diff_ref, col_ref, skip_ref):
    ddt_ref, par_ref, state_ref, dstate_ref, more_ref, sum_sc, thru_sc = refs
    heads = dt_ref.shape[1]
    toks = x_ref.shape[1]
    part = pl.program_id(0)
    gate = gate_ref[seq]
    pieces = ends_ref.shape[0]
    piece = NS // pieces
    pairs = LANES // PAIR

    @pl.when(part == 0)
    def _():
        sum_sc[...] = jnp.zeros_like(sum_sc)
        thru_sc[...] = jnp.zeros_like(thru_sc)

    tail_part = spread_part(heads, 0, part * LANES, LANES)
    grow_part = spread_part(heads, heads, part * LANES, LANES)
    ones_part = sum_part(heads, part * LANES, LANES)

    def state_of(scan):
        return jnp.concatenate(
            [
                ends_ref[:, (scan * pairs + p) * piece : (scan * pairs + p + 1) * piece].reshape(
                    NS, PAIR
                )
                for p in range(pairs)
            ],
            axis=1,
        )

    grows = [dot(scal_ref[0, b * QB : (b + 1) * QB], grow_part, NN) for b in range(2)]
    ends = [grow[QB - 1 : QB] for grow in grows]
    enter, leave = state_of(0), state_of(1)
    states = [enter, ends[0] * enter + first_ref[0]]
    dstates = [ends[1] * leave + last_ref[0], leave]
    for blk in range(2):
        rows = slice(blk * QB, (blk + 1) * QB)
        state_ref[blk] = states[blk].astype(BF16)
        dstate_ref[blk] = dstates[blk].astype(BF16)
        live = live_rows(token_base(toks) + blk * QB, len_ref[seq], QB)
        g_grow = jnp.where(live, g_ref[0, rows].astype(F32) * grows[blk], 0.0)
        y = exact_dot(c_ref[0, rows], states[blk], NN)
        sum_sc[0, rows] += lane_sums(g_grow * y, ones_part)
        tail = dot(scal_ref[0, rows], tail_part, NN)
        u = tail * exact_dot(b_ref[0, rows], dstates[blk], NN)
        sum_sc[1, rows] += lane_sums(x_ref[0, rows].astype(F32) * u, ones_part)
        through = ends[blk] * jnp.sum(states[blk] * dstates[blk], axis=0, keepdims=True)
        thru_sc[blk] += lane_sums(jnp.broadcast_to(through, (8, LANES)), ones_part)

    @pl.when(part == pl.num_programs(0) - 1)
    def _():
        ones_upper = upper_ones()
        raw = dt_ref[0] + column(bias_ref)
        step = softplus(raw)
        rate = -jnp.exp(column(alog_ref))
        ga = jnp.zeros((heads, 1), F32)
        gb = jnp.zeros((heads, 1), F32)
        for blk in range(2):
            rows = slice(blk * QB, (blk + 1) * QB)
            row = sum_sc[0, rows].T[:heads]
            col = sum_sc[1, rows].T[:heads]
            through = thru_sc[blk].T[:heads, 0:1]
            later = dot(diff_ref[0, :, rows] + row, ones_upper, NT, HIGH)
            earlier = dot(col, ones_upper, NN, HIGH) - col
            dlogs = later + earlier + through
            step_here = step[:, rows]
            dstep = (col_ref[0, :, rows] + col) / step_here + rate * dlogs
            ddt = gate * dstep * jax.nn.sigmoid(raw[:, rows])
            ddt_ref[0, :, rows] = ddt
            gb = gb + jnp.sum(ddt, axis=1, keepdims=True)
            ga = ga + gate * rate * jnp.sum(step_here * dlogs, axis=1, keepdims=True)
        skips = gate * jnp.sum(skip_ref[0], axis=0)
        skips = lane_sums(jnp.broadcast_to(skips, (8, heads * HP)), sum_part(heads, 0, heads * HP))
        rows = [flat(ga, 128), flat(gb, 128), skips[0:1]]
        tile = jnp.concatenate(rows + [jnp.zeros((TILE - 3, 128), F32)], axis=0)
        if more_ref is not None:
            tile = tile + more_ref[0]
        par_ref[...] = jnp.broadcast_to(tile[None], par_ref.shape)


def final_first(len_ref, gate_ref, *refs):
    final_kernel(0, (*refs[14:18], None, *refs[18:]), len_ref, gate_ref, *refs[:14])


def final_second(len_ref, gate_ref, *refs):
    final_kernel(1, (*refs[16:20], refs[14], *refs[20:]), len_ref, gate_ref, *refs[:14])


def groups_kernel(seq, gate_ref, b_ref, scal_ref, xv_ref, gg_ref, state_ref, dstate_ref, dxi_ref,
                  dbi_ref, dci_ref, *refs):
    dx_ref, db_ref, dc_ref, db_sc, dc_sc = refs[-5:]
    part = pl.program_id(0)
    gate = gate_ref[seq]

    @pl.when(part == 0)
    def _():
        db_sc[...] = dbi_ref[0]
        dc_sc[...] = dci_ref[0]

    tail_part = spread_part(NS // 16, 0, part * LANES, LANES)
    for blk in range(2):
        rows = slice(blk * QB, (blk + 1) * QB)
        db_sc[rows] += dot(xv_ref[0, rows], dstate_ref[blk], NT)
        dc_sc[rows] += dot(gg_ref[0, rows], state_ref[blk], NT)
        tail = dot(scal_ref[0, rows], tail_part, NN)
        u = tail * dot(b_ref[0, rows], dstate_ref[blk], NN)
        dx_ref[0, rows] = (gate * (dxi_ref[0, rows] + u)).astype(BF16)

    @pl.when(part == pl.num_programs(0) - 1)
    def _():
        db_ref[0] = (gate * db_sc[...]).astype(BF16)
        dc_ref[0] = (gate * dc_sc[...]).astype(BF16)


def sum_tensor(value):
    count = lax.axis_size("tensor")
    if count == 1:
        return value
    value = value + lax.ppermute(value, "tensor", [(i, i ^ 1) for i in range(count)])
    parts = [
        lax.ppermute(value, "tensor", [(i, (i + 2 * turn) % count) for i in range(count)])
        for turn in range(1, count // 2)
    ]
    return sum(parts, value)


def on_device(
    seq_inputs, b_proj, c_proj, dt_raw, dt_bias, a_log, d_skip, out_grad, log_ratio, lengths
):
    seqs, toks, width = seq_inputs.shape
    heads = dt_bias.shape[0]
    count = lax.axis_size("context")
    parts = width // LANES
    piece = NS // count
    chunk = 2 * (LANES // PAIR) * piece
    bias_row, alog_row, gain_row = dt_bias[None], a_log[None], d_skip[None]
    smem = pl.BlockSpec(memory_space=pltpu.SMEM)
    anywhere = pl.BlockSpec(memory_space=pl.ANY)
    params = pltpu.CompilerParams(vmem_limit_bytes=VMEM)
    whole = lambda *shape: pl.BlockSpec(shape, lambda *at: (0,) * len(shape))
    small = [whole(1, heads), whole(1, heads)]

    work = seqs * parts
    wide = pl.BlockSpec(
        (1, toks, LANES),
        lambda i: (jnp.minimum(i, work - 1) // parts, 0, jnp.minimum(i, work - 1) % parts),
    )
    thin = pl.BlockSpec((1, toks, NS), lambda i: (jnp.minimum(i, work - 1) // parts, 0, 0))
    state_out = pl.BlockSpec(
        (1, NS, LANES),
        lambda i: (jnp.minimum(i, work - 1) // parts, 0, jnp.minimum(i, work - 1) % parts),
    )
    local, first, last = pl.pallas_call(
        states_kernel,
        grid=(work + 1,),
        in_specs=[
            smem, wide, wide, thin, thin,
            pl.BlockSpec((1, heads, toks), lambda i: (jnp.minimum(i, work - 1) // parts, 0, 0)),
            *small, whole(*log_ratio.shape),
        ],
        out_specs=[pl.BlockSpec((count, chunk, PAIR), lambda i: (0, i, 0)), state_out, state_out],
        out_shape=[
            jax.ShapeDtypeStruct((count, work * chunk + TILE, PAIR), F32),
            jax.ShapeDtypeStruct((seqs, NS, width), F32),
            jax.ShapeDtypeStruct((seqs, NS, width), F32),
        ],
        scratch_shapes=[
            pltpu.VMEM((4, NS, QB), BF16), pltpu.VMEM((2, QB, 3 * 128), BF16),
            pltpu.VMEM((TILE, 128), F32),
        ],
        compiler_params=params,
        name="states",
    )(lengths, seq_inputs, out_grad, b_proj, c_proj, dt_raw, bias_row, alog_row, log_ratio)

    owned = lax.all_to_all(local, "context", 0, 0)

    tok_spec = lambda w: pl.BlockSpec((1, QB, w), lambda s, b: (s, b, 0))
    head_spec = pl.BlockSpec((1, heads, QB), lambda s, b: (s, 0, b))
    blocks = toks // QB
    dxi, dbi, dci, diff, col, skips, xv, gg, scal = pl.pallas_call(
        intra_kernel,
        grid=(seqs, blocks),
        in_specs=[smem, tok_spec(width), tok_spec(width), tok_spec(NS), tok_spec(NS),
                  head_spec, *small, whole(1, heads)],
        out_specs=[tok_spec(width), tok_spec(NS), tok_spec(NS), head_spec, head_spec,
                   pl.BlockSpec((1, 1, 1, width), lambda s, b: (s, b, 0, 0)),
                   tok_spec(width), tok_spec(width), tok_spec(3 * 128)],
        out_shape=[
            jax.ShapeDtypeStruct((seqs, toks, width), F32),
            jax.ShapeDtypeStruct((seqs, toks, NS), F32),
            jax.ShapeDtypeStruct((seqs, toks, NS), F32),
            jax.ShapeDtypeStruct((seqs, heads, toks), F32),
            jax.ShapeDtypeStruct((seqs, heads, toks), F32),
            jax.ShapeDtypeStruct((seqs, blocks, 1, width), F32),
            jax.ShapeDtypeStruct((seqs, toks, width), BF16),
            jax.ShapeDtypeStruct((seqs, toks, width), BF16),
            jax.ShapeDtypeStruct((seqs, toks, 3 * 128), BF16),
        ],
        scratch_shapes=[
            pltpu.VMEM((QB, width), F32), pltpu.VMEM((QB, width), F32),
            pltpu.VMEM((QB, width), BF16),
        ],
        compiler_params=params,
        name="intra",
    )(lengths, seq_inputs, out_grad, b_proj, c_proj, dt_raw, bias_row, alog_row, gain_row)

    def chained(seq):
        return pl.pallas_call(
            lambda *refs: chain_kernel(seq, heads, *refs),
            grid=(parts,),
            in_specs=[
                pl.BlockSpec((count, TILE, PAIR), lambda p: (0, work * chunk // TILE, 0)),
                pl.BlockSpec((count, chunk, PAIR), lambda p: (0, seq * parts + p, 0)),
            ],
            out_specs=[pl.BlockSpec((count, chunk, PAIR), lambda p: (0, p, 0)), whole(TILE, 128)],
            out_shape=[
                jax.ShapeDtypeStruct((count, parts * chunk, PAIR), F32),
                jax.ShapeDtypeStruct((TILE, 128), F32),
            ],
            scratch_shapes=[pltpu.VMEM((heads // 2, count, PAIR), F32)],
            compiler_params=params,
            name="chain",
        )(owned, owned)

    owned, dxi = lax.optimization_barrier((owned, dxi))
    chain0, sums = chained(0)
    back0 = lax.all_to_all(chain0, "context", 0, 0)
    chain1, _ = chained(1)
    back1 = lax.all_to_all(chain1, "context", 0, 0)
    totals = sum_tensor(sums[2:4])[:, 0]
    signs = jnp.where(jnp.arange(2, dtype=jnp.int32) == 0, -1.0, 1.0).astype(F32)
    margin = -jnp.sum(signs * totals)
    gate = signs * BETA * jax.nn.sigmoid(-BETA * margin)

    def final(seq, back, *before):
        of_seq = lambda *shape: pl.BlockSpec((1,) + shape, lambda p: (seq,) + (0,) * len(shape))
        laned = lambda rows: pl.BlockSpec((1, rows, LANES), lambda p: (seq, 0, p))
        halves = pl.BlockSpec((2, NS, LANES), lambda p: (0, 0, p))
        return pl.pallas_call(
            final_second if seq else final_first,
            grid=(parts,),
            in_specs=[
                smem, smem, laned(toks), laned(toks), of_seq(toks, NS), of_seq(toks, NS),
                of_seq(heads, toks), *small,
                pl.BlockSpec((count, chunk, PAIR), lambda p: (0, p, 0)),
                laned(NS), laned(NS), of_seq(toks, 3 * 128), of_seq(heads, toks),
                of_seq(heads, toks), of_seq(blocks, 1, width),
            ] + ([whole(1, TILE, 128), anywhere] if seq else []),
            out_specs=[of_seq(heads, toks), whole(count, TILE, 128), halves, halves],
            out_shape=[
                jax.ShapeDtypeStruct((seqs, heads, toks), F32),
                jax.ShapeDtypeStruct((count, TILE, 128), F32),
                jax.ShapeDtypeStruct((2, NS, width), BF16),
                jax.ShapeDtypeStruct((2, NS, width), BF16),
            ],
            scratch_shapes=[pltpu.VMEM((2, toks, 128), F32), pltpu.VMEM((2, 8, 128), F32)],
            input_output_aliases={17: 0} if seq else {},
            compiler_params=params,
            name="final",
        )(lengths, gate, seq_inputs, out_grad, b_proj, c_proj, dt_raw, bias_row, alog_row,
          back, first, last, scal, diff, col, skips, *before)

    def groups(seq, state, dstate, *before):
        of_seq = lambda *shape: pl.BlockSpec((1,) + shape, lambda p: (seq,) + (0,) * len(shape))
        laned = lambda rows: pl.BlockSpec((1, rows, LANES), lambda p: (seq, 0, p))
        halves = pl.BlockSpec((2, NS, LANES), lambda p: (0, 0, p))
        thin_of = of_seq(toks, NS)
        return pl.pallas_call(
            lambda *refs: groups_kernel(seq, *refs),
            grid=(parts,),
            in_specs=[smem, thin_of, of_seq(toks, 3 * 128), laned(toks), laned(toks), halves, halves,
                      laned(toks), thin_of, thin_of] + [anywhere] * len(before),
            out_specs=[laned(toks), thin_of, thin_of],
            out_shape=[jax.ShapeDtypeStruct((seqs, toks, w), BF16) for w in (width, NS, NS)],
            scratch_shapes=[pltpu.VMEM((toks, NS), F32), pltpu.VMEM((toks, NS), F32)],
            input_output_aliases={10: 0, 11: 1, 12: 2} if before else {},
            compiler_params=params,
            name="groups",
        )(gate, b_proj, scal, xv, gg, state, dstate, dxi, dbi, dci, *before)

    ddt, pars, state, dstate = final(0, back0)
    dx, db, dc = groups(0, state, dstate)
    back1, dx = lax.optimization_barrier((back1, dx))
    ddt, pars, state, dstate = final(1, back1, pars, ddt)
    closing = lax.all_to_all(pars, "context", 0, 0)
    dx, db, dc = groups(1, state, dstate, dx, db, dc)
    sums = jnp.sum(closing, axis=0)[:3, :heads]
    return dx, db, dc, ddt, sums[0], sums[1], sums[2]


def solution(mesh):
    return jax.shard_map(
        on_device,
        mesh=mesh,
        in_specs=(
            P(None, "context", "tensor"),
            P(None, "context", "tensor"),
            P(None, "context", "tensor"),
            P(None, "tensor", "context"),
            P("tensor"),
            P("tensor"),
            P("tensor"),
            P(None, "context", "tensor"),
            P(None, ("context", "tensor")),
            P(),
        ),
        out_specs=(
            P(None, "context", "tensor"),
            P(None, "context", "tensor"),
            P(None, "context", "tensor"),
            P(None, "tensor", "context"),
            P("tensor"),
            P("tensor"),
            P("tensor"),
        ),
        check_vma=False,
    )
```

time: 288 us -> 177 us (0.61)
  blocking collectives: 220 us -> 0 us
  waiting for transfers between devices: 0.01 us -> 82.4 us
  Pallas kernels: 44.6 us -> 63.4 us
  starting transfers between devices: 12 us -> 25.2 us
    psum x2 -> x0, blocking collectives: 144 us -> none  [the longest x1 106 us: on_device(): lax.psum(jnp.sum(ratio_live * log_ratio, axis=1), ('context', 'tensor'))]
    all_to_all x2 -> x4, waiting for transfers between devices: 0.01 us -> 77.5 us  [the longest x1 46 us: on_device(): owned = lax.all_to_all(local, 'context', 0, 0)]
    all_gather x1 -> x0, blocking collectives: 75.6 us -> none  [on_device(): decays = jnp.exp(lax.all_gather(logs, 'context'))]
    pallas_call x3 -> x7, Pallas kernels: 29 us -> 45.3 us  [the longest x2 18.5 us: final(): pl.pallas_call(final_second if seq else final_first, grid=(parts,), in_sp...]
    all_to_all x2 -> x4, starting transfers between devices: 12 us -> 19.8 us  [the longest x1 7.16 us: on_device(): owned = lax.all_to_all(local, 'context', 0, 0)]
    ppermute x0 -> x4, starting transfers between devices: none -> 5.43 us  [the longest x3 5.35 us: sum_tensor(): lax.ppermute(value, 'tensor', [(i, (i + 2 * turn) % count) for i in range...]
    ppermute x0 -> x4, waiting for transfers between devices: none -> 4.95 us  [the longest x3 3.82 us: sum_tensor(): lax.ppermute(value, 'tensor', [(i, (i + 2 * turn) % count) for i in range...]
    broadcast_in_dim x4 -> x0, local copies, waits for them, and re-layouts: 3.44 us -> none  [the longest x1 1.33 us: on_device(): bias_col = dt_bias[:, None]]
  transfers between devices with their start and end apart: 2 -> 8, of which waited for: 0 -> 6; matrix products, arithmetic and copies ran while one was open for 1% -> 1% of each run, Pallas kernels for 5% -> 23%
where the time goes in v2:
time: 177 us
  waiting for transfers between devices  82.4 us (47%)
  Pallas kernels  63.4 us (36%)
  starting transfers between devices  25.2 us (14%)
  local copies, waits for them, and re-layouts  3.3 us (2%)
    all_to_all x1, waiting for transfers between devices, on_device(): owned = lax.all_to_all(local, 'context', 0, 0)  46 us
    all_to_all x1, waiting for transfers between devices, on_device(): back0 = lax.all_to_all(chain0, 'context', 0, 0)  26.5 us
    pallas_call x2, Pallas kernels, final(): pl.pallas_call(final_second if seq else final_first, grid=(parts,), in_sp...  18.5 us
    pallas_call x1, Pallas kernels, on_device(): pl.pallas_call(intra_kernel, grid=(seqs, blocks), in_specs=[smem, tok_spe...  18.1 us
    pallas_call x2, Pallas kernels, groups(): pl.pallas_call(lambda *refs: groups_kernel(seq, *refs), grid=(parts,), in...  11.3 us
    pallas_call x1, Pallas kernels, on_device(): pl.pallas_call(states_kernel, grid=(work + 1,), in_specs=[smem, wide, wid...  9.81 us
    all_to_all x1, starting transfers between devices, on_device(): owned = lax.all_to_all(local, 'context', 0, 0)  7.16 us
    pallas_call x2, Pallas kernels, chained(): pl.pallas_call(lambda *refs: chain_kernel(seq, heads, *refs), grid=(parts...  5.7 us
  transfers between devices with their start and end apart: 8, of which 6 were waited for; matrix products, arithmetic and copies ran while one was open for 1% of the time, Pallas kernels for 23%

profile of v2, /device:TPU:0, one launch (start us, length us, event | category | flops | bytes accessed | tf_op | source)
XLA Modules:
  0.0 176.9 jit_solution(6641789241270731827)
XLA Ops:
  0.6 9.8 %states.1 = (f32[16,520,128]{2,1,0:T(8,128)}, f32[2,256,1024]{2,1,0:T(8,128)}, f32[2,256,1024]{2,1,0:T(8,128)}) custom-call(s32[2]{0:T(128)} %len_ref.7, bf16[2,512,1024]{2,1,0:T(8,128)(2,1)} %refs_0_.3, bf16[2,512,1024]{2,1,0:T(8,128)(2,1)} %refs_1_.6, bf16[2,512,256]{2,1,0:T(8,128)(2,1)} %refs_1_.7, bf16[2,512,256]{2,1,0:T(8,128)(2,1)} %refs_3_.3, ...), custom_call_target="tpu_custom_call" | custom-call | tf_op jit(solution)/shard_map/states/pallas_call | solution.py:458
  10.4 7.2 %all-to-all-start = ((f32[16,520,128]{2,1,0:T(8,128)}), f32[16,520,128]{2,1,0:T(8,128)}, u32[]{:S(2)}, u32[]{:S(2)}) async-start(f32[16,520,128]{2,1,0:T(8,128)} %get-tuple-element.40), calls=%async_computation | async-start | bytes 8519680 | tf_op jit(solution)/shard_map/all_to_all | solution.py:480
  17.6 18.1 %intra.1 = (f32[2,512,1024]{2,1,0:T(8,128)}, f32[2,512,256]{2,1,0:T(8,128)}, f32[2,512,256]{2,1,0:T(8,128)}, f32[2,16,512]{2,1,0:T(8,128)}, f32[2,16,512]{2,1,0:...) custom-call(s32[2]{0:T(128)} %len_ref.7, ...), custom_call_target="tpu_custom_call" | custom-call | tf_op jit(solution)/shard_map/intra/pallas_call | solution.py:485
  35.7 46.0 %all-to-all-done.refs_0_.refs_1_ = f32[16,520,128]{2,1,0:T(8,128)} async-done(((f32[16,520,128]{2,1,0:T(8,128)}), f32[16,520,128]{2,1,0:T(8,128)}, u32[]{:S(2)}, u32[]{:S(2)}) %all-to-all-start) | async-done | bytes 4259872 | tf_op jit(solution)/shard_map/all_to_all | solution.py:480
  81.8 2.8 %chain.2 = (f32[16,256,128]{2,1,0:T(8,128)}, f32[8,128]{1,0:T(8,128)}) custom-call(f32[16,520,128]{2,1,0:T(8,128)} %all-to-all-done.refs_0_.refs_1_, f32[16,520,128]{2,1,0:T(8,128)} %all-to-all-done.refs_0_.refs_1_), custom_call_target="tpu_custom_call" | custom-call | tf_op jit(solution)/shard_map/chain/pallas_call | solution.py:513
  84.6 4.6 %all-to-all-start.2 = ((f32[16,256,128]{2,1,0:T(8,128)}), f32[16,256,128]{2,1,0:T(8,128)S(1)}, u32[]{:S(2)}, u32[]{:S(2)}) async-start(f32[16,256,128]{2,1,0:T(8,128)} %get-tuple-element.48), calls=%async_computation.2 | async-start | bytes 4194304 | tf_op jit(solution)/shard_map/all_to_all | solution.py:532
  89.2 2.9 %chain.3 = (f32[16,256,128]{2,1,0:T(8,128)}, f32[8,128]{1,0:T(8,128)}) custom-call(f32[16,520,128]{2,1,0:T(8,128)} %all-to-all-done.refs_0_.refs_1_, f32[16,520,128]{2,1,0:T(8,128)} %all-to-all-done.refs_0_.refs_1_), custom_call_target="tpu_custom_call" | custom-call | tf_op jit(solution)/shard_map/chain/pallas_call | solution.py:513
  92.1 26.5 %all-to-all-done.2.refs_7_ = f32[16,256,128]{2,1,0:T(8,128)S(1)} async-done(((f32[16,256,128]{2,1,0:T(8,128)}), f32[16,256,128]{2,1,0:T(8,128)S(1)}, u32[]{:S(2)}, u32[]{:S(2)}) %all-to-all-start.2) | async-done | bytes 2097184 | tf_op jit(solution)/shard_map/all_to_all | solution.py:532
  118.6 1.3 copy-done.1
  119.9 3.7 %all-to-all-start.1 = ((f32[16,256,128]{2,1,0:T(8,128)}), f32[16,256,128]{2,1,0:T(8,128)S(1)}, u32[]{:S(2)}, u32[]{:S(2)}) async-start(f32[16,256,128]{2,1,0:T(8,128)} %get-tuple-element.47), calls=%async_computation.1 | async-start | bytes 4194304 | tf_op jit(solution)/shard_map/all_to_all | solution.py:534
  123.8 1.1 collective-permute-done
  124.9 4.1 %collective-permute-start.3 = (f32[2,128]{1,0:T(2,128)S(1)}, f32[2,128]{1,0:T(2,128)S(1)}, u32[]{:S(2)}, u32[]{:S(2)}) collective-permute-start(f32[2,128]{1,0:T(2,128)S(1)} %slice_add_fusion), channel_id=1, source_target_pairs={{0,6},{1,7},{2,0},{3,1},{4,2},{5,3},{6,4},{7,5},{8,14},{9,15},{10,... | collective-permute-start | bytes 3080 | tf_op jit(solution)/shard_map/ppermute | solution.py:426
  129.0 1.2 collective-permute-start.1
  130.3 3.8 %collective-permute-done.2 = f32[2,128]{1,0:T(2,128)S(1)} collective-permute-done((f32[2,128]{1,0:T(2,128)S(1)}, f32[2,128]{1,0:T(2,128)S(1)}, u32[]{:S(2)}, u32[]{:S(2)}) %collective-permute-start.2) | collective-permute-done | bytes 1056 | tf_op jit(solution)/shard_map/ppermute | solution.py:426
  134.2 0.6 multiply_reduce_fusion
  136.1 9.2 %final.2 = (f32[2,16,512]{2,1,0:T(8,128)}, f32[16,8,128]{2,1,0:T(8,128)}, bf16[2,256,1024]{2,1,0:T(8,128)(2,1)}, bf16[2,256,1024]{2,1,0:T(8,128)(2,1)}) custom-call(s32[2]{0:T(128)} %len_ref.7, f32[2]{0:T(128)} %fusion.gate_ref.refs_0_, bf16[2,512,1024]{2,1,0:T(8,128)(2,1)} %refs_0_.3, bf16[2,512,1024]{2,1,0:T(8,128)(2,1)} %refs_1_.6, ...), custom_call_target="tpu_custom_call" | custom-call | tf_op jit(solution)/shard_map/final/pallas_call | solution.py:544
  145.3 5.6 %groups.2 = (bf16[2,512,1024]{2,1,0:T(8,128)(2,1)}, bf16[2,512,256]{2,1,0:T(8,128)(2,1)}, bf16[2,512,256]{2,1,0:T(8,128)(2,1)}) custom-call(f32[2]{0:T(128)} %fusion.gate_ref.refs_0_, bf16[2,512,256]{2,1,0:T(8,128)(2,1)} %refs_1_.7, bf16[2,512,384]{2,1,0:T(8,128)(2,1)} %get-tuple-element.44.refs_10_.refs_2_, ...), custom_call_target="tpu_custom_call" | custom-call | tf_op jit(solution)/shard_map/groups/pallas_call | solution.py:573
  151.0 2.9 %all-to-all-done.1.refs_7_ = f32[16,256,128]{2,1,0:T(8,128)S(1)} async-done(((f32[16,256,128]{2,1,0:T(8,128)}), f32[16,256,128]{2,1,0:T(8,128)S(1)}, u32[]{:S(2)}, u32[]{:S(2)}) %all-to-all-start.1) | async-done | bytes 2097184 | tf_op jit(solution)/shard_map/all_to_all | solution.py:534
  153.9 1.3 copy-done
  155.2 9.2 %final.3 = (f32[2,16,512]{2,1,0:T(8,128)}, f32[16,8,128]{2,1,0:T(8,128)}, bf16[2,256,1024]{2,1,0:T(8,128)(2,1)}, bf16[2,256,1024]{2,1,0:T(8,128)(2,1)}) custom-call(s32[2]{0:T(128)} %len_ref.7, f32[2]{0:T(128)} %fusion.gate_ref.refs_0_, bf16[2,512,1024]{2,1,0:T(8,128)(2,1)} %refs_0_.3, ...), custom_call_target="tpu_custom_call", output_to_operand_aliasing={{0}: (17, {})} | custom-call | tf_op jit(solution)/shard_map/final/pallas_call | solution.py:544
  164.4 4.2 %all-to-all-start.3 = ((f32[16,8,128]{2,1,0:T(8,128)}), f32[16,8,128]{2,1,0:T(8,128)S(1)}, u32[]{:S(2)}, u32[]{:S(2)}) async-start(f32[16,8,128]{2,1,0:T(8,128)} %get-tuple-element.72), calls=%async_computation.3 | async-start | bytes 131072 | tf_op jit(solution)/shard_map/all_to_all | solution.py:590
  168.7 5.7 %groups.3 = (bf16[2,512,1024]{2,1,0:T(8,128)(2,1)}, bf16[2,512,256]{2,1,0:T(8,128)(2,1)}, bf16[2,512,256]{2,1,0:T(8,128)(2,1)}) custom-call(f32[2]{0:T(128)} %fusion.gate_ref.refs_0_, bf16[2,512,256]{2,1,0:T(8,128)(2,1)} %refs_1_.7, ...), custom_call_target="tpu_custom_call", output_to_operand_aliasing={{0}: (10, {}), {1}: (11, {}), {2}: (12, {})} | custom-call | tf_op jit(solution)/shard_map/groups/pallas_call | solution.py:573
  174.4 2.0 %all-to-all-done.3 = f32[16,8,128]{2,1,0:T(8,128)S(1)} async-done(((f32[16,8,128]{2,1,0:T(8,128)}), f32[16,8,128]{2,1,0:T(8,128)S(1)}, u32[]{:S(2)}, u32[]{:S(2)}) %all-to-all-start.3) | async-done | bytes 65568 | tf_op jit(solution)/shard_map/all_to_all | solution.py:590
  176.4 0.5 slice_bitcast_fusion
  (14 shorter events, 0.8 us)
Async XLA Ops:
  10.4 71.3 %all-to-all-start = ((f32[16,520,128]{2,1,0:T(8,128)}), f32[16,520,128]{2,1,0:T(8,128)}, u32[]{:S(2)}, u32[]{:S(2)}) async-start(f32[16,520,128]{2,1,0:T(8,128)} %get-tuple-element.40), calls=%async_computation | async-start | bytes 8519680 | tf_op jit(solution)/shard_map/all_to_all | solution.py:480
  84.6 34.0 %all-to-all-start.2 = ((f32[16,256,128]{2,1,0:T(8,128)}), f32[16,256,128]{2,1,0:T(8,128)S(1)}, u32[]{:S(2)}, u32[]{:S(2)}) async-start(f32[16,256,128]{2,1,0:T(8,128)} %get-tuple-element.48), calls=%async_computation.2 | async-start | bytes 4194304 | tf_op jit(solution)/shard_map/all_to_all | solution.py:532
  118.6 1.3 copy-start.1
  118.6 5.0 %copy-start.2 = (f32[8,128]{1,0:T(8,128)S(1)}, f32[8,128]{1,0:T(8,128)}, u32[]{:S(2)}) copy-start(f32[8,128]{1,0:T(8,128)} %get-tuple-element.43) | copy-start | bytes 12292
  119.9 33.9 %all-to-all-start.1 = ((f32[16,256,128]{2,1,0:T(8,128)}), f32[16,256,128]{2,1,0:T(8,128)S(1)}, u32[]{:S(2)}, u32[]{:S(2)}) async-start(f32[16,256,128]{2,1,0:T(8,128)} %get-tuple-element.47), calls=%async_computation.1 | async-start | bytes 4194304 | tf_op jit(solution)/shard_map/all_to_all | solution.py:534
  123.7 1.2 collective-permute-start
  124.9 5.4 %collective-permute-start.3 = (f32[2,128]{1,0:T(2,128)S(1)}, f32[2,128]{1,0:T(2,128)S(1)}, u32[]{:S(2)}, u32[]{:S(2)}) collective-permute-start(f32[2,128]{1,0:T(2,128)S(1)} %slice_add_fusion), channel_id=1, source_target_pairs={{0,6},{1,7},{2,0},{3,1},{4,2},{5,3},{6,4},{7,5},{8,14},{9,15},{10,... | collective-permute-start | bytes 3080 | tf_op jit(solution)/shard_map/ppermute | solution.py:426
  129.0 5.1 %collective-permute-start.2 = (f32[2,128]{1,0:T(2,128)S(1)}, f32[2,128]{1,0:T(2,128)S(1)}, u32[]{:S(2)}, u32[]{:S(2)}) collective-permute-start(f32[2,128]{1,0:T(2,128)S(1)} %slice_add_fusion), channel_id=1, source_target_pairs={{0,4},{1,5},{2,6},{3,7},{4,0},{5,1},{6,2},{7,3},{8,12},{9,13},{10,... | collective-permute-start | bytes 3080 | tf_op jit(solution)/shard_map/ppermute | solution.py:426
  129.0 5.1 %collective-permute-start.1 = (f32[2,128]{1,0:T(2,128)S(1)}, f32[2,128]{1,0:T(2,128)S(1)}, u32[]{:S(2)}, u32[]{:S(2)}) collective-permute-start(f32[2,128]{1,0:T(2,128)S(1)} %slice_add_fusion), channel_id=1, source_target_pairs={{0,2},{1,3},{2,4},{3,5},{4,6},{5,7},{6,0},{7,1},{8,10},{9,11},{10,... | collective-permute-start | bytes 3080 | tf_op jit(solution)/shard_map/ppermute | solution.py:426
  153.9 1.3 copy-start
  164.4 11.9 %all-to-all-start.3 = ((f32[16,8,128]{2,1,0:T(8,128)}), f32[16,8,128]{2,1,0:T(8,128)S(1)}, u32[]{:S(2)}, u32[]{:S(2)}) async-start(f32[16,8,128]{2,1,0:T(8,128)} %get-tuple-element.72), calls=%async_computation.3 | async-start | bytes 131072 | tf_op jit(solution)/shard_map/all_to_all | solution.py:590

commit v3 on v2

v3 whole, which is shorter than its diff:
```python
import jax
import jax.numpy as jnp
import numpy as np
from jax import lax
from jax.experimental import pallas as pl
from jax.experimental.pallas import tpu as pltpu
from jax.sharding import PartitionSpec as P

HP = 64
NS = 256
QB = 256
HALF = 128
BETA = 0.5
PAIR = 2 * HP
LANES = 8 * HP
TILE = 8
VMEM = 56 * 1024 * 1024
F32 = jnp.float32
BF16 = jnp.bfloat16
HIGH = lax.Precision.HIGHEST


def dot(lhs, rhs, dims, precision=None):
    return lax.dot_general(
        lhs, rhs, (dims, ((), ())), precision=precision, preferred_element_type=F32
    )


NN = ((1,), (0,))
NT = ((1,), (1,))
TN = ((0,), (0,))


def split3(value):
    top = value.astype(BF16)
    rest = value - top.astype(F32)
    mid = rest.astype(BF16)
    return top, mid, (rest - mid.astype(F32)).astype(BF16)


def spread_matrix(heads):
    row = lax.broadcasted_iota(jnp.int32, (3 * heads, heads * HP), 0)
    lane = lax.broadcasted_iota(jnp.int32, (3 * heads, heads * HP), 1)
    return (lax.rem(row, heads) == lax.div(lane, HP)).astype(BF16)


def spread(values, ones_rows):
    return dot(jnp.concatenate(split3(values), axis=0), ones_rows, TN)


def head_sums(product, ones_rows, heads):
    top = product.astype(BF16)
    low = (product - top.astype(F32)).astype(BF16)
    ones = ones_rows[:heads]
    return dot(ones, top, NT) + dot(ones, low, NT)


def softplus(value):
    return jnp.maximum(value, 0.0) + jnp.log1p(jnp.exp(-jnp.abs(value)))


def upper_ones():
    row = lax.broadcasted_iota(jnp.int32, (QB, QB), 0)
    col = lax.broadcasted_iota(jnp.int32, (QB, QB), 1)
    return (row <= col).astype(BF16)


def running_sum(values, ones, dims=NN):
    rows = values.shape[0]
    sums = dot(jnp.concatenate(split3(values), axis=0), ones, dims)
    return sums[:rows] + sums[rows : 2 * rows] + sums[2 * rows :]


def live_rows(base, length, count):
    row = lax.broadcasted_iota(jnp.int32, (count, 1), 0)
    return base + row < length


def column(row_ref):
    heads = row_ref.shape[1]
    same = lax.broadcasted_iota(jnp.int32, (heads, heads), 0) == lax.broadcasted_iota(
        jnp.int32, (heads, heads), 1
    )
    return jnp.sum(jnp.where(same, row_ref[...], 0.0), axis=1, keepdims=True)


def token_base(toks):
    return lax.axis_index("context") * toks


def flat(column_values, lanes):
    heads = column_values.shape[0]
    same = lax.broadcasted_iota(jnp.int32, (heads, lanes), 0) == lax.broadcasted_iota(
        jnp.int32, (heads, lanes), 1
    )
    return jnp.sum(jnp.where(same, column_values, 0.0), axis=0, keepdims=True)


GAP = 32


def scale_columns(tail, grow):
    rows = jnp.concatenate([tail, grow], axis=0)
    parts = [part.astype(F32) for part in split3(rows)]
    return jnp.concatenate(parts + [jnp.zeros_like(rows)], axis=0).T.astype(BF16)


def spreads(heads):
    row, lane = np.arange(128)[:, None], np.arange(heads * HP)[None, :] // HP
    used = row < 3 * GAP
    return np.stack([used & (row % GAP == lane), used & (row % GAP == lane + GAP // 2)])


def gathers(heads):
    lane, col = np.arange(heads * HP)[:, None] // HP, np.arange(128)[None, :]
    return np.stack([lane == col, lane == col - GAP // 2])


def lane_sums(product, ones_part):
    top = product.astype(BF16)
    low = (product - top.astype(F32)).astype(BF16)
    return dot(top, ones_part, NN) + dot(low, ones_part, NN)


def exact_dot(lhs, rhs, dims):
    top = rhs.astype(BF16)
    low = (rhs - top.astype(F32)).astype(BF16)
    return dot(lhs, top, dims) + dot(lhs, low, dims)


def device_sums(step, rate, ones):
    logs = step * rate
    heads = step.shape[0]
    both = running_sum(jnp.concatenate([logs[:, :QB], logs[:, QB:]], axis=0), ones)
    return both[:heads], both[heads:]


def states_kernel(len_ref, x_ref, g_ref, b_ref, c_ref, dt_ref, bias_ref, alog_ref, ratio_ref,
                  spread_ref, out_ref, scal_sc, tile_sc):
    heads = dt_ref.shape[1]
    toks = x_ref.shape[1]
    pieces = out_ref.shape[0]
    piece = NS // pieces
    at = pl.program_id(0)
    work = 2

    @pl.when(at == 0)
    def _():
        ones = upper_ones()
        bias, rate = column(bias_ref), -jnp.exp(column(alog_ref))
        for seq in range(2):
            step = softplus(dt_ref[seq] + bias)
            cums = device_sums(step, rate, ones)
            mid = cums[0][:, QB - 1 : QB]
            last = mid + cums[1][:, QB - 1 : QB]
            for blk in range(2):
                rows = slice(blk * QB, (blk + 1) * QB)
                cum = cums[blk] + blk * mid
                scal_sc[seq, rows] = scale_columns(jnp.exp(last - cum) * step[:, rows], jnp.exp(cum))
            tile_sc[seq : seq + 1] = flat(jnp.exp(last), 128)

    @pl.when(at < work)
    def _():
        scal = scal_sc[at]
        x_tail = x_ref[0].astype(F32) * dot(scal, spread_ref[0], NN)
        live = live_rows(token_base(toks), len_ref[at], toks)
        g_grow = jnp.where(live, g_ref[0].astype(F32) * dot(scal, spread_ref[1], NN), 0.0)
        whole = (exact_dot(b_ref[0].T, x_tail, NN), exact_dot(c_ref[0].T, g_grow, NN))
        for scan in range(2):
            for pair in range(heads // 2):
                row = (2 * pair + scan) * piece
                out_ref[:, row : row + piece] = whole[scan][:, pair * PAIR : (pair + 1) * PAIR].reshape(
                    pieces, piece, PAIR
                )

    @pl.when(at == work)
    def _():
        ratio = ratio_ref[...]
        rows = ratio.shape[1]
        first = lax.axis_index(("context", "tensor")) * rows
        place = lax.broadcasted_iota(jnp.int32, ratio.shape, 1) + first
        seq = lax.broadcasted_iota(jnp.int32, ratio.shape, 0)
        length = jnp.where(seq == 0, len_ref[0], len_ref[1])
        totals = jnp.sum(jnp.where(place < length, ratio, 0.0), axis=1, keepdims=True)
        tile_sc[2:4] = jnp.broadcast_to(totals, (2, 128))
        tile_sc[4:] = jnp.zeros((TILE - 4, 128), F32)
        out_ref[:, 0:TILE] = jnp.broadcast_to(tile_sc[...][None], (pieces, TILE, 128))


def chain_kernel(unit, heads, tile_ref, in_ref, spread_ref, out_ref, sums_ref, decay_sc):
    count = in_ref.shape[0]
    piece = NS // count
    parts = heads * HP // LANES
    at = pl.program_id(0) + unit
    part = lax.rem(at, parts)

    @pl.when(pl.program_id(0) == 0)
    def _():
        tiles = [tile_ref[src] for src in range(count)]
        sums_ref[...] = sum(tiles[1:], tiles[0])
        decay = jnp.concatenate(
            [tile[seq : seq + 1] for seq in range(2) for tile in tiles], axis=0
        )
        top, mid, low = [split.astype(F32) for split in split3(decay)]
        columns = top + pltpu.roll(mid, GAP, 1) + pltpu.roll(low, 2 * GAP, 1)
        wide = dot(columns.astype(BF16), spread_ref[0], NN)
        for seq in range(2):
            for pair in range(heads // 2):
                decay_sc[seq * (heads // 2) + pair] = wide[
                    seq * count : (seq + 1) * count, pair * PAIR : (pair + 1) * PAIR
                ]

    pairs = LANES // PAIR
    for pair in range(pairs):
        decay = decay_sc[lax.div(at, parts) * (heads // 2) + part * pairs + pair]
        rows = slice(2 * pair * piece, (2 * pair + 1) * piece)
        total = jnp.zeros((piece, PAIR), F32)
        for src in range(count):
            out_ref[src, rows] = total
            total = decay[src : src + 1] * total + in_ref[src, rows]
        rows = slice((2 * pair + 1) * piece, (2 * pair + 2) * piece)
        total = jnp.zeros((piece, PAIR), F32)
        for src in reversed(range(count)):
            out_ref[src, rows] = total
            total = decay[src : src + 1] * total + in_ref[src, rows]


def intra_kernel(len_ref, x_ref, g_ref, b_ref, c_ref, dt_ref, bias_ref, alog_ref, gain_ref, gather_ref,
                 dx_ref, db_ref, dc_ref, diff_ref, col_ref, skip_ref, xv_ref, gg_ref, scal_ref, near_ref, aux_ref,
                 y_sc, d_sc, g_sc):
    heads = dt_ref.shape[1]
    seq, blk = pl.program_id(0), pl.program_id(1)
    ones_rows = spread_matrix(heads)
    raw = dt_ref[0] + column(bias_ref)
    step_all = softplus(raw)
    rate = -jnp.exp(column(alog_ref))
    cums = device_sums(step_all, rate, upper_ones())
    first = blk == 0
    cum = jnp.where(first, cums[0], cums[1])
    step = jnp.where(first, step_all[:, :QB], step_all[:, QB:])
    raw = jnp.where(first, raw[:, :QB], raw[:, QB:])
    cum_t = cum.T
    mid, over = cums[0][:, QB - 1 : QB], cums[1][:, QB - 1 : QB]
    slope = jax.nn.sigmoid(raw)
    aux_ref[0, 0] = slope / step
    aux_ref[0, 1] = slope * rate
    aux_ref[0, 2] = step * rate
    tail = jnp.exp(cum[:, QB - 1 : QB] - cum) * step
    grow = jnp.exp(cum)
    near_ref[0] = scale_columns(tail, grow)
    tail = jnp.exp(jnp.where(first, mid + over, over) - cum) * step
    grow = jnp.exp(cum + jnp.where(first, 0.0, mid))
    scal_ref[0] = scale_columns(tail, grow)
    live = live_rows(token_base(pl.num_programs(1) * QB) + blk * QB, len_ref[seq], QB)
    x_full = x_ref[0].astype(F32)
    g_full = jnp.where(live, g_ref[0].astype(F32), 0.0)
    g_sc[...] = g_full.astype(BF16)
    skips = jnp.sum(x_full * g_full, axis=0, keepdims=True)
    skip_ref[0, 0] = lane_sums(jnp.broadcast_to(skips, (TILE, heads * HP)), gather_ref[0])
    xv_ref[0] = (x_full * spread(tail, ones_rows)).astype(BF16)
    gg_ref[0] = (g_full * spread(grow, ones_rows)).astype(BF16)
    gram = dot(c_ref[0], b_ref[0], NT)
    causal = (
        lax.broadcasted_iota(jnp.int32, (HALF, HALF), 0)
        >= lax.broadcasted_iota(jnp.int32, (HALF, HALF), 1)
    )
    low, high = slice(0, HALF), slice(HALF, QB)
    tiles = ((low, low), (high, low), (high, high))
    grams = [jnp.where(causal, gram[t, k], 0.0) if t is k else gram[t, k] for t, k in tiles]
    left = lax.broadcasted_iota(jnp.int32, (QB, PAIR), 1) < HP
    zero = jnp.zeros((QB, PAIR), BF16)
    dgrams = [jnp.zeros((HALF, HALF), F32) for _ in tiles]
    for pair in range(heads // 2):
        lanes = slice(pair * PAIR, (pair + 1) * PAIR)
        xx = x_ref[0, :, lanes]
        gg = g_sc[:, lanes]
        gs = [jnp.where(left, gg, zero), jnp.where(left, zero, gg)]
        xs = [jnp.where(left, xx, zero), jnp.where(left, zero, xx)]
        weights = []
        for one in range(2):
            head = 2 * pair + one
            mine = []
            dlow = dot(gs[one], xx[low], NT)
            dhigh = dot(gs[one][high], xx[high], NT)
            dparts = (dlow[low], dlow[high], dhigh)
            for which, (t, k) in enumerate(tiles):
                gap = cum_t[t, head : head + 1] - cum[head : head + 1, k]
                if t is k:
                    gap = jnp.minimum(gap, 0.0)
                decay = jnp.exp(gap) * step[head : head + 1, k]
                mine.append((grams[which] * decay).astype(BF16))
                dgrams[which] = dgrams[which] + dparts[which] * decay
            weights.append(mine)
        (a0, a1, a2), (b0, b1, b2) = weights
        y_sc[low, lanes] = dot(
            jnp.concatenate([a0, b0], axis=1), jnp.concatenate([xs[0][low], xs[1][low]], axis=0), NN
        )
        y_sc[high, lanes] = dot(
            jnp.concatenate([a1, a2, b1, b2], axis=1), jnp.concatenate(xs, axis=0), NN
        )
        d_sc[low, lanes] = dot(
            jnp.concatenate([a0, a1, b0, b1], axis=0), jnp.concatenate(gs, axis=0), TN
        )
        d_sc[high, lanes] = dot(
            jnp.concatenate([a2, b2], axis=0),
            jnp.concatenate([gs[0][high], gs[1][high]], axis=0), TN,
        )
    row = head_sums(g_full * y_sc[...], ones_rows, heads)
    col = head_sums(x_full * d_sc[...], ones_rows, heads)
    diff_ref[0] = row - col
    col_ref[0] = col
    gain = spread(jnp.broadcast_to(column(gain_ref), (heads, 8)), ones_rows)[0:1]
    dx_ref[0] = d_sc[...] + gain * g_full
    dgram = jnp.concatenate(
        [
            jnp.concatenate(
                [jnp.where(causal, dgrams[0], 0.0), jnp.zeros((HALF, HALF), F32)], axis=1
            ),
            jnp.concatenate([dgrams[1], jnp.where(causal, dgrams[2], 0.0)], axis=1),
        ],
        axis=0,
    ).astype(BF16)
    dc_ref[0] = dot(dgram, b_ref[0], NN)
    db_ref[0] = dot(dgram, c_ref[0], TN)


def cross_kernel(len_ref, x_ref, g_ref, b_ref, c_ref, near_ref, spread_ref, gather_ref,
                 diff_ref, col_ref, dxi_ref, dbi_ref, dci_ref,
                 dlog_ref, cols_ref, dx_ref, db_ref, dc_ref):
    heads = diff_ref.shape[1]
    seq = pl.program_id(0)
    toks = near_ref.shape[1]
    x_tail = x_ref[0].astype(F32) * dot(near_ref[0, :QB], spread_ref[0], NN)
    live = live_rows(token_base(toks) + QB, len_ref[seq], QB)
    g_grow = jnp.where(live, g_ref[0].astype(F32), 0.0) * dot(near_ref[0, QB:], spread_ref[1], NN)
    early, late = x_tail.astype(BF16), g_grow.astype(BF16)
    b_early, c_late = b_ref[0], c_ref[0]
    gram = dot(c_late, b_early, NT)
    y, back = 0.0, 0.0
    for part in split3(gram)[:2]:
        y = y + exact_dot(part, x_tail, NN)
        back = back + exact_dot(part, g_grow, TN)
    dgram = dot(late, early, NT).astype(BF16)
    dc_ref[0] = dci_ref[0] + dot(dgram, b_early, NN)
    db_ref[0] = dbi_ref[0] + dot(dgram, c_late, TN)
    dx_ref[0] = dxi_ref[0] + dot(near_ref[0, :QB], spread_ref[0], NN) * back
    row = lane_sums(g_grow * y, gather_ref[0]).T[:heads]
    col = lane_sums(x_tail * back, gather_ref[0]).T[:heads]
    ones = upper_ones()
    dlog_ref[0, :, :QB] = (
        running_sum(diff_ref[0, :, :QB], ones, NT) + running_sum(col, ones) - col
    )
    dlog_ref[0, :, QB:] = running_sum(diff_ref[0, :, QB:] + row, ones, NT)
    cols_ref[0, :, :QB] = col_ref[0, :, :QB] + col
    cols_ref[0, :, QB:] = col_ref[0, :, QB:]


def state_of(ends_ref, scan):
    piece = NS // ends_ref.shape[0]
    pairs = ends_ref.shape[1] // (2 * piece)
    return jnp.concatenate(
        [
            ends_ref[:, (2 * p + scan) * piece : (2 * p + scan + 1) * piece].reshape(NS, PAIR)
            for p in range(pairs)
        ],
        axis=1,
    )


def final_kernel(unit, heads, len_ref, gate_ref, x_ref, g_ref, b_ref, c_ref, ends_ref, scal_ref,
                 aux_ref, dlog_ref, cols_ref, skip_ref, spread_ref, gather_ref, *refs):
    ddt_ref, par_ref, part_ref, thru_ref, sum_sc, thru_sc, tile_sc = refs[-7:]
    before = refs[:-7]
    toks = x_ref.shape[1]
    parts = heads * HP // LANES
    at = pl.program_id(0) + unit
    seq, part = lax.div(at, parts), lax.rem(at, parts)
    gate = gate_ref[seq]

    @pl.when(pl.program_id(0) == 0)
    def _():
        tile_sc[...] = before[0][0] if before else jnp.zeros_like(tile_sc)
        if before:
            sum_sc[...] = before[1][...]
            thru_sc[...] = before[2][...]

    @pl.when(part == 0)
    def _():
        sum_sc[...] = jnp.zeros_like(sum_sc)
        thru_sc[...] = jnp.zeros_like(thru_sc)

    enter, leave = state_of(ends_ref, 0), state_of(ends_ref, 1)
    for blk in range(2):
        rows = slice(blk * QB, (blk + 1) * QB)
        live = live_rows(token_base(toks) + blk * QB, len_ref[seq], QB)
        grow = dot(scal_ref[0, rows], spread_ref[1], NN)
        g_grow = jnp.where(live, g_ref[0, rows].astype(F32) * grow, 0.0)
        y = exact_dot(c_ref[0, rows], enter, NN)
        tail = dot(scal_ref[0, rows], spread_ref[0], NN)
        u = tail * exact_dot(b_ref[0, rows], leave, NN)
        sum_sc[rows] += lane_sums(g_grow * y, gather_ref[0]) + lane_sums(
            x_ref[0, rows].astype(F32) * u, gather_ref[1]
        )
    product = grow[QB - 1 : QB] * jnp.sum(enter * leave, axis=0, keepdims=True)
    thru_sc[...] += lane_sums(jnp.broadcast_to(product, (TILE, LANES)), gather_ref[0])

    @pl.when(part == parts - 1)
    def _():
        ones = upper_ones()
        halves = [slice(blk * QB, (blk + 1) * QB) for blk in range(2)]
        sums = [sum_sc[rows].T for rows in halves]
        both = jnp.concatenate([half[:heads] for half in sums], axis=0)
        cols = jnp.concatenate([half[heads : 2 * heads] for half in sums], axis=0)
        later = running_sum(both, ones, NT)
        earlier = running_sum(cols, ones)
        thru = thru_sc[...].T[:heads, 0:1]
        rest = (
            later[heads:, 0:1] + thru,
            earlier[:heads, QB - 1 : QB] + thru,
        )
        gb = jnp.zeros((heads, 1), F32)
        ga = jnp.zeros((heads, 1), F32)
        for blk, rows in enumerate(halves):
            mine = slice(blk * heads, (blk + 1) * heads)
            dlog = dlog_ref[0, :, rows] + later[mine] + earlier[mine] - cols[mine] + rest[blk]
            col = cols_ref[0, :, rows] + cols[mine]
            ddt = gate * (aux_ref[0, 0, :, rows] * col + aux_ref[0, 1, :, rows] * dlog)
            ddt_ref[0, :, rows] = ddt
            gb = gb + jnp.sum(ddt, axis=1, keepdims=True)
            ga = ga + gate * jnp.sum(aux_ref[0, 2, :, rows] * dlog, axis=1, keepdims=True)
        skips = gate * (skip_ref[0, 0] + skip_ref[0, 1])
        rows = [flat(ga, 128), flat(gb, 128), skips[0:1]]
        tile_sc[...] += jnp.concatenate(rows + [jnp.zeros((TILE - 3, 128), F32)], axis=0)

    @pl.when(pl.program_id(0) == pl.num_programs(0) - 1)
    def _():
        par_ref[...] = jnp.broadcast_to(tile_sc[...][None], par_ref.shape)
        part_ref[...] = sum_sc[...]
        thru_ref[...] = thru_sc[...]


def groups_kernel(seq, gate_ref, b_ref, scal_ref, xv_ref, gg_ref, dxi_ref, dbi_ref, dci_ref,
                  spread_ref, *refs):
    dx_ref, db_ref, dc_ref, db_sc, dc_sc = refs[-5:]
    ends = refs[:2] if seq else refs[:1]
    part = pl.program_id(0)
    gate = gate_ref[seq]

    @pl.when(part == 0)
    def _():
        db_sc[...] = dbi_ref[0]
        dc_sc[...] = dci_ref[0]

    def add(ends_ref):
        enter = state_of(ends_ref, 0).astype(BF16)
        leave = state_of(ends_ref, 1).astype(BF16)
        db_sc[...] += dot(xv_ref[0], leave, NT)
        dc_sc[...] += dot(gg_ref[0], enter, NT)
        u = dot(scal_ref[0], spread_ref[0], NN) * dot(b_ref[0], leave, NN)
        dx_ref[0] = (gate * (dxi_ref[0] + u)).astype(BF16)

    if seq:
        pl.when(part == 0)(lambda: add(ends[0]))
        pl.when(part == 1)(lambda: add(ends[1]))
    else:
        add(ends[0])

    @pl.when(part == pl.num_programs(0) - 1)
    def _():
        db_ref[0] = (gate * db_sc[...]).astype(BF16)
        dc_ref[0] = (gate * dc_sc[...]).astype(BF16)


def sum_tensor(value):
    count = lax.axis_size("tensor")
    if count == 1:
        return value
    value = value + lax.ppermute(value, "tensor", [(i, i ^ 1) for i in range(count)])
    parts = [
        lax.ppermute(value, "tensor", [(i, (i + 2 * turn) % count) for i in range(count)])
        for turn in range(1, count // 2)
    ]
    return sum(parts, value)


def on_device(
    seq_inputs, b_proj, c_proj, dt_raw, dt_bias, a_log, d_skip, out_grad, log_ratio, lengths
):
    seqs, toks, width = seq_inputs.shape
    heads = dt_bias.shape[0]
    count = lax.axis_size("context")
    parts = width // LANES
    units = seqs * parts
    head_units = units - 1
    chunk = 2 * (LANES // PAIR) * (NS // count)
    spread_ones = jnp.asarray(spreads(heads), BF16)
    gather_ones = jnp.asarray(gathers(heads), BF16)
    bias_row, alog_row, gain_row = dt_bias[None], a_log[None], d_skip[None]
    smem = pl.BlockSpec(memory_space=pltpu.SMEM)
    anywhere = pl.BlockSpec(memory_space=pl.ANY)
    params = pltpu.CompilerParams(vmem_limit_bytes=VMEM)
    whole = lambda *shape: pl.BlockSpec(shape, lambda *at: (0,) * len(shape))
    small = [whole(1, heads), whole(1, heads)]

    of_either = lambda *shape: pl.BlockSpec(
        (1,) + shape, lambda i: (jnp.minimum(i, seqs - 1),) + (0,) * len(shape)
    )
    local = pl.pallas_call(
        states_kernel,
        grid=(seqs + 1,),
        in_specs=[
            smem, of_either(toks, width), of_either(toks, width), of_either(toks, NS),
            of_either(toks, NS), whole(*dt_raw.shape), *small, whole(*log_ratio.shape),
            whole(2, 128, width),
        ],
        out_specs=pl.BlockSpec((count, parts * chunk, PAIR), lambda i: (0, i, 0)),
        out_shape=jax.ShapeDtypeStruct((count, units * chunk + TILE, PAIR), F32),
        scratch_shapes=[pltpu.VMEM((seqs, toks, 128), BF16), pltpu.VMEM((TILE, 128), F32)],
        compiler_params=params,
        name="states",
    )(lengths, seq_inputs, out_grad, b_proj, c_proj, dt_raw, bias_row, alog_row, log_ratio,
      spread_ones)

    owned = lax.all_to_all(local, "context", 0, 0)

    tok_spec = lambda w: pl.BlockSpec((1, QB, w), lambda s, b: (s, b, 0))
    head_spec = pl.BlockSpec((1, heads, QB), lambda s, b: (s, 0, b))
    blocks = toks // QB
    dxi, dbi, dci, diff, col, skips, xv, gg, scal, near, aux = pl.pallas_call(
        intra_kernel,
        grid=(seqs, blocks),
        in_specs=[smem, tok_spec(width), tok_spec(width), tok_spec(NS), tok_spec(NS),
                  pl.BlockSpec((1, heads, toks), lambda s, b: (s, 0, 0)), *small, whole(1, heads),
                  whole(2, width, 128)],
        out_specs=[tok_spec(width), tok_spec(NS), tok_spec(NS), head_spec, head_spec,
                   pl.BlockSpec((1, 1, TILE, 128), lambda s, b: (s, b, 0, 0)),
                   tok_spec(width), tok_spec(width), tok_spec(128), tok_spec(128),
                   pl.BlockSpec((1, 3, heads, QB), lambda s, b: (s, 0, 0, b))],
        out_shape=[
            jax.ShapeDtypeStruct((seqs, toks, width), F32),
            jax.ShapeDtypeStruct((seqs, toks, NS), F32),
            jax.ShapeDtypeStruct((seqs, toks, NS), F32),
            jax.ShapeDtypeStruct((seqs, heads, toks), F32),
            jax.ShapeDtypeStruct((seqs, heads, toks), F32),
            jax.ShapeDtypeStruct((seqs, blocks, TILE, 128), F32),
            jax.ShapeDtypeStruct((seqs, toks, width), BF16),
            jax.ShapeDtypeStruct((seqs, toks, width), BF16),
            jax.ShapeDtypeStruct((seqs, toks, 128), BF16),
            jax.ShapeDtypeStruct((seqs, toks, 128), BF16),
            jax.ShapeDtypeStruct((seqs, 3, heads, toks), F32),
        ],
        scratch_shapes=[
            pltpu.VMEM((QB, width), F32), pltpu.VMEM((QB, width), F32),
            pltpu.VMEM((QB, width), BF16),
        ],
        compiler_params=params,
        name="intra",
    )(lengths, seq_inputs, out_grad, b_proj, c_proj, dt_raw, bias_row, alog_row, gain_row,
      gather_ones)

    of_seq = lambda *shape: pl.BlockSpec((1,) + shape, lambda i: (i,) + (0,) * len(shape))
    early = lambda w: pl.BlockSpec((1, QB, w), lambda i: (i, 0, 0))
    late = lambda w: pl.BlockSpec((1, QB, w), lambda i: (i, 1, 0))
    dlog, cols, dxi, dbi, dci = pl.pallas_call(
        cross_kernel,
        grid=(seqs,),
        in_specs=[smem, early(width), late(width), early(NS), late(NS), of_seq(toks, 128),
                  whole(2, 128, width), whole(2, width, 128), of_seq(heads, toks),
                  of_seq(heads, toks), early(width), early(NS), late(NS)],
        out_specs=[of_seq(heads, toks), of_seq(heads, toks), early(width), early(NS), late(NS)],
        out_shape=[
            jax.ShapeDtypeStruct((seqs, heads, toks), F32),
            jax.ShapeDtypeStruct((seqs, heads, toks), F32),
            jax.ShapeDtypeStruct((seqs, toks, width), F32),
            jax.ShapeDtypeStruct((seqs, toks, NS), F32),
            jax.ShapeDtypeStruct((seqs, toks, NS), F32),
        ],
        input_output_aliases={10: 2, 11: 3, 12: 4},
        compiler_params=params,
        name="cross",
    )(lengths, seq_inputs, out_grad, b_proj, c_proj, near, spread_ones, gather_ones, diff, col,
      dxi, dbi, dci)

    def chained(unit, number):
        return pl.pallas_call(
            lambda *refs: chain_kernel(unit, heads, *refs),
            grid=(number,),
            in_specs=[
                pl.BlockSpec((count, TILE, PAIR), lambda i: (0, units * chunk // TILE, 0)),
                pl.BlockSpec((count, chunk, PAIR), lambda i: (0, i + unit, 0)),
                whole(2, 128, width),
            ],
            out_specs=[pl.BlockSpec((count, chunk, PAIR), lambda i: (0, i, 0)), whole(TILE, 128)],
            out_shape=[
                jax.ShapeDtypeStruct((count, number * chunk, PAIR), F32),
                jax.ShapeDtypeStruct((TILE, 128), F32),
            ],
            scratch_shapes=[pltpu.VMEM((seqs * heads // 2, count, PAIR), F32)],
            compiler_params=params,
            name="chain",
        )(owned, owned, spread_ones)

    owned, dxi = lax.optimization_barrier((owned, dxi))
    most, sums = chained(0, head_units)
    most = lax.all_to_all(most, "context", 0, 0)
    least, _ = chained(head_units, units - head_units)
    least = lax.all_to_all(least, "context", 0, 0)
    totals = sum_tensor(sums[2:4])[:, 0]
    signs = jnp.where(jnp.arange(2, dtype=jnp.int32) == 0, -1.0, 1.0).astype(F32)
    margin = -jnp.sum(signs * totals)
    gate = signs * BETA * jax.nn.sigmoid(-BETA * margin)

    def final(unit, number, back, *before):
        at_seq = lambda *shape: pl.BlockSpec(
            (1,) + shape, lambda i: ((i + unit) // parts,) + (0,) * len(shape)
        )
        laned = pl.BlockSpec(
            (1, toks, LANES), lambda i: ((i + unit) // parts, 0, (i + unit) % parts)
        )
        return pl.pallas_call(
            lambda *refs: final_kernel(unit, heads, *refs),
            grid=(number,),
            in_specs=[
                smem, smem, laned, laned, at_seq(toks, NS), at_seq(toks, NS),
                pl.BlockSpec((count, chunk, PAIR), lambda i: (0, i, 0)),
                at_seq(toks, 128), at_seq(3, heads, toks), at_seq(heads, toks),
                at_seq(heads, toks), at_seq(blocks, TILE, 128),
                pl.BlockSpec((2, 128, LANES), lambda i: (0, 0, (i + unit) % parts)),
                pl.BlockSpec((2, LANES, 128), lambda i: (0, (i + unit) % parts, 0)),
            ] + ([whole(1, TILE, 128), whole(toks, 128), whole(TILE, 128), anywhere] if before else []),
            out_specs=[at_seq(heads, toks), whole(count, TILE, 128), whole(toks, 128),
                       whole(TILE, 128)],
            out_shape=[
                jax.ShapeDtypeStruct((seqs, heads, toks), F32),
                jax.ShapeDtypeStruct((count, TILE, 128), F32),
                jax.ShapeDtypeStruct((toks, 128), F32),
                jax.ShapeDtypeStruct((TILE, 128), F32),
            ],
            scratch_shapes=[pltpu.VMEM((toks, 128), F32), pltpu.VMEM((TILE, 128), F32),
                            pltpu.VMEM((TILE, 128), F32)],
            input_output_aliases={17: 0} if before else {},
            compiler_params=params,
            name="final",
        )(lengths, gate, seq_inputs, out_grad, b_proj, c_proj, back, scal, aux, dlog, cols, skips,
          spread_ones, gather_ones, *before)

    def groups(seq, states, *before):
        of_seq = lambda *shape: pl.BlockSpec((1,) + shape, lambda p: (seq,) + (0,) * len(shape))
        laned = pl.BlockSpec((1, toks, LANES), lambda p: (seq, 0, p))
        if seq:
            last = pl.BlockSpec((count, chunk, PAIR), lambda p: (0, 0, 0))
            ends = [pl.BlockSpec((count, chunk, PAIR), lambda p: (0, head_units - 1, 0)), last]
        else:
            ends = [pl.BlockSpec((count, chunk, PAIR), lambda p: (0, p, 0))]
        return pl.pallas_call(
            lambda *refs: groups_kernel(seq, *refs),
            grid=(parts,),
            in_specs=[smem, of_seq(toks, NS), of_seq(toks, 128), laned, laned, laned,
                      of_seq(toks, NS), of_seq(toks, NS),
                      pl.BlockSpec((2, 128, LANES), lambda p: (0, 0, p))]
            + ends + [anywhere] * len(before),
            out_specs=[laned, of_seq(toks, NS), of_seq(toks, NS)],
            out_shape=[jax.ShapeDtypeStruct((seqs, toks, w), BF16) for w in (width, NS, NS)],
            scratch_shapes=[pltpu.VMEM((toks, NS), F32), pltpu.VMEM((toks, NS), F32)],
            input_output_aliases={9 + len(ends) + k: k for k in range(len(before))},
            compiler_params=params,
            name="groups",
        )(gate, b_proj, scal, xv, gg, dxi, dbi, dci, spread_ones, *states, *before)

    ddt, pars, some, thru = final(0, head_units, most)
    dx, db, dc = groups(0, (most,))
    least, dx, some = lax.optimization_barrier((least, dx, some))
    ddt, pars, _, _ = final(head_units, units - head_units, least, pars, some, thru, ddt)
    closing = lax.all_to_all(pars, "context", 0, 0)
    dx, db, dc = groups(1, (most, least), dx, db, dc)
    sums = jnp.sum(closing, axis=0)[:3, :heads]
    return dx, db, dc, ddt, sums[0], sums[1], sums[2]


def solution(mesh):
    return jax.shard_map(
        on_device,
        mesh=mesh,
        in_specs=(
            P(None, "context", "tensor"),
            P(None, "context", "tensor"),
            P(None, "context", "tensor"),
            P(None, "tensor", "context"),
            P("tensor"),
            P("tensor"),
            P("tensor"),
            P(None, "context", "tensor"),
            P(None, ("context", "tensor")),
            P(),
        ),
        out_specs=(
            P(None, "context", "tensor"),
            P(None, "context", "tensor"),
            P(None, "context", "tensor"),
            P(None, "tensor", "context"),
            P("tensor"),
            P("tensor"),
            P("tensor"),
        ),
        check_vma=False,
    )
```

time: 177 us -> 185 us (1.045)
  Pallas kernels: 63.4 us -> 67.1 us
  starting transfers between devices: 25.2 us -> 28.6 us
  local copies, waits for them, and re-layouts: 3.3 us -> 0.65 us
  waiting for transfers between devices: 82.4 us -> 85 us
    all_to_all x2, waiting for transfers between devices: 29.4 us -> 41.2 us  [the longest x1 41.2 us: on_device(): most = lax.all_to_all(most, 'context', 0, 0)]
    all_to_all x1, waiting for transfers between devices: 46 us -> 36.5 us  [on_device(): owned = lax.all_to_all(local, 'context', 0, 0)]
    pallas_call x5 -> x6, Pallas kernels: 34 us -> 39.2 us  [the longest x2 13.2 us: final(): pl.pallas_call(lambda *refs: final_kernel(unit, heads, *refs), grid=(numb...]
    all_to_all x1, starting transfers between devices: 4.24 us -> 7.08 us  [on_device(): closing = lax.all_to_all(pars, 'context', 0, 0)]
    unnamed x6 -> x4, local copies, waits for them, and re-layouts: 2.65 us -> 0.01 us
  transfers between devices with their start and end apart: 8 -> 8, of which waited for: 6 -> 5; matrix products, arithmetic and copies ran while one was open for 1% -> 1% of each run, Pallas kernels for 23% -> 27%
where the time goes in v3:
time: 185 us; the launch traced here: 184 us
  waiting for transfers between devices  85 us (46%)
  Pallas kernels  67.1 us (36%)
  starting transfers between devices  28.6 us (15%)
    all_to_all x1, waiting for transfers between devices, on_device(): most = lax.all_to_all(most, 'context', 0, 0)  41.2 us
    all_to_all x1, waiting for transfers between devices, on_device(): owned = lax.all_to_all(local, 'context', 0, 0)  36.5 us
    pallas_call x1, Pallas kernels, on_device(): pl.pallas_call(intra_kernel, grid=(seqs, blocks), in_specs=[smem, tok_spe...  17.4 us
    pallas_call x2, Pallas kernels, final(): pl.pallas_call(lambda *refs: final_kernel(unit, heads, *refs), grid=(numb...  13.2 us
    pallas_call x2, Pallas kernels, groups(): pl.pallas_call(lambda *refs: groups_kernel(seq, *refs), grid=(parts,), in...  10.5 us
    pallas_call x1, Pallas kernels, on_device(): pl.pallas_call(cross_kernel, grid=(seqs,), in_specs=[smem, early(width),...  10.3 us
    pallas_call x1, Pallas kernels, on_device(): pl.pallas_call(states_kernel, grid=(seqs + 1,), in_specs=[smem, of_either...  8.2 us
    pallas_call x2, Pallas kernels, chained(): pl.pallas_call(lambda *refs: chain_kernel(unit, heads, *refs), grid=(numb...  7.59 us
  transfers between devices with their start and end apart: 8, of which 5 were waited for; matrix products, arithmetic and copies ran while one was open for 1% of the time, Pallas kernels for 27%

profile of v3, /device:TPU:0, one launch (start us, length us, event | category | flops | bytes accessed | tf_op | source)
XLA Modules:
  0.0 184.1 jit_solution(17456093494212699664)
XLA Ops:
  0.6 8.2 %states.1 = f32[16,520,128]{2,1,0:T(8,128)} custom-call(s32[2]{0:T(128)} %refs_0_.3, bf16[2,512,1024]{2,1,0:T(8,128)(2,1)} %refs_2_.5, bf16[2,512,1024]{2,1,0:T(8,128)(2,1)} %refs_3_.3, bf16[2,512,256]{2,1,0:T(8,128)(2,1)} %refs_4_.3, bf16[2,512,256]{2,1,0:T(8,128)(2,1)} %refs_5_.3, f32[2,16,512]{2,1,0:T(8,128)} %dt_ref.3, f32[1,16]{1,0:T(1,128)} %bitcast.9, ...), custom_call_target="tpu_custom_call" | custom-call | tf_op jit(solution)/shard_map/states/pallas_call | solution.py:508
  8.8 7.2 %all-to-all-start = ((f32[16,520,128]{2,1,0:T(8,128)}), f32[16,520,128]{2,1,0:T(8,128)}, u32[]{:S(2)}, u32[]{:S(2)}) async-start(f32[16,520,128]{2,1,0:T(8,128)} %states.1), calls=%async_computation | async-start | bytes 8519680 | tf_op jit(solution)/shard_map/all_to_all | solution.py:524
  16.0 17.4 %intra.1 = (f32[2,512,1024]{2,1,0:T(8,128)}, f32[2,512,256]{2,1,0:T(8,128)}, f32[2,512,256]{2,1,0:T(8,128)}, f32[2,16,512]{2,1,0:T(8,128)}, f32[2,16,512]{2,1,0:...) custom-call(s32[2]{0:T(128)} %refs_0_.3, ...), custom_call_target="tpu_custom_call" | custom-call | tf_op jit(solution)/shard_map/intra/pallas_call | solution.py:529
  33.4 10.3 %cross.1 = (f32[2,16,512]{2,1,0:T(8,128)}, f32[2,16,512]{2,1,0:T(8,128)}, f32[2,512,1024]{2,1,0:T(8,128)}, f32[2,512,256]{2,1,0:T(8,128)}, f32[2,512,256]{2,1,0:T(8,128)}) custom-call(s32[2]{0:T(128)} %refs_0_.3, bf16[2,512,1024]{2,1,0:T(8,128)(2,1)} %refs_2_.5, ...), custom_call_target="tpu_custom_call", output_to_operand_aliasing={{2}: (10, {}), {3}: (11, {}), {4}: (12, {})} | custom-call | tf_op jit(solution)/shard_map/cross/pallas_call | solution.py:564
  43.7 36.5 %all-to-all-done.refs_0_.refs_1_ = f32[16,520,128]{2,1,0:T(8,128)} async-done(((f32[16,520,128]{2,1,0:T(8,128)}), f32[16,520,128]{2,1,0:T(8,128)}, u32[]{:S(2)}, u32[]{:S(2)}) %all-to-all-start) | async-done | bytes 4259872 | tf_op jit(solution)/shard_map/all_to_all | solution.py:524
  80.2 4.8 %chain.2 = (f32[16,384,128]{2,1,0:T(8,128)}, f32[8,128]{1,0:T(8,128)}) custom-call(f32[16,520,128]{2,1,0:T(8,128)} %all-to-all-done.refs_0_.refs_1_, f32[16,520,128]{2,1,0:T(8,128)} %all-to-all-done.refs_0_.refs_1_, bf16[2,128,1024]{2,1,0:T(8,128)(2,1)} %constant.16.clone.spread_ref.refs_2_.refs_8_.refs_12_), custom_call_target="tpu_custom_call" | custom-call | tf_op jit(solution)/shard_map/chain/pallas_call | solution.py:585
  85.0 4.7 %all-to-all-start.1 = ((f32[16,384,128]{2,1,0:T(8,128)}), f32[16,384,128]{2,1,0:T(8,128)S(1)}, u32[]{:S(2)}, u32[]{:S(2)}) async-start(f32[16,384,128]{2,1,0:T(8,128)} %get-tuple-element.58), calls=%async_computation.1 | async-start | bytes 6291456 | tf_op jit(solution)/shard_map/all_to_all | solution.py:605
  89.7 2.8 %chain.3 = (f32[16,128,128]{2,1,0:T(8,128)}, f32[8,128]{1,0:T(8,128)}) custom-call(f32[16,520,128]{2,1,0:T(8,128)} %all-to-all-done.refs_0_.refs_1_, f32[16,520,128]{2,1,0:T(8,128)} %all-to-all-done.refs_0_.refs_1_, bf16[2,128,1024]{2,1,0:T(8,128)(2,1)} %constant.16.clone.spread_ref.refs_2_.refs_8_.refs_12_), custom_call_target="tpu_custom_call" | custom-call | tf_op jit(solution)/shard_map/chain/pallas_call | solution.py:585
  92.4 41.2 %all-to-all-done.1.refs_9_.refs_6_ = f32[16,384,128]{2,1,0:T(8,128)S(1)} async-done(((f32[16,384,128]{2,1,0:T(8,128)}), f32[16,384,128]{2,1,0:T(8,128)S(1)}, u32[]{:S(2)}, u32[]{:S(2)}) %all-to-all-start.1) | async-done | bytes 3145760 | tf_op jit(solution)/shard_map/all_to_all | solution.py:605
  133.7 4.3 %all-to-all-start.2 = ((f32[16,128,128]{2,1,0:T(8,128)}), f32[16,128,128]{2,1,0:T(8,128)}, u32[]{:S(2)}, u32[]{:S(2)}) async-start(f32[16,128,128]{2,1,0:T(8,128)} %get-tuple-element.59), calls=%async_computation.2 | async-start | bytes 2097152 | tf_op jit(solution)/shard_map/all_to_all | solution.py:607
  138.1 1.1 collective-permute-done
  139.3 4.0 %collective-permute-start.3 = (f32[2,128]{1,0:T(2,128)S(1)}, f32[2,128]{1,0:T(2,128)S(1)}, u32[]{:S(2)}, u32[]{:S(2)}) collective-permute-start(f32[2,128]{1,0:T(2,128)S(1)} %slice_add_fusion), channel_id=1, source_target_pairs={{0,6},{1,7},{2,0},{3,1},{4,2},{5,3},{6,4},{7,5},{8,14},{9,15},{10,... | collective-permute-start | bytes 3080 | tf_op jit(solution)/shard_map/ppermute | solution.py:480
  143.3 1.3 collective-permute-start.1
  144.6 3.8 %collective-permute-done.2 = f32[2,128]{1,0:T(2,128)S(1)} collective-permute-done((f32[2,128]{1,0:T(2,128)S(1)}, f32[2,128]{1,0:T(2,128)S(1)}, u32[]{:S(2)}, u32[]{:S(2)}) %collective-permute-start.2) | collective-permute-done | bytes 1056 | tf_op jit(solution)/shard_map/ppermute | solution.py:480
  148.4 0.1 slice_reduce_fusion
  148.5 0.6 multiply_reduce_fusion
  149.9 0.5 fusion.refs_0_.refs_1_
  150.4 8.4 %final.2 = (f32[2,16,512]{2,1,0:T(8,128)}, f32[16,8,128]{2,1,0:T(8,128)}, f32[512,128]{1,0:T(8,128)}, f32[8,128]{1,0:T(8,128)}) custom-call(s32[2]{0:T(128)} %refs_0_.3, f32[2]{0:T(128)} %fusion.refs_0_.refs_1_, bf16[2,512,1024]{2,1,0:T(8,128)(2,1)} %refs_2_.5, bf16[2,512,1024]{2,1,0:T(8,128)(2,1)} %refs_3_.3, bf16[2,512,256]{2,1,0:T(8,128)(2,1)} %refs_4_.3, ...), custom_call_target="tpu_custom_call" | custom-call | tf_op jit(solution)/shard_map/final/pallas_call | solution.py:620
  158.8 5.2 %groups.2 = (bf16[2,512,1024]{2,1,0:T(8,128)(2,1)}, bf16[2,512,256]{2,1,0:T(8,128)(2,1)}, bf16[2,512,256]{2,1,0:T(8,128)(2,1)}) custom-call(f32[2]{0:T(128)} %fusion.refs_0_.refs_1_, bf16[2,512,256]{2,1,0:T(8,128)(2,1)} %refs_4_.3, bf16[2,512,128]{2,1,0:T(8,128)(2,1)} %get-tuple-element.52.refs_2_.refs_7_, bf16[2,512,1024]{2,1,0:T(8,128)(2,1)} %get-tuple-element.53.refs_3_, ...), custom_call_target="tpu_custom_call" | custom-call | tf_op jit(solution)/shard_map/groups/pallas_call | solution.py:655
  164.0 4.8 %final.3 = (f32[2,16,512]{2,1,0:T(8,128)}, f32[16,8,128]{2,1,0:T(8,128)}, f32[512,128]{1,0:T(8,128)}, f32[8,128]{1,0:T(8,128)}) custom-call(s32[2]{0:T(128)} %refs_0_.3, f32[2]{0:T(128)} %fusion.refs_0_.refs_1_, bf16[2,512,1024]{2,1,0:T(8,128)(2,1)} %refs_2_.5, bf16[2,512,1024]{2,1,0:T(8,128)(2,1)} %refs_3_.3, ...), custom_call_target="tpu_custom_call", output_to_operand_aliasing={{0}: (17, {})} | custom-call | tf_op jit(solution)/shard_map/final/pallas_call | solution.py:620
  168.8 7.1 %all-to-all-start.3 = ((f32[16,8,128]{2,1,0:T(8,128)}), f32[16,8,128]{2,1,0:T(8,128)S(1)}, u32[]{:S(2)}, u32[]{:S(2)}) async-start(f32[16,8,128]{2,1,0:T(8,128)} %get-tuple-element.78), calls=%async_computation.3 | async-start | bytes 131072 | tf_op jit(solution)/shard_map/all_to_all | solution.py:674
  175.9 5.3 %groups.3 = (bf16[2,512,1024]{2,1,0:T(8,128)(2,1)}, bf16[2,512,256]{2,1,0:T(8,128)(2,1)}, bf16[2,512,256]{2,1,0:T(8,128)(2,1)}) custom-call(f32[2]{0:T(128)} %fusion.refs_0_.refs_1_, bf16[2,512,256]{2,1,0:T(8,128)(2,1)} %refs_4_.3, ...), custom_call_target="tpu_custom_call", output_to_operand_aliasing={{0}: (11, {}), {1}: (12, {}), {2}: (13, {})} | custom-call | tf_op jit(solution)/shard_map/groups/pallas_call | solution.py:655
  181.2 2.4 %all-to-all-done.3 = f32[16,8,128]{2,1,0:T(8,128)S(1)} async-done(((f32[16,8,128]{2,1,0:T(8,128)}), f32[16,8,128]{2,1,0:T(8,128)S(1)}, u32[]{:S(2)}, u32[]{:S(2)}) %all-to-all-start.3) | async-done | bytes 65568 | tf_op jit(solution)/shard_map/all_to_all | solution.py:674
  183.6 0.5 slice_bitcast_fusion
  (13 shorter events, 0.2 us)
Async XLA Ops:
  8.8 71.3 %all-to-all-start = ((f32[16,520,128]{2,1,0:T(8,128)}), f32[16,520,128]{2,1,0:T(8,128)}, u32[]{:S(2)}, u32[]{:S(2)}) async-start(f32[16,520,128]{2,1,0:T(8,128)} %states.1), calls=%async_computation | async-start | bytes 8519680 | tf_op jit(solution)/shard_map/all_to_all | solution.py:524
  85.0 48.7 %all-to-all-start.1 = ((f32[16,384,128]{2,1,0:T(8,128)}), f32[16,384,128]{2,1,0:T(8,128)S(1)}, u32[]{:S(2)}, u32[]{:S(2)}) async-start(f32[16,384,128]{2,1,0:T(8,128)} %get-tuple-element.58), calls=%async_computation.1 | async-start | bytes 6291456 | tf_op jit(solution)/shard_map/all_to_all | solution.py:605
  89.7 48.4 %copy-start.1 = (f32[8,128]{1,0:T(8,128)S(1)}, f32[8,128]{1,0:T(8,128)}, u32[]{:S(2)}) copy-start(f32[8,128]{1,0:T(8,128)} %get-tuple-element.51) | copy-start | bytes 12292
  133.7 16.7 %copy-start = (f32[16,384,128]{2,1,0:T(8,128)}, f32[16,384,128]{2,1,0:T(8,128)S(1)}, u32[]{:S(2)}) copy-start(f32[16,384,128]{2,1,0:T(8,128)S(1)} %all-to-all-done.1.refs_9_.refs_6_) | copy-start | bytes 9437188
  133.7 30.3 %all-to-all-start.2 = ((f32[16,128,128]{2,1,0:T(8,128)}), f32[16,128,128]{2,1,0:T(8,128)}, u32[]{:S(2)}, u32[]{:S(2)}) async-start(f32[16,128,128]{2,1,0:T(8,128)} %get-tuple-element.59), calls=%async_computation.2 | async-start | bytes 2097152 | tf_op jit(solution)/shard_map/all_to_all | solution.py:607
  138.1 1.2 collective-permute-start
  139.3 5.3 %collective-permute-start.3 = (f32[2,128]{1,0:T(2,128)S(1)}, f32[2,128]{1,0:T(2,128)S(1)}, u32[]{:S(2)}, u32[]{:S(2)}) collective-permute-start(f32[2,128]{1,0:T(2,128)S(1)} %slice_add_fusion), channel_id=1, source_target_pairs={{0,6},{1,7},{2,0},{3,1},{4,2},{5,3},{6,4},{7,5},{8,14},{9,15},{10,... | collective-permute-start | bytes 3080 | tf_op jit(solution)/shard_map/ppermute | solution.py:480
  143.3 5.1 %collective-permute-start.2 = (f32[2,128]{1,0:T(2,128)S(1)}, f32[2,128]{1,0:T(2,128)S(1)}, u32[]{:S(2)}, u32[]{:S(2)}) collective-permute-start(f32[2,128]{1,0:T(2,128)S(1)} %slice_add_fusion), channel_id=1, source_target_pairs={{0,4},{1,5},{2,6},{3,7},{4,0},{5,1},{6,2},{7,3},{8,12},{9,13},{10,... | collective-permute-start | bytes 3080 | tf_op jit(solution)/shard_map/ppermute | solution.py:480
  143.3 5.1 %collective-permute-start.1 = (f32[2,128]{1,0:T(2,128)S(1)}, f32[2,128]{1,0:T(2,128)S(1)}, u32[]{:S(2)}, u32[]{:S(2)}) collective-permute-start(f32[2,128]{1,0:T(2,128)S(1)} %slice_add_fusion), channel_id=1, source_target_pairs={{0,2},{1,3},{2,4},{3,5},{4,6},{5,7},{6,0},{7,1},{8,10},{9,11},{10,... | collective-permute-start | bytes 3080 | tf_op jit(solution)/shard_map/ppermute | solution.py:480
  168.8 14.8 %all-to-all-start.3 = ((f32[16,8,128]{2,1,0:T(8,128)}), f32[16,8,128]{2,1,0:T(8,128)S(1)}, u32[]{:S(2)}, u32[]{:S(2)}) async-start(f32[16,8,128]{2,1,0:T(8,128)} %get-tuple-element.78), calls=%async_computation.3 | async-start | bytes 131072 | tf_op jit(solution)/shard_map/all_to_all | solution.py:674

commit v4 on v3

--- a/solution.py
+++ b/solution.py
@@ -523,6 +523,29 @@
 
     owned = lax.all_to_all(local, "context", 0, 0)
 
+    def chained(unit, number):
+        return pl.pallas_call(
+            lambda *refs: chain_kernel(unit, heads, *refs),
+            grid=(number,),
+            in_specs=[
+                pl.BlockSpec((count, TILE, PAIR), lambda i: (0, units * chunk // TILE, 0)),
+                pl.BlockSpec((count, chunk, PAIR), lambda i: (0, i + unit, 0)),
+                whole(2, 128, width),
+            ],
+            out_specs=[pl.BlockSpec((count, chunk, PAIR), lambda i: (0, i, 0)), whole(TILE, 128)],
+            out_shape=[
+                jax.ShapeDtypeStruct((count, number * chunk, PAIR), F32),
+                jax.ShapeDtypeStruct((TILE, 128), F32),
+            ],
+            scratch_shapes=[pltpu.VMEM((seqs * heads // 2, count, PAIR), F32)],
+            compiler_params=params,
+            name="chain",
+        )(owned, owned, spread_ones)
+
+    most, sums = chained(0, head_units)
+    most, dt_raw = lax.optimization_barrier((most, dt_raw))
+    most = lax.all_to_all(most, "context", 0, 0)
+
     tok_spec = lambda w: pl.BlockSpec((1, QB, w), lambda s, b: (s, b, 0))
     head_spec = pl.BlockSpec((1, heads, QB), lambda s, b: (s, 0, b))
     blocks = toks // QB
@@ -581,34 +604,13 @@
     )(lengths, seq_inputs, out_grad, b_proj, c_proj, near, spread_ones, gather_ones, diff, col,
       dxi, dbi, dci)
 
-    def chained(unit, number):
-        return pl.pallas_call(
-            lambda *refs: chain_kernel(unit, heads, *refs),
-            grid=(number,),
-            in_specs=[
-                pl.BlockSpec((count, TILE, PAIR), lambda i: (0, units * chunk // TILE, 0)),
-                pl.BlockSpec((count, chunk, PAIR), lambda i: (0, i + unit, 0)),
-                whole(2, 128, width),
-            ],
-            out_specs=[pl.BlockSpec((count, chunk, PAIR), lambda i: (0, i, 0)), whole(TILE, 128)],
-            out_shape=[
-                jax.ShapeDtypeStruct((count, number * chunk, PAIR), F32),
-                jax.ShapeDtypeStruct((TILE, 128), F32),
-            ],
-            scratch_shapes=[pltpu.VMEM((seqs * heads // 2, count, PAIR), F32)],
-            compiler_params=params,
-            name="chain",
-        )(owned, owned, spread_ones)
-
-    owned, dxi = lax.optimization_barrier((owned, dxi))
-    most, sums = chained(0, head_units)
-    most = lax.all_to_all(most, "context", 0, 0)
     least, _ = chained(head_units, units - head_units)
-    least = lax.all_to_all(least, "context", 0, 0)
     totals = sum_tensor(sums[2:4])[:, 0]
     signs = jnp.where(jnp.arange(2, dtype=jnp.int32) == 0, -1.0, 1.0).astype(F32)
     margin = -jnp.sum(signs * totals)
     gate = signs * BETA * jax.nn.sigmoid(-BETA * margin)
+    least, gate, dxi = lax.optimization_barrier((least, gate, dxi))
+    least = lax.all_to_all(least, "context", 0, 0)
 
     def final(unit, number, back, *before):
         at_seq = lambda *shape: pl.BlockSpec(

time: 185 us -> 160 us (0.86)
  waiting for transfers between devices: 85 us -> 10.8 us
  blocking collectives: 0 us -> 58.8 us
  starting transfers between devices: 28.6 us -> 18.9 us
    all_to_all x0 -> x1, blocking collectives: none -> 58.8 us  [on_device(): owned = lax.all_to_all(local, 'context', 0, 0)]
    all_to_all x1 -> x0, waiting for transfers between devices: 36.5 us -> none  [on_device(): owned = lax.all_to_all(local, 'context', 0, 0)]
    all_to_all x1, waiting for transfers between devices: 41.2 us -> 5.54 us  [on_device(): most = lax.all_to_all(most, 'context', 0, 0)]
    all_to_all x1 -> x0, starting transfers between devices: 7.16 us -> none  [on_device(): owned = lax.all_to_all(local, 'context', 0, 0)]
    ppermute x3, waiting for transfers between devices: 3.81 us -> 0.01 us  [sum_tensor(): lax.ppermute(value, 'tensor', [(i, (i + 2 * turn) % count) for i in range...]
    all_to_all x1, starting transfers between devices: 7.08 us -> 5.16 us  [on_device(): closing = lax.all_to_all(pars, 'context', 0, 0)]
  transfers between devices with their start and end apart: 8 -> 7, of which waited for: 5 -> 4; matrix products, arithmetic and copies ran while one was open for 1% -> 1% of each run, Pallas kernels for 27% -> 31%
where the time goes in v4:
time: 160 us; the launch traced here: 159 us
  Pallas kernels  67.1 us (42%)
  blocking collectives  58.8 us (37%)
  starting transfers between devices  18.9 us (12%)
  waiting for transfers between devices  10.8 us (7%)
    all_to_all x1, blocking collectives, on_device(): owned = lax.all_to_all(local, 'context', 0, 0)  58.8 us
    pallas_call x1, Pallas kernels, on_device(): pl.pallas_call(intra_kernel, grid=(seqs, blocks), in_specs=[smem, tok_spe...  17.4 us
    pallas_call x2, Pallas kernels, final(): pl.pallas_call(lambda *refs: final_kernel(unit, heads, *refs), grid=(numb...  13.2 us
    pallas_call x2, Pallas kernels, groups(): pl.pallas_call(lambda *refs: groups_kernel(seq, *refs), grid=(parts,), in...  10.5 us
    pallas_call x1, Pallas kernels, on_device(): pl.pallas_call(cross_kernel, grid=(seqs,), in_specs=[smem, early(width),...  10.2 us
    pallas_call x1, Pallas kernels, on_device(): pl.pallas_call(states_kernel, grid=(seqs + 1,), in_specs=[smem, of_either...  8.21 us
    pallas_call x2, Pallas kernels, chained(): pl.pallas_call(lambda *refs: chain_kernel(unit, heads, *refs), grid=(numb...  7.57 us
    all_to_all x1, waiting for transfers between devices, on_device(): most = lax.all_to_all(most, 'context', 0, 0)  5.54 us
  transfers between devices with their start and end apart: 7, of which 4 were waited for; matrix products, arithmetic and copies ran while one was open for 1% of the time, Pallas kernels for 31%

profile of v4, /device:TPU:0, one launch (start us, length us, event | category | flops | bytes accessed | tf_op | source)
XLA Modules:
  0.0 159.0 jit_solution(18424014161483960518)
XLA Ops:
  0.6 8.2 %states.1 = f32[16,520,128]{2,1,0:T(8,128)} custom-call(s32[2]{0:T(128)} %refs_0_.3, bf16[2,512,1024]{2,1,0:T(8,128)(2,1)} %refs_2_.5, bf16[2,512,1024]{2,1,0:T(8,128)(2,1)} %refs_3_.3, bf16[2,512,256]{2,1,0:T(8,128)(2,1)} %refs_4_.3, bf16[2,512,256]{2,1,0:T(8,128)(2,1)} %refs_5_.3, f32[2,16,512]{2,1,0:T(8,128)} %dt_ref.2, f32[1,16]{1,0:T(1,128)} %bitcast.9, ...), custom_call_target="tpu_custom_call" | custom-call | tf_op jit(solution)/shard_map/states/pallas_call | solution.py:508
  8.8 58.8 %all_to_all.20.refs_0_.refs_1_ = f32[16,520,128]{2,1,0:T(8,128)} all-to-all(f32[16,520,128]{2,1,0:T(8,128)} %states.1), channel_id=1, replica_groups=mesh['context'=16,'tensor'=8] {'context'}, dimensions={0} | all-to-all | bytes 8519680 | tf_op jit(solution)/shard_map/all_to_all | solution.py:524
  67.6 4.8 %chain.3 = (f32[16,384,128]{2,1,0:T(8,128)}, f32[8,128]{1,0:T(8,128)}) custom-call(f32[16,520,128]{2,1,0:T(8,128)} %all_to_all.20.refs_0_.refs_1_, f32[16,520,128]{2,1,0:T(8,128)} %all_to_all.20.refs_0_.refs_1_, bf16[2,128,1024]{2,1,0:T(8,128)(2,1)} %constant.16.clone.spread_ref.refs_2_.refs_8_.refs_12_), custom_call_target="tpu_custom_call" | custom-call | tf_op jit(solution)/shard_map/chain/pallas_call | solution.py:527
  72.5 3.9 %all-to-all-start.1 = ((f32[16,384,128]{2,1,0:T(8,128)}), f32[16,384,128]{2,1,0:T(8,128)S(1)}, u32[]{:S(2)}, u32[]{:S(2)}) async-start(f32[16,384,128]{2,1,0:T(8,128)} %get-tuple-element.64), calls=%async_computation.1 | async-start | bytes 6291456 | tf_op jit(solution)/shard_map/all_to_all | solution.py:547
  76.4 0.1 collective-permute-start
  76.5 1.1 collective-permute-done
  77.6 4.0 %collective-permute-start.3 = (f32[2,128]{1,0:T(2,128)S(1)}, f32[2,128]{1,0:T(2,128)S(1)}, u32[]{:S(2)}, u32[]{:S(2)}) collective-permute-start(f32[2,128]{1,0:T(2,128)S(1)} %slice_add_fusion), channel_id=1, source_target_pairs={{0,6},{1,7},{2,0},{3,1},{4,2},{5,3},{6,4},{7,5},{8,14},{9,15},{10,... | collective-permute-start | bytes 3080 | tf_op jit(solution)/shard_map/ppermute | solution.py:480
  81.7 1.3 collective-permute-start.1
  82.9 17.4 %intra.1 = (f32[2,512,1024]{2,1,0:T(8,128)}, f32[2,512,256]{2,1,0:T(8,128)}, f32[2,512,256]{2,1,0:T(8,128)}, f32[2,16,512]{2,1,0:T(8,128)}, f32[2,16,512]{2,1,0:...) custom-call(s32[2]{0:T(128)} %refs_0_.3, ...), custom_call_target="tpu_custom_call" | custom-call | tf_op jit(solution)/shard_map/intra/pallas_call | solution.py:552
  100.3 10.2 %cross.1 = (f32[2,16,512]{2,1,0:T(8,128)}, f32[2,16,512]{2,1,0:T(8,128)}, f32[2,512,1024]{2,1,0:T(8,128)}, f32[2,512,256]{2,1,0:T(8,128)}, f32[2,512,256]{2,1,0:T(8,128)}) custom-call(s32[2]{0:T(128)} %refs_0_.3, bf16[2,512,1024]{2,1,0:T(8,128)(2,1)} %refs_2_.5, ...), custom_call_target="tpu_custom_call", output_to_operand_aliasing={{2}: (10, {}), {3}: (11, {}), {4}: (12, {})} | custom-call | tf_op jit(solution)/shard_map/cross/pallas_call | solution.py:587
  110.5 2.7 %chain.2 = (f32[16,128,128]{2,1,0:T(8,128)}, f32[8,128]{1,0:T(8,128)}) custom-call(f32[16,520,128]{2,1,0:T(8,128)} %all_to_all.20.refs_0_.refs_1_, f32[16,520,128]{2,1,0:T(8,128)} %all_to_all.20.refs_0_.refs_1_, bf16[2,128,1024]{2,1,0:T(8,128)(2,1)} %constant.16.clone.spread_ref.refs_2_.refs_8_.refs_12_), custom_call_target="tpu_custom_call" | custom-call | tf_op jit(solution)/shard_map/chain/pallas_call | solution.py:527
  113.3 0.1 slice_reduce_fusion
  113.4 0.6 multiply_reduce_fusion
  114.8 0.5 fusion.refs_0_.refs_1_
  115.3 5.5 %all-to-all-done.1.refs_9_.refs_6_ = f32[16,384,128]{2,1,0:T(8,128)S(1)} async-done(((f32[16,384,128]{2,1,0:T(8,128)}), f32[16,384,128]{2,1,0:T(8,128)S(1)}, u32[]{:S(2)}, u32[]{:S(2)}) %all-to-all-start.1) | async-done | bytes 3145760 | tf_op jit(solution)/shard_map/all_to_all | solution.py:547
  120.8 4.5 %all-to-all-start.2 = ((f32[16,128,128]{2,1,0:T(8,128)}), f32[16,128,128]{2,1,0:T(8,128)}, u32[]{:S(2)}, u32[]{:S(2)}) async-start(f32[16,128,128]{2,1,0:T(8,128)} %get-tuple-element.65), calls=%async_computation.2 | async-start | bytes 2097152 | tf_op jit(solution)/shard_map/all_to_all | solution.py:613
  125.4 8.5 %final.2 = (f32[2,16,512]{2,1,0:T(8,128)}, f32[16,8,128]{2,1,0:T(8,128)}, f32[512,128]{1,0:T(8,128)}, f32[8,128]{1,0:T(8,128)}) custom-call(s32[2]{0:T(128)} %refs_0_.3, f32[2]{0:T(128)} %fusion.refs_0_.refs_1_, bf16[2,512,1024]{2,1,0:T(8,128)(2,1)} %refs_2_.5, bf16[2,512,1024]{2,1,0:T(8,128)(2,1)} %refs_3_.3, bf16[2,512,256]{2,1,0:T(8,128)(2,1)} %refs_4_.3, ...), custom_call_target="tpu_custom_call" | custom-call | tf_op jit(solution)/shard_map/final/pallas_call | solution.py:622
  133.8 5.2 %groups.2 = (bf16[2,512,1024]{2,1,0:T(8,128)(2,1)}, bf16[2,512,256]{2,1,0:T(8,128)(2,1)}, bf16[2,512,256]{2,1,0:T(8,128)(2,1)}) custom-call(f32[2]{0:T(128)} %fusion.refs_0_.refs_1_, bf16[2,512,256]{2,1,0:T(8,128)(2,1)} %refs_4_.3, bf16[2,512,128]{2,1,0:T(8,128)(2,1)} %get-tuple-element.58.refs_2_.refs_7_, bf16[2,512,1024]{2,1,0:T(8,128)(2,1)} %get-tuple-element.59.refs_3_, ...), custom_call_target="tpu_custom_call" | custom-call | tf_op jit(solution)/shard_map/groups/pallas_call | solution.py:657
  139.0 1.8 %all-to-all-done.2.refs_10_.refs_6_ = f32[16,128,128]{2,1,0:T(8,128)} async-done(((f32[16,128,128]{2,1,0:T(8,128)}), f32[16,128,128]{2,1,0:T(8,128)}, u32[]{:S(2)}, u32[]{:S(2)}) %all-to-all-start.2) | async-done | bytes 1048608 | tf_op jit(solution)/shard_map/all_to_all | solution.py:613
  140.8 4.7 %final.3 = (f32[2,16,512]{2,1,0:T(8,128)}, f32[16,8,128]{2,1,0:T(8,128)}, f32[512,128]{1,0:T(8,128)}, f32[8,128]{1,0:T(8,128)}) custom-call(s32[2]{0:T(128)} %refs_0_.3, f32[2]{0:T(128)} %fusion.refs_0_.refs_1_, bf16[2,512,1024]{2,1,0:T(8,128)(2,1)} %refs_2_.5, bf16[2,512,1024]{2,1,0:T(8,128)(2,1)} %refs_3_.3, ...), custom_call_target="tpu_custom_call", output_to_operand_aliasing={{0}: (17, {})} | custom-call | tf_op jit(solution)/shard_map/final/pallas_call | solution.py:622
  145.6 5.2 %all-to-all-start.3 = ((f32[16,8,128]{2,1,0:T(8,128)}), f32[16,8,128]{2,1,0:T(8,128)S(1)}, u32[]{:S(2)}, u32[]{:S(2)}) async-start(f32[16,8,128]{2,1,0:T(8,128)} %get-tuple-element.84), calls=%async_computation.3 | async-start | bytes 131072 | tf_op jit(solution)/shard_map/all_to_all | solution.py:676
  150.8 5.3 %groups.3 = (bf16[2,512,1024]{2,1,0:T(8,128)(2,1)}, bf16[2,512,256]{2,1,0:T(8,128)(2,1)}, bf16[2,512,256]{2,1,0:T(8,128)(2,1)}) custom-call(f32[2]{0:T(128)} %fusion.refs_0_.refs_1_, bf16[2,512,256]{2,1,0:T(8,128)(2,1)} %refs_4_.3, ...), custom_call_target="tpu_custom_call", output_to_operand_aliasing={{0}: (11, {}), {1}: (12, {}), {2}: (13, {})} | custom-call | tf_op jit(solution)/shard_map/groups/pallas_call | solution.py:657
  156.1 2.4 %all-to-all-done.3 = f32[16,8,128]{2,1,0:T(8,128)S(1)} async-done(((f32[16,8,128]{2,1,0:T(8,128)}), f32[16,8,128]{2,1,0:T(8,128)S(1)}, u32[]{:S(2)}, u32[]{:S(2)}) %all-to-all-start.3) | async-done | bytes 65568 | tf_op jit(solution)/shard_map/all_to_all | solution.py:676
  158.4 0.5 slice_bitcast_fusion
  (12 shorter events, 0.1 us)
Async XLA Ops:
  72.5 3.9 %copy-start.1 = (f32[8,128]{1,0:T(8,128)S(1)}, f32[8,128]{1,0:T(8,128)}, u32[]{:S(2)}) copy-start(f32[8,128]{1,0:T(8,128)} %get-tuple-element.47) | copy-start | bytes 12292
  72.5 48.3 %all-to-all-start.1 = ((f32[16,384,128]{2,1,0:T(8,128)}), f32[16,384,128]{2,1,0:T(8,128)S(1)}, u32[]{:S(2)}, u32[]{:S(2)}) async-start(f32[16,384,128]{2,1,0:T(8,128)} %get-tuple-element.64), calls=%async_computation.1 | async-start | bytes 6291456 | tf_op jit(solution)/shard_map/all_to_all | solution.py:547
  76.4 1.2 collective-permute-start
  77.6 35.7 %collective-permute-start.3 = (f32[2,128]{1,0:T(2,128)S(1)}, f32[2,128]{1,0:T(2,128)S(1)}, u32[]{:S(2)}, u32[]{:S(2)}) collective-permute-start(f32[2,128]{1,0:T(2,128)S(1)} %slice_add_fusion), channel_id=1, source_target_pairs={{0,6},{1,7},{2,0},{3,1},{4,2},{5,3},{6,4},{7,5},{8,14},{9,15},{10,... | collective-permute-start | bytes 3080 | tf_op jit(solution)/shard_map/ppermute | solution.py:480
  81.7 31.6 %collective-permute-start.2 = (f32[2,128]{1,0:T(2,128)S(1)}, f32[2,128]{1,0:T(2,128)S(1)}, u32[]{:S(2)}, u32[]{:S(2)}) collective-permute-start(f32[2,128]{1,0:T(2,128)S(1)} %slice_add_fusion), channel_id=1, source_target_pairs={{0,4},{1,5},{2,6},{3,7},{4,0},{5,1},{6,2},{7,3},{8,12},{9,13},{10,... | collective-permute-start | bytes 3080 | tf_op jit(solution)/shard_map/ppermute | solution.py:480
  81.7 31.6 %collective-permute-start.1 = (f32[2,128]{1,0:T(2,128)S(1)}, f32[2,128]{1,0:T(2,128)S(1)}, u32[]{:S(2)}, u32[]{:S(2)}) collective-permute-start(f32[2,128]{1,0:T(2,128)S(1)} %slice_add_fusion), channel_id=1, source_target_pairs={{0,2},{1,3},{2,4},{3,5},{4,6},{5,7},{6,0},{7,1},{8,10},{9,11},{10,... | collective-permute-start | bytes 3080 | tf_op jit(solution)/shard_map/ppermute | solution.py:480
  120.8 4.5 %copy-start = (f32[16,384,128]{2,1,0:T(8,128)}, f32[16,384,128]{2,1,0:T(8,128)S(1)}, u32[]{:S(2)}) copy-start(f32[16,384,128]{2,1,0:T(8,128)S(1)} %all-to-all-done.1.refs_9_.refs_6_) | copy-start | bytes 9437188
  120.8 20.0 %all-to-all-start.2 = ((f32[16,128,128]{2,1,0:T(8,128)}), f32[16,128,128]{2,1,0:T(8,128)}, u32[]{:S(2)}, u32[]{:S(2)}) async-start(f32[16,128,128]{2,1,0:T(8,128)} %get-tuple-element.65), calls=%async_computation.2 | async-start | bytes 2097152 | tf_op jit(solution)/shard_map/all_to_all | solution.py:613
  145.6 12.8 %all-to-all-start.3 = ((f32[16,8,128]{2,1,0:T(8,128)}), f32[16,8,128]{2,1,0:T(8,128)S(1)}, u32[]{:S(2)}, u32[]{:S(2)}) async-start(f32[16,8,128]{2,1,0:T(8,128)} %get-tuple-element.84), calls=%async_computation.3 | async-start | bytes 131072 | tf_op jit(solution)/shard_map/all_to_all | solution.py:676

commit v5 on v4

--- a/solution.py
+++ b/solution.py
@@ -14,6 +14,7 @@
 PAIR = 2 * HP
 LANES = 8 * HP
 TILE = 8
+COLS = 4
 VMEM = 56 * 1024 * 1024
 F32 = jnp.float32
 BF16 = jnp.bfloat16
@@ -36,23 +37,6 @@
     rest = value - top.astype(F32)
     mid = rest.astype(BF16)
     return top, mid, (rest - mid.astype(F32)).astype(BF16)
-
-
-def spread_matrix(heads):
-    row = lax.broadcasted_iota(jnp.int32, (3 * heads, heads * HP), 0)
-    lane = lax.broadcasted_iota(jnp.int32, (3 * heads, heads * HP), 1)
-    return (lax.rem(row, heads) == lax.div(lane, HP)).astype(BF16)
-
-
-def spread(values, ones_rows):
-    return dot(jnp.concatenate(split3(values), axis=0), ones_rows, TN)
-
-
-def head_sums(product, ones_rows, heads):
-    top = product.astype(BF16)
-    low = (product - top.astype(F32)).astype(BF16)
-    ones = ones_rows[:heads]
-    return dot(ones, top, NT) + dot(ones, low, NT)
 
 
 def softplus(value):
@@ -210,27 +194,27 @@
                     seq * count : (seq + 1) * count, pair * PAIR : (pair + 1) * PAIR
                 ]
 
+    order = np.argsort(snake(count)).tolist()
     pairs = LANES // PAIR
     for pair in range(pairs):
         decay = decay_sc[lax.div(at, parts) * (heads // 2) + part * pairs + pair]
         rows = slice(2 * pair * piece, (2 * pair + 1) * piece)
         total = jnp.zeros((piece, PAIR), F32)
-        for src in range(count):
+        for src in order:
             out_ref[src, rows] = total
             total = decay[src : src + 1] * total + in_ref[src, rows]
         rows = slice((2 * pair + 1) * piece, (2 * pair + 2) * piece)
         total = jnp.zeros((piece, PAIR), F32)
-        for src in reversed(range(count)):
+        for src in reversed(order):
             out_ref[src, rows] = total
             total = decay[src : src + 1] * total + in_ref[src, rows]
 
 
-def intra_kernel(len_ref, x_ref, g_ref, b_ref, c_ref, dt_ref, bias_ref, alog_ref, gain_ref, gather_ref,
-                 dx_ref, db_ref, dc_ref, diff_ref, col_ref, skip_ref, xv_ref, gg_ref, scal_ref, near_ref, aux_ref,
+def intra_kernel(len_ref, x_ref, g_ref, b_ref, c_ref, dt_ref, bias_ref, alog_ref, gain_ref, spread_ref,
+                 gather_ref, dx_ref, db_ref, dc_ref, diff_ref, col_ref, skip_ref, xv_ref, gg_ref, scal_ref, near_ref, aux_ref,
                  y_sc, d_sc, g_sc):
     heads = dt_ref.shape[1]
     seq, blk = pl.program_id(0), pl.program_id(1)
-    ones_rows = spread_matrix(heads)
     raw = dt_ref[0] + column(bias_ref)
     step_all = softplus(raw)
     rate = -jnp.exp(column(alog_ref))
@@ -248,17 +232,20 @@
     tail = jnp.exp(cum[:, QB - 1 : QB] - cum) * step
     grow = jnp.exp(cum)
     near_ref[0] = scale_columns(tail, grow)
+    gain = jnp.broadcast_to(column(gain_ref), (heads, TILE))
+    gain = dot(scale_columns(gain, gain), spread_ref[0], NN)[0:1]
     tail = jnp.exp(jnp.where(first, mid + over, over) - cum) * step
     grow = jnp.exp(cum + jnp.where(first, 0.0, mid))
-    scal_ref[0] = scale_columns(tail, grow)
+    scal = scale_columns(tail, grow)
+    scal_ref[0] = scal
     live = live_rows(token_base(pl.num_programs(1) * QB) + blk * QB, len_ref[seq], QB)
     x_full = x_ref[0].astype(F32)
     g_full = jnp.where(live, g_ref[0].astype(F32), 0.0)
     g_sc[...] = g_full.astype(BF16)
     skips = jnp.sum(x_full * g_full, axis=0, keepdims=True)
     skip_ref[0, 0] = lane_sums(jnp.broadcast_to(skips, (TILE, heads * HP)), gather_ref[0])
-    xv_ref[0] = (x_full * spread(tail, ones_rows)).astype(BF16)
-    gg_ref[0] = (g_full * spread(grow, ones_rows)).astype(BF16)
+    xv_ref[0] = (x_full * dot(scal, spread_ref[0], NN)).astype(BF16)
+    gg_ref[0] = (g_full * dot(scal, spread_ref[1], NN)).astype(BF16)
     gram = dot(c_ref[0], b_ref[0], NT)
     causal = (
         lax.broadcasted_iota(jnp.int32, (HALF, HALF), 0)
@@ -305,11 +292,11 @@
             jnp.concatenate([a2, b2], axis=0),
             jnp.concatenate([gs[0][high], gs[1][high]], axis=0), TN,
         )
-    row = head_sums(g_full * y_sc[...], ones_rows, heads)
-    col = head_sums(x_full * d_sc[...], ones_rows, heads)
+    sums = lane_sums(g_full * y_sc[...], gather_ref[0])
+    sums = (sums + lane_sums(x_full * d_sc[...], gather_ref[1])).T
+    row, col = sums[:heads], sums[heads : 2 * heads]
     diff_ref[0] = row - col
     col_ref[0] = col
-    gain = spread(jnp.broadcast_to(column(gain_ref), (heads, 8)), ones_rows)[0:1]
     dx_ref[0] = d_sc[...] + gain * g_full
     dgram = jnp.concatenate(
         [
@@ -390,18 +377,16 @@
         thru_sc[...] = jnp.zeros_like(thru_sc)
 
     enter, leave = state_of(ends_ref, 0), state_of(ends_ref, 1)
-    for blk in range(2):
-        rows = slice(blk * QB, (blk + 1) * QB)
-        live = live_rows(token_base(toks) + blk * QB, len_ref[seq], QB)
-        grow = dot(scal_ref[0, rows], spread_ref[1], NN)
-        g_grow = jnp.where(live, g_ref[0, rows].astype(F32) * grow, 0.0)
-        y = exact_dot(c_ref[0, rows], enter, NN)
-        tail = dot(scal_ref[0, rows], spread_ref[0], NN)
-        u = tail * exact_dot(b_ref[0, rows], leave, NN)
-        sum_sc[rows] += lane_sums(g_grow * y, gather_ref[0]) + lane_sums(
-            x_ref[0, rows].astype(F32) * u, gather_ref[1]
-        )
-    product = grow[QB - 1 : QB] * jnp.sum(enter * leave, axis=0, keepdims=True)
+    live = live_rows(token_base(toks), len_ref[seq], toks)
+    grow = dot(scal_ref[0], spread_ref[1], NN)
+    g_grow = jnp.where(live, g_ref[0].astype(F32) * grow, 0.0)
+    y = exact_dot(c_ref[0], enter, NN)
+    tail = dot(scal_ref[0], spread_ref[0], NN)
+    u = tail * exact_dot(b_ref[0], leave, NN)
+    sum_sc[...] += lane_sums(g_grow * y, gather_ref[0]) + lane_sums(
+        x_ref[0].astype(F32) * u, gather_ref[1]
+    )
+    product = grow[toks - 1 : toks] * jnp.sum(enter * leave, axis=0, keepdims=True)
     thru_sc[...] += lane_sums(jnp.broadcast_to(product, (TILE, LANES)), gather_ref[0])
 
     @pl.when(part == parts - 1)
@@ -471,6 +456,19 @@
         dc_ref[0] = (gate * dc_sc[...]).astype(BF16)
 
 
+def snake(count):
+    return [
+        COLS * y + (x if y % 2 == 0 else COLS - 1 - x)
+        for y in range(count // COLS)
+        for x in range(COLS)
+    ]
+
+
+def exchange(value):
+    order = snake(lax.axis_size("context"))
+    return lax.all_to_all(value, "context", 0, 0, axis_index_groups=[order])
+
+
 def sum_tensor(value):
     count = lax.axis_size("tensor")
     if count == 1:
@@ -521,7 +519,7 @@
     )(lengths, seq_inputs, out_grad, b_proj, c_proj, dt_raw, bias_row, alog_row, log_ratio,
       spread_ones)
 
-    owned = lax.all_to_all(local, "context", 0, 0)
+    owned = exchange(local)
 
     def chained(unit, number):
         return pl.pallas_call(
@@ -544,7 +542,7 @@
 
     most, sums = chained(0, head_units)
     most, dt_raw = lax.optimization_barrier((most, dt_raw))
-    most = lax.all_to_all(most, "context", 0, 0)
+    most = exchange(most)
 
     tok_spec = lambda w: pl.BlockSpec((1, QB, w), lambda s, b: (s, b, 0))
     head_spec = pl.BlockSpec((1, heads, QB), lambda s, b: (s, 0, b))
@@ -554,7 +552,7 @@
         grid=(seqs, blocks),
         in_specs=[smem, tok_spec(width), tok_spec(width), tok_spec(NS), tok_spec(NS),
                   pl.BlockSpec((1, heads, toks), lambda s, b: (s, 0, 0)), *small, whole(1, heads),
-                  whole(2, width, 128)],
+                  whole(2, 128, width), whole(2, width, 128)],
         out_specs=[tok_spec(width), tok_spec(NS), tok_spec(NS), head_spec, head_spec,
                    pl.BlockSpec((1, 1, TILE, 128), lambda s, b: (s, b, 0, 0)),
                    tok_spec(width), tok_spec(width), tok_spec(128), tok_spec(128),
@@ -579,7 +577,7 @@
         compiler_params=params,
         name="intra",
     )(lengths, seq_inputs, out_grad, b_proj, c_proj, dt_raw, bias_row, alog_row, gain_row,
-      gather_ones)
+      spread_ones, gather_ones)
 
     of_seq = lambda *shape: pl.BlockSpec((1,) + shape, lambda i: (i,) + (0,) * len(shape))
     early = lambda w: pl.BlockSpec((1, QB, w), lambda i: (i, 0, 0))
@@ -610,7 +608,7 @@
     margin = -jnp.sum(signs * totals)
     gate = signs * BETA * jax.nn.sigmoid(-BETA * margin)
     least, gate, dxi = lax.optimization_barrier((least, gate, dxi))
-    least = lax.all_to_all(least, "context", 0, 0)
+    least = exchange(least)
 
     def final(unit, number, back, *before):
         at_seq = lambda *shape: pl.BlockSpec(
@@ -673,7 +671,7 @@
     dx, db, dc = groups(0, (most,))
     least, dx, some = lax.optimization_barrier((least, dx, some))
     ddt, pars, _, _ = final(head_units, units - head_units, least, pars, some, thru, ddt)
-    closing = lax.all_to_all(pars, "context", 0, 0)
+    closing = exchange(pars)
     dx, db, dc = groups(1, (most, least), dx, db, dc)
     sums = jnp.sum(closing, axis=0)[:3, :heads]
     return dx, db, dc, ddt, sums[0], sums[1], sums[2]

time: 160 us -> 158 us (0.988)
  waiting for transfers between devices: 10.8 us -> 5.8 us
  starting transfers between devices: 18.9 us -> 21.6 us
    all_to_all x3, waiting for transfers between devices: 9.7 us -> 4.66 us  [exchange(): return lax.all_to_all(value, 'context', 0, 0, axis_index_groups=[order])]
    all_to_all x3, starting transfers between devices: 13.6 us -> 16.3 us  [exchange(): return lax.all_to_all(value, 'context', 0, 0, axis_index_groups=[order])]
  transfers between devices with their start and end apart: 7 -> 7, of which waited for: 4 -> 3; matrix products, arithmetic and copies ran while one was open for 1% -> 1% of each run, Pallas kernels for 31% -> 32%
where the time goes in v5:
time: 158 us; the launch traced here: 157 us
  Pallas kernels  67.6 us (43%)
  blocking collectives  58.7 us (37%)
  starting transfers between devices  21.6 us (14%)
  waiting for transfers between devices  5.8 us (4%)
    all_to_all x1, blocking collectives, exchange(): return lax.all_to_all(value, 'context', 0, 0, axis_index_groups=[order])  58.7 us
    pallas_call x1, Pallas kernels, on_device(): pl.pallas_call(intra_kernel, grid=(seqs, blocks), in_specs=[smem, tok_spe...  17.9 us
    all_to_all x3, starting transfers between devices, exchange(): return lax.all_to_all(value, 'context', 0, 0, axis_index_groups=[order])  16.3 us
    pallas_call x2, Pallas kernels, final(): pl.pallas_call(lambda *refs: final_kernel(unit, heads, *refs), grid=(numb...  13.2 us
    pallas_call x2, Pallas kernels, groups(): pl.pallas_call(lambda *refs: groups_kernel(seq, *refs), grid=(parts,), in...  10.5 us
    pallas_call x1, Pallas kernels, on_device(): pl.pallas_call(cross_kernel, grid=(seqs,), in_specs=[smem, early(width),...  10.2 us
    pallas_call x1, Pallas kernels, on_device(): pl.pallas_call(states_kernel, grid=(seqs + 1,), in_specs=[smem, of_either...  8.21 us
    pallas_call x2, Pallas kernels, chained(): pl.pallas_call(lambda *refs: chain_kernel(unit, heads, *refs), grid=(numb...  7.57 us
  transfers between devices with their start and end apart: 7, of which 3 were waited for; matrix products, arithmetic and copies ran while one was open for 1% of the time, Pallas kernels for 32%

profile of v5, /device:TPU:0, one launch (start us, length us, event | category | flops | bytes accessed | tf_op | source)
XLA Modules:
  0.0 157.0 jit_solution(13155712025033587075)
XLA Ops:
  0.6 8.2 %states.1 = f32[16,520,128]{2,1,0:T(8,128)} custom-call(s32[2]{0:T(128)} %refs_0_.3, bf16[2,512,1024]{2,1,0:T(8,128)(2,1)} %refs_2_.5, bf16[2,512,1024]{2,1,0:T(8,128)(2,1)} %refs_3_.3, bf16[2,512,256]{2,1,0:T(8,128)(2,1)} %refs_4_.3, bf16[2,512,256]{2,1,0:T(8,128)(2,1)} %refs_5_.3, f32[2,16,512]{2,1,0:T(8,128)} %dt_ref.2, f32[1,16]{1,0:T(1,128)} %bitcast.9, ...), custom_call_target="tpu_custom_call" | custom-call | tf_op jit(solution)/shard_map/states/pallas_call | solution.py:506
  8.8 58.7 %all_to_all.20.refs_0_.refs_1_ = f32[16,520,128]{2,1,0:T(8,128)} all-to-all(f32[16,520,128]{2,1,0:T(8,128)} %states.1), channel_id=1, replica_groups={{0,8,16,24,56,48,40,32,64,72,80,88,120,112,104,96},{1,9,17,25,57,49,41,..., dimensions={0} | all-to-all | bytes 8519680 | tf_op jit(solution)/shard_map/all_to_all | solution.py:469
  67.6 4.8 %chain.3 = (f32[16,384,128]{2,1,0:T(8,128)}, f32[8,128]{1,0:T(8,128)}) custom-call(f32[16,520,128]{2,1,0:T(8,128)} %all_to_all.20.refs_0_.refs_1_, f32[16,520,128]{2,1,0:T(8,128)} %all_to_all.20.refs_0_.refs_1_, bf16[2,128,1024]{2,1,0:T(8,128)(2,1)} %constant.16.clone.spread_ref.refs_2_.refs_8_.refs_12_), custom_call_target="tpu_custom_call" | custom-call | tf_op jit(solution)/shard_map/chain/pallas_call | solution.py:525
  72.4 3.9 %all-to-all-start.1 = ((f32[16,384,128]{2,1,0:T(8,128)}), f32[16,384,128]{2,1,0:T(8,128)S(1)}, u32[]{:S(2)}, u32[]{:S(2)}) async-start(f32[16,384,128]{2,1,0:T(8,128)} %get-tuple-element.64), calls=%async_computation.1 | async-start | bytes 6291456 | tf_op jit(solution)/shard_map/all_to_all | solution.py:469
  76.3 0.1 collective-permute-start
  76.4 1.1 collective-permute-done
  77.5 4.0 %collective-permute-start.3 = (f32[2,128]{1,0:T(2,128)S(1)}, f32[2,128]{1,0:T(2,128)S(1)}, u32[]{:S(2)}, u32[]{:S(2)}) collective-permute-start(f32[2,128]{1,0:T(2,128)S(1)} %slice_add_fusion), channel_id=1, source_target_pairs={{0,6},{1,7},{2,0},{3,1},{4,2},{5,3},{6,4},{7,5},{8,14},{9,15},{10,... | collective-permute-start | bytes 3080 | tf_op jit(solution)/shard_map/ppermute | solution.py:478
  81.6 1.3 collective-permute-start.1
  82.8 17.9 %intra.1 = (f32[2,512,1024]{2,1,0:T(8,128)}, f32[2,512,256]{2,1,0:T(8,128)}, f32[2,512,256]{2,1,0:T(8,128)}, f32[2,16,512]{2,1,0:T(8,128)}, f32[2,16,512]{2,1,0:...) custom-call(s32[2]{0:T(128)} %refs_0_.3, ...), custom_call_target="tpu_custom_call" | custom-call | tf_op jit(solution)/shard_map/intra/pallas_call | solution.py:550
  100.7 10.2 %cross.1 = (f32[2,16,512]{2,1,0:T(8,128)}, f32[2,16,512]{2,1,0:T(8,128)}, f32[2,512,1024]{2,1,0:T(8,128)}, f32[2,512,256]{2,1,0:T(8,128)}, f32[2,512,256]{2,1,0:T(8,128)}) custom-call(s32[2]{0:T(128)} %refs_0_.3, bf16[2,512,1024]{2,1,0:T(8,128)(2,1)} %refs_2_.5, ...), custom_call_target="tpu_custom_call", output_to_operand_aliasing={{2}: (10, {}), {3}: (11, {}), {4}: (12, {})} | custom-call | tf_op jit(solution)/shard_map/cross/pallas_call | solution.py:585
  111.0 2.7 %chain.2 = (f32[16,128,128]{2,1,0:T(8,128)}, f32[8,128]{1,0:T(8,128)}) custom-call(f32[16,520,128]{2,1,0:T(8,128)} %all_to_all.20.refs_0_.refs_1_, f32[16,520,128]{2,1,0:T(8,128)} %all_to_all.20.refs_0_.refs_1_, bf16[2,128,1024]{2,1,0:T(8,128)(2,1)} %constant.16.clone.spread_ref.refs_2_.refs_8_.refs_12_), custom_call_target="tpu_custom_call" | custom-call | tf_op jit(solution)/shard_map/chain/pallas_call | solution.py:525
  113.7 0.0 collective-permute-done.1
  113.7 0.1 slice_reduce_fusion
  113.8 0.6 multiply_reduce_fusion
  115.2 0.5 fusion.refs_0_.refs_1_
  115.7 7.5 %all-to-all-start.2 = ((f32[16,128,128]{2,1,0:T(8,128)}), f32[16,128,128]{2,1,0:T(8,128)}, u32[]{:S(2)}, u32[]{:S(2)}) async-start(f32[16,128,128]{2,1,0:T(8,128)} %get-tuple-element.65), calls=%async_computation.2 | async-start | bytes 2097152 | tf_op jit(solution)/shard_map/all_to_all | solution.py:469
  123.2 8.4 %final.2 = (f32[2,16,512]{2,1,0:T(8,128)}, f32[16,8,128]{2,1,0:T(8,128)}, f32[512,128]{1,0:T(8,128)}, f32[8,128]{1,0:T(8,128)}) custom-call(s32[2]{0:T(128)} %refs_0_.3, f32[2]{0:T(128)} %fusion.refs_0_.refs_1_, bf16[2,512,1024]{2,1,0:T(8,128)(2,1)} %refs_2_.5, bf16[2,512,1024]{2,1,0:T(8,128)(2,1)} %refs_3_.3, bf16[2,512,256]{2,1,0:T(8,128)(2,1)} %refs_4_.3, ...), custom_call_target="tpu_custom_call" | custom-call | tf_op jit(solution)/shard_map/final/pallas_call | solution.py:620
  131.7 5.2 %groups.2 = (bf16[2,512,1024]{2,1,0:T(8,128)(2,1)}, bf16[2,512,256]{2,1,0:T(8,128)(2,1)}, bf16[2,512,256]{2,1,0:T(8,128)(2,1)}) custom-call(f32[2]{0:T(128)} %fusion.refs_0_.refs_1_, bf16[2,512,256]{2,1,0:T(8,128)(2,1)} %refs_4_.3, bf16[2,512,128]{2,1,0:T(8,128)(2,1)} %get-tuple-element.58.refs_2_.refs_7_, bf16[2,512,1024]{2,1,0:T(8,128)(2,1)} %get-tuple-element.59.refs_3_, ...), custom_call_target="tpu_custom_call" | custom-call | tf_op jit(solution)/shard_map/groups/pallas_call | solution.py:655
  136.9 2.3 %all-to-all-done.2.refs_10_.refs_6_ = f32[16,128,128]{2,1,0:T(8,128)} async-done(((f32[16,128,128]{2,1,0:T(8,128)}), f32[16,128,128]{2,1,0:T(8,128)}, u32[]{:S(2)}, u32[]{:S(2)}) %all-to-all-start.2) | async-done | bytes 1048608 | tf_op jit(solution)/shard_map/all_to_all | solution.py:469
  139.2 4.8 %final.3 = (f32[2,16,512]{2,1,0:T(8,128)}, f32[16,8,128]{2,1,0:T(8,128)}, f32[512,128]{1,0:T(8,128)}, f32[8,128]{1,0:T(8,128)}) custom-call(s32[2]{0:T(128)} %refs_0_.3, f32[2]{0:T(128)} %fusion.refs_0_.refs_1_, bf16[2,512,1024]{2,1,0:T(8,128)(2,1)} %refs_2_.5, bf16[2,512,1024]{2,1,0:T(8,128)(2,1)} %refs_3_.3, ...), custom_call_target="tpu_custom_call", output_to_operand_aliasing={{0}: (17, {})} | custom-call | tf_op jit(solution)/shard_map/final/pallas_call | solution.py:620
  144.0 4.8 %all-to-all-start.3 = ((f32[16,8,128]{2,1,0:T(8,128)}), f32[16,8,128]{2,1,0:T(8,128)S(1)}, u32[]{:S(2)}, u32[]{:S(2)}) async-start(f32[16,8,128]{2,1,0:T(8,128)} %get-tuple-element.84), calls=%async_computation.3 | async-start | bytes 131072 | tf_op jit(solution)/shard_map/all_to_all | solution.py:469
  148.8 5.3 %groups.3 = (bf16[2,512,1024]{2,1,0:T(8,128)(2,1)}, bf16[2,512,256]{2,1,0:T(8,128)(2,1)}, bf16[2,512,256]{2,1,0:T(8,128)(2,1)}) custom-call(f32[2]{0:T(128)} %fusion.refs_0_.refs_1_, bf16[2,512,256]{2,1,0:T(8,128)(2,1)} %refs_4_.3, ...), custom_call_target="tpu_custom_call", output_to_operand_aliasing={{0}: (11, {}), {1}: (12, {}), {2}: (13, {})} | custom-call | tf_op jit(solution)/shard_map/groups/pallas_call | solution.py:655
  154.1 2.3 %all-to-all-done.3 = f32[16,8,128]{2,1,0:T(8,128)S(1)} async-done(((f32[16,8,128]{2,1,0:T(8,128)}), f32[16,8,128]{2,1,0:T(8,128)S(1)}, u32[]{:S(2)}, u32[]{:S(2)}) %all-to-all-start.3) | async-done | bytes 65568 | tf_op jit(solution)/shard_map/all_to_all | solution.py:469
  156.5 0.5 slice_bitcast_fusion
  (12 shorter events, 0.1 us)
Async XLA Ops:
  72.4 3.9 %copy-start.1 = (f32[8,128]{1,0:T(8,128)S(1)}, f32[8,128]{1,0:T(8,128)}, u32[]{:S(2)}) copy-start(f32[8,128]{1,0:T(8,128)} %get-tuple-element.47) | copy-start | bytes 12292
  72.4 43.3 %all-to-all-start.1 = ((f32[16,384,128]{2,1,0:T(8,128)}), f32[16,384,128]{2,1,0:T(8,128)S(1)}, u32[]{:S(2)}, u32[]{:S(2)}) async-start(f32[16,384,128]{2,1,0:T(8,128)} %get-tuple-element.64), calls=%async_computation.1 | async-start | bytes 6291456 | tf_op jit(solution)/shard_map/all_to_all | solution.py:469
  76.3 1.2 collective-permute-start
  77.5 36.2 %collective-permute-start.3 = (f32[2,128]{1,0:T(2,128)S(1)}, f32[2,128]{1,0:T(2,128)S(1)}, u32[]{:S(2)}, u32[]{:S(2)}) collective-permute-start(f32[2,128]{1,0:T(2,128)S(1)} %slice_add_fusion), channel_id=1, source_target_pairs={{0,6},{1,7},{2,0},{3,1},{4,2},{5,3},{6,4},{7,5},{8,14},{9,15},{10,... | collective-permute-start | bytes 3080 | tf_op jit(solution)/shard_map/ppermute | solution.py:478
  81.6 32.1 %collective-permute-start.2 = (f32[2,128]{1,0:T(2,128)S(1)}, f32[2,128]{1,0:T(2,128)S(1)}, u32[]{:S(2)}, u32[]{:S(2)}) collective-permute-start(f32[2,128]{1,0:T(2,128)S(1)} %slice_add_fusion), channel_id=1, source_target_pairs={{0,4},{1,5},{2,6},{3,7},{4,0},{5,1},{6,2},{7,3},{8,12},{9,13},{10,... | collective-permute-start | bytes 3080 | tf_op jit(solution)/shard_map/ppermute | solution.py:478
  81.6 32.1 %collective-permute-start.1 = (f32[2,128]{1,0:T(2,128)S(1)}, f32[2,128]{1,0:T(2,128)S(1)}, u32[]{:S(2)}, u32[]{:S(2)}) collective-permute-start(f32[2,128]{1,0:T(2,128)S(1)} %slice_add_fusion), channel_id=1, source_target_pairs={{0,2},{1,3},{2,4},{3,5},{4,6},{5,7},{6,0},{7,1},{8,10},{9,11},{10,... | collective-permute-start | bytes 3080 | tf_op jit(solution)/shard_map/ppermute | solution.py:478
  115.7 7.5 %copy-start = (f32[16,384,128]{2,1,0:T(8,128)}, f32[16,384,128]{2,1,0:T(8,128)S(1)}, u32[]{:S(2)}) copy-start(f32[16,384,128]{2,1,0:T(8,128)S(1)} %all-to-all-done.1.refs_9_.refs_6_) | copy-start | bytes 9437188
  115.7 23.5 %all-to-all-start.2 = ((f32[16,128,128]{2,1,0:T(8,128)}), f32[16,128,128]{2,1,0:T(8,128)}, u32[]{:S(2)}, u32[]{:S(2)}) async-start(f32[16,128,128]{2,1,0:T(8,128)} %get-tuple-element.65), calls=%async_computation.2 | async-start | bytes 2097152 | tf_op jit(solution)/shard_map/all_to_all | solution.py:469
  144.0 12.5 %all-to-all-start.3 = ((f32[16,8,128]{2,1,0:T(8,128)}), f32[16,8,128]{2,1,0:T(8,128)S(1)}, u32[]{:S(2)}, u32[]{:S(2)}) async-start(f32[16,8,128]{2,1,0:T(8,128)} %get-tuple-element.84), calls=%async_computation.3 | async-start | bytes 131072 | tf_op jit(solution)/shard_map/all_to_all | solution.py:469

commit v6 on v5

--- a/solution.py
+++ b/solution.py
@@ -194,19 +194,20 @@
                     seq * count : (seq + 1) * count, pair * PAIR : (pair + 1) * PAIR
                 ]
 
-    order = np.argsort(snake(count)).tolist()
+    came, goes = np.argsort(backwards(count)).tolist(), np.argsort(snake(count)).tolist()
+    order = list(zip(came, goes))
     pairs = LANES // PAIR
     for pair in range(pairs):
         decay = decay_sc[lax.div(at, parts) * (heads // 2) + part * pairs + pair]
         rows = slice(2 * pair * piece, (2 * pair + 1) * piece)
         total = jnp.zeros((piece, PAIR), F32)
-        for src in order:
-            out_ref[src, rows] = total
+        for src, dst in order:
+            out_ref[dst, rows] = total
             total = decay[src : src + 1] * total + in_ref[src, rows]
         rows = slice((2 * pair + 1) * piece, (2 * pair + 2) * piece)
         total = jnp.zeros((piece, PAIR), F32)
-        for src in reversed(order):
-            out_ref[src, rows] = total
+        for src, dst in reversed(order):
+            out_ref[dst, rows] = total
             total = decay[src : src + 1] * total + in_ref[src, rows]
 
 
@@ -323,10 +324,9 @@
     early, late = x_tail.astype(BF16), g_grow.astype(BF16)
     b_early, c_late = b_ref[0], c_ref[0]
     gram = dot(c_late, b_early, NT)
-    y, back = 0.0, 0.0
-    for part in split3(gram)[:2]:
-        y = y + exact_dot(part, x_tail, NN)
-        back = back + exact_dot(part, g_grow, TN)
+    top, low, _ = split3(gram)
+    y = exact_dot(top, x_tail, NN) + dot(low, early, NN)
+    back = exact_dot(top, g_grow, TN) + dot(low, late, TN)
     dgram = dot(late, early, NT).astype(BF16)
     dc_ref[0] = dci_ref[0] + dot(dgram, b_early, NN)
     db_ref[0] = dbi_ref[0] + dot(dgram, c_late, TN)
@@ -343,15 +343,16 @@
 
 
 def state_of(ends_ref, scan):
-    piece = NS // ends_ref.shape[0]
+    count = ends_ref.shape[0]
+    piece = NS // count
     pairs = ends_ref.shape[1] // (2 * piece)
-    return jnp.concatenate(
-        [
-            ends_ref[:, (2 * p + scan) * piece : (2 * p + scan + 1) * piece].reshape(NS, PAIR)
-            for p in range(pairs)
-        ],
-        axis=1,
-    )
+    goes = np.argsort(snake(count))
+    places = [int(goes[owner]) for owner in backwards(count)]
+    columns = []
+    for pair in range(pairs):
+        rows = slice((2 * pair + scan) * piece, (2 * pair + scan + 1) * piece)
+        columns.append(jnp.concatenate([ends_ref[place, rows] for place in places], axis=0))
+    return jnp.concatenate(columns, axis=1)
 
 
 def final_kernel(unit, heads, len_ref, gate_ref, x_ref, g_ref, b_ref, c_ref, ends_ref, scal_ref,
@@ -464,9 +465,14 @@
     ]
 
 
-def exchange(value):
-    order = snake(lax.axis_size("context"))
-    return lax.all_to_all(value, "context", 0, 0, axis_index_groups=[order])
+def backwards(count):
+    return list(range(count))[::-1]
+
+
+def exchange(value, order):
+    return lax.all_to_all(
+        value, "context", 0, 0, axis_index_groups=[order(lax.axis_size("context"))]
+    )
 
 
 def sum_tensor(value):
@@ -519,7 +525,7 @@
     )(lengths, seq_inputs, out_grad, b_proj, c_proj, dt_raw, bias_row, alog_row, log_ratio,
       spread_ones)
 
-    owned = exchange(local)
+    owned = exchange(local, backwards)
 
     def chained(unit, number):
         return pl.pallas_call(
@@ -542,7 +548,7 @@
 
     most, sums = chained(0, head_units)
     most, dt_raw = lax.optimization_barrier((most, dt_raw))
-    most = exchange(most)
+    most = exchange(most, snake)
 
     tok_spec = lambda w: pl.BlockSpec((1, QB, w), lambda s, b: (s, b, 0))
     head_spec = pl.BlockSpec((1, heads, QB), lambda s, b: (s, 0, b))
@@ -608,7 +614,7 @@
     margin = -jnp.sum(signs * totals)
     gate = signs * BETA * jax.nn.sigmoid(-BETA * margin)
     least, gate, dxi = lax.optimization_barrier((least, gate, dxi))
-    least = exchange(least)
+    least = exchange(least, snake)
 
     def final(unit, number, back, *before):
         at_seq = lambda *shape: pl.BlockSpec(
@@ -671,7 +677,7 @@
     dx, db, dc = groups(0, (most,))
     least, dx, some = lax.optimization_barrier((least, dx, some))
     ddt, pars, _, _ = final(head_units, units - head_units, least, pars, some, thru, ddt)
-    closing = exchange(pars)
+    closing = exchange(pars, snake)
     dx, db, dc = groups(1, (most, least), dx, db, dc)
     sums = jnp.sum(closing, axis=0)[:3, :heads]
     return dx, db, dc, ddt, sums[0], sums[1], sums[2]

time: 158 us -> 159 us (level)
  transfers between devices with their start and end apart: 7 -> 7, of which waited for: 3 -> 4; matrix products, arithmetic and copies ran while one was open for 1% -> 1% of each run, Pallas kernels for 32% -> 31%
where the time goes in v6:
time: 159 us; the launch traced here: 158 us
  Pallas kernels  67 us (42%)
  blocking collectives  58.1 us (37%)
  starting transfers between devices  22.8 us (14%)
  waiting for transfers between devices  6.79 us (4%)
    all_to_all x1, blocking collectives, exchange(): lax.all_to_all(value, 'context', 0, 0, axis_index_groups=[order(lax.axis_...  58.1 us
    pallas_call x1, Pallas kernels, on_device(): pl.pallas_call(intra_kernel, grid=(seqs, blocks), in_specs=[smem, tok_spe...  17.9 us
    all_to_all x3, starting transfers between devices, exchange(): lax.all_to_all(value, 'context', 0, 0, axis_index_groups=[order(lax.axis_...  17.4 us
    pallas_call x2, Pallas kernels, final(): pl.pallas_call(lambda *refs: final_kernel(unit, heads, *refs), grid=(numb...  13.2 us
    pallas_call x2, Pallas kernels, groups(): pl.pallas_call(lambda *refs: groups_kernel(seq, *refs), grid=(parts,), in...  10.5 us
    pallas_call x1, Pallas kernels, on_device(): pl.pallas_call(cross_kernel, grid=(seqs,), in_specs=[smem, early(width),...  9.67 us
    pallas_call x1, Pallas kernels, on_device(): pl.pallas_call(states_kernel, grid=(seqs + 1,), in_specs=[smem, of_either...  8.21 us
    pallas_call x2, Pallas kernels, chained(): pl.pallas_call(lambda *refs: chain_kernel(unit, heads, *refs), grid=(numb...  7.56 us
  transfers between devices with their start and end apart: 7, of which 4 were waited for; matrix products, arithmetic and copies ran while one was open for 1% of the time, Pallas kernels for 31%

profile of v6, /device:TPU:0, one launch (start us, length us, event | category | flops | bytes accessed | tf_op | source)
XLA Modules:
  0.0 158.0 jit_solution(9286733794528002049)
XLA Ops:
  0.6 8.2 %states.1 = f32[16,520,128]{2,1,0:T(8,128)} custom-call(s32[2]{0:T(128)} %refs_0_.3, bf16[2,512,1024]{2,1,0:T(8,128)(2,1)} %refs_2_.5, bf16[2,512,1024]{2,1,0:T(8,128)(2,1)} %refs_3_.3, bf16[2,512,256]{2,1,0:T(8,128)(2,1)} %refs_4_.3, bf16[2,512,256]{2,1,0:T(8,128)(2,1)} %refs_5_.3, f32[2,16,512]{2,1,0:T(8,128)} %dt_ref.2, f32[1,16]{1,0:T(1,128)} %bitcast.9, ...), custom_call_target="tpu_custom_call" | custom-call | tf_op jit(solution)/shard_map/states/pallas_call | solution.py:512
  8.8 58.1 %all_to_all.20.refs_0_.refs_1_ = f32[16,520,128]{2,1,0:T(8,128)} all-to-all(f32[16,520,128]{2,1,0:T(8,128)} %states.1), channel_id=1, replica_groups={{120,112,104,96,88,80,72,64,56,48,40,32,24,16,8,0},{121,113,105,97,89,8..., dimensions={0} | all-to-all | bytes 8519680 | tf_op jit(solution)/shard_map/all_to_all | solution.py:473
  66.9 4.8 %chain.3 = (f32[16,384,128]{2,1,0:T(8,128)}, f32[8,128]{1,0:T(8,128)}) custom-call(f32[16,520,128]{2,1,0:T(8,128)} %all_to_all.20.refs_0_.refs_1_, f32[16,520,128]{2,1,0:T(8,128)} %all_to_all.20.refs_0_.refs_1_, bf16[2,128,1024]{2,1,0:T(8,128)(2,1)} %constant.16.clone.spread_ref.refs_2_.refs_8_.refs_12_), custom_call_target="tpu_custom_call" | custom-call | tf_op jit(solution)/shard_map/chain/pallas_call | solution.py:531
  71.8 5.1 %all-to-all-start.1 = ((f32[16,384,128]{2,1,0:T(8,128)}), f32[16,384,128]{2,1,0:T(8,128)S(1)}, u32[]{:S(2)}, u32[]{:S(2)}) async-start(f32[16,384,128]{2,1,0:T(8,128)} %get-tuple-element.64), calls=%async_computation.1 | async-start | bytes 6291456 | tf_op jit(solution)/shard_map/all_to_all | solution.py:473
  76.9 0.1 collective-permute-start
  77.0 1.1 collective-permute-done
  78.1 4.0 %collective-permute-start.3 = (f32[2,128]{1,0:T(2,128)S(1)}, f32[2,128]{1,0:T(2,128)S(1)}, u32[]{:S(2)}, u32[]{:S(2)}) collective-permute-start(f32[2,128]{1,0:T(2,128)S(1)} %slice_add_fusion), channel_id=1, source_target_pairs={{0,6},{1,7},{2,0},{3,1},{4,2},{5,3},{6,4},{7,5},{8,14},{9,15},{10,... | collective-permute-start | bytes 3080 | tf_op jit(solution)/shard_map/ppermute | solution.py:484
  82.2 1.3 collective-permute-start.1
  83.4 17.9 %intra.1 = (f32[2,512,1024]{2,1,0:T(8,128)}, f32[2,512,256]{2,1,0:T(8,128)}, f32[2,512,256]{2,1,0:T(8,128)}, f32[2,16,512]{2,1,0:T(8,128)}, f32[2,16,512]{2,1,0:...) custom-call(s32[2]{0:T(128)} %refs_0_.3, ...), custom_call_target="tpu_custom_call" | custom-call | tf_op jit(solution)/shard_map/intra/pallas_call | solution.py:556
  101.3 9.7 %cross.1 = (f32[2,16,512]{2,1,0:T(8,128)}, f32[2,16,512]{2,1,0:T(8,128)}, f32[2,512,1024]{2,1,0:T(8,128)}, f32[2,512,256]{2,1,0:T(8,128)}, f32[2,512,256]{2,1,0:T(8,128)}) custom-call(s32[2]{0:T(128)} %refs_0_.3, bf16[2,512,1024]{2,1,0:T(8,128)(2,1)} %refs_2_.5, ...), custom_call_target="tpu_custom_call", output_to_operand_aliasing={{2}: (10, {}), {3}: (11, {}), {4}: (12, {})} | custom-call | tf_op jit(solution)/shard_map/cross/pallas_call | solution.py:591
  111.0 2.7 %chain.2 = (f32[16,128,128]{2,1,0:T(8,128)}, f32[8,128]{1,0:T(8,128)}) custom-call(f32[16,520,128]{2,1,0:T(8,128)} %all_to_all.20.refs_0_.refs_1_, f32[16,520,128]{2,1,0:T(8,128)} %all_to_all.20.refs_0_.refs_1_, bf16[2,128,1024]{2,1,0:T(8,128)(2,1)} %constant.16.clone.spread_ref.refs_2_.refs_8_.refs_12_), custom_call_target="tpu_custom_call" | custom-call | tf_op jit(solution)/shard_map/chain/pallas_call | solution.py:531
  113.8 0.1 slice_reduce_fusion
  113.9 0.6 multiply_reduce_fusion
  115.2 0.5 fusion.refs_0_.refs_1_
  115.7 0.9 all-to-all-done.1.refs_9_.refs_6_
  116.6 7.5 %all-to-all-start.2 = ((f32[16,128,128]{2,1,0:T(8,128)}), f32[16,128,128]{2,1,0:T(8,128)}, u32[]{:S(2)}, u32[]{:S(2)}) async-start(f32[16,128,128]{2,1,0:T(8,128)} %get-tuple-element.65), calls=%async_computation.2 | async-start | bytes 2097152 | tf_op jit(solution)/shard_map/all_to_all | solution.py:473
  124.2 8.4 %final.2 = (f32[2,16,512]{2,1,0:T(8,128)}, f32[16,8,128]{2,1,0:T(8,128)}, f32[512,128]{1,0:T(8,128)}, f32[8,128]{1,0:T(8,128)}) custom-call(s32[2]{0:T(128)} %refs_0_.3, f32[2]{0:T(128)} %fusion.refs_0_.refs_1_, bf16[2,512,1024]{2,1,0:T(8,128)(2,1)} %refs_2_.5, bf16[2,512,1024]{2,1,0:T(8,128)(2,1)} %refs_3_.3, bf16[2,512,256]{2,1,0:T(8,128)(2,1)} %refs_4_.3, ...), custom_call_target="tpu_custom_call" | custom-call | tf_op jit(solution)/shard_map/final/pallas_call | solution.py:626
  132.6 5.2 %groups.2 = (bf16[2,512,1024]{2,1,0:T(8,128)(2,1)}, bf16[2,512,256]{2,1,0:T(8,128)(2,1)}, bf16[2,512,256]{2,1,0:T(8,128)(2,1)}) custom-call(f32[2]{0:T(128)} %fusion.refs_0_.refs_1_, bf16[2,512,256]{2,1,0:T(8,128)(2,1)} %refs_4_.3, bf16[2,512,128]{2,1,0:T(8,128)(2,1)} %get-tuple-element.58.refs_2_.refs_7_, bf16[2,512,1024]{2,1,0:T(8,128)(2,1)} %get-tuple-element.59.refs_3_, ...), custom_call_target="tpu_custom_call" | custom-call | tf_op jit(solution)/shard_map/groups/pallas_call | solution.py:661
  137.8 2.5 %all-to-all-done.2.refs_10_.refs_6_ = f32[16,128,128]{2,1,0:T(8,128)} async-done(((f32[16,128,128]{2,1,0:T(8,128)}), f32[16,128,128]{2,1,0:T(8,128)}, u32[]{:S(2)}, u32[]{:S(2)}) %all-to-all-start.2) | async-done | bytes 1048608 | tf_op jit(solution)/shard_map/all_to_all | solution.py:473
  140.3 4.8 %final.3 = (f32[2,16,512]{2,1,0:T(8,128)}, f32[16,8,128]{2,1,0:T(8,128)}, f32[512,128]{1,0:T(8,128)}, f32[8,128]{1,0:T(8,128)}) custom-call(s32[2]{0:T(128)} %refs_0_.3, f32[2]{0:T(128)} %fusion.refs_0_.refs_1_, bf16[2,512,1024]{2,1,0:T(8,128)(2,1)} %refs_2_.5, bf16[2,512,1024]{2,1,0:T(8,128)(2,1)} %refs_3_.3, ...), custom_call_target="tpu_custom_call", output_to_operand_aliasing={{0}: (17, {})} | custom-call | tf_op jit(solution)/shard_map/final/pallas_call | solution.py:626
  145.0 4.8 %all-to-all-start.3 = ((f32[16,8,128]{2,1,0:T(8,128)}), f32[16,8,128]{2,1,0:T(8,128)S(1)}, u32[]{:S(2)}, u32[]{:S(2)}) async-start(f32[16,8,128]{2,1,0:T(8,128)} %get-tuple-element.84), calls=%async_computation.3 | async-start | bytes 131072 | tf_op jit(solution)/shard_map/all_to_all | solution.py:473
  149.8 5.3 %groups.3 = (bf16[2,512,1024]{2,1,0:T(8,128)(2,1)}, bf16[2,512,256]{2,1,0:T(8,128)(2,1)}, bf16[2,512,256]{2,1,0:T(8,128)(2,1)}) custom-call(f32[2]{0:T(128)} %fusion.refs_0_.refs_1_, bf16[2,512,256]{2,1,0:T(8,128)(2,1)} %refs_4_.3, ...), custom_call_target="tpu_custom_call", output_to_operand_aliasing={{0}: (11, {}), {1}: (12, {}), {2}: (13, {})} | custom-call | tf_op jit(solution)/shard_map/groups/pallas_call | solution.py:661
  155.1 2.3 %all-to-all-done.3 = f32[16,8,128]{2,1,0:T(8,128)S(1)} async-done(((f32[16,8,128]{2,1,0:T(8,128)}), f32[16,8,128]{2,1,0:T(8,128)S(1)}, u32[]{:S(2)}, u32[]{:S(2)}) %all-to-all-start.3) | async-done | bytes 65568 | tf_op jit(solution)/shard_map/all_to_all | solution.py:473
  157.5 0.5 slice_bitcast_fusion
  (12 shorter events, 0.1 us)
Async XLA Ops:
  71.8 5.1 %copy-start.1 = (f32[8,128]{1,0:T(8,128)S(1)}, f32[8,128]{1,0:T(8,128)}, u32[]{:S(2)}) copy-start(f32[8,128]{1,0:T(8,128)} %get-tuple-element.47) | copy-start | bytes 12292
  71.8 44.9 %all-to-all-start.1 = ((f32[16,384,128]{2,1,0:T(8,128)}), f32[16,384,128]{2,1,0:T(8,128)S(1)}, u32[]{:S(2)}, u32[]{:S(2)}) async-start(f32[16,384,128]{2,1,0:T(8,128)} %get-tuple-element.64), calls=%async_computation.1 | async-start | bytes 6291456 | tf_op jit(solution)/shard_map/all_to_all | solution.py:473
  76.9 1.2 collective-permute-start
  78.1 35.6 %collective-permute-start.3 = (f32[2,128]{1,0:T(2,128)S(1)}, f32[2,128]{1,0:T(2,128)S(1)}, u32[]{:S(2)}, u32[]{:S(2)}) collective-permute-start(f32[2,128]{1,0:T(2,128)S(1)} %slice_add_fusion), channel_id=1, source_target_pairs={{0,6},{1,7},{2,0},{3,1},{4,2},{5,3},{6,4},{7,5},{8,14},{9,15},{10,... | collective-permute-start | bytes 3080 | tf_op jit(solution)/shard_map/ppermute | solution.py:484
  82.2 31.6 %collective-permute-start.2 = (f32[2,128]{1,0:T(2,128)S(1)}, f32[2,128]{1,0:T(2,128)S(1)}, u32[]{:S(2)}, u32[]{:S(2)}) collective-permute-start(f32[2,128]{1,0:T(2,128)S(1)} %slice_add_fusion), channel_id=1, source_target_pairs={{0,4},{1,5},{2,6},{3,7},{4,0},{5,1},{6,2},{7,3},{8,12},{9,13},{10,... | collective-permute-start | bytes 3080 | tf_op jit(solution)/shard_map/ppermute | solution.py:484
  82.2 31.6 %collective-permute-start.1 = (f32[2,128]{1,0:T(2,128)S(1)}, f32[2,128]{1,0:T(2,128)S(1)}, u32[]{:S(2)}, u32[]{:S(2)}) collective-permute-start(f32[2,128]{1,0:T(2,128)S(1)} %slice_add_fusion), channel_id=1, source_target_pairs={{0,2},{1,3},{2,4},{3,5},{4,6},{5,7},{6,0},{7,1},{8,10},{9,11},{10,... | collective-permute-start | bytes 3080 | tf_op jit(solution)/shard_map/ppermute | solution.py:484
  116.6 7.5 %copy-start = (f32[16,384,128]{2,1,0:T(8,128)}, f32[16,384,128]{2,1,0:T(8,128)S(1)}, u32[]{:S(2)}) copy-start(f32[16,384,128]{2,1,0:T(8,128)S(1)} %all-to-all-done.1.refs_9_.refs_6_) | copy-start | bytes 9437188
  116.6 23.6 %all-to-all-start.2 = ((f32[16,128,128]{2,1,0:T(8,128)}), f32[16,128,128]{2,1,0:T(8,128)}, u32[]{:S(2)}, u32[]{:S(2)}) async-start(f32[16,128,128]{2,1,0:T(8,128)} %get-tuple-element.65), calls=%async_computation.2 | async-start | bytes 2097152 | tf_op jit(solution)/shard_map/all_to_all | solution.py:473
  145.0 12.4 %all-to-all-start.3 = ((f32[16,8,128]{2,1,0:T(8,128)}), f32[16,8,128]{2,1,0:T(8,128)S(1)}, u32[]{:S(2)}, u32[]{:S(2)}) async-start(f32[16,8,128]{2,1,0:T(8,128)} %get-tuple-element.84), calls=%async_computation.3 | async-start | bytes 131072 | tf_op jit(solution)/shard_map/all_to_all | solution.py:473

commit v7 on v5

--- a/solution.py
+++ b/solution.py
@@ -323,10 +323,9 @@
     early, late = x_tail.astype(BF16), g_grow.astype(BF16)
     b_early, c_late = b_ref[0], c_ref[0]
     gram = dot(c_late, b_early, NT)
-    y, back = 0.0, 0.0
-    for part in split3(gram)[:2]:
-        y = y + exact_dot(part, x_tail, NN)
-        back = back + exact_dot(part, g_grow, TN)
+    top, low, _ = split3(gram)
+    y = exact_dot(top, x_tail, NN) + dot(low, early, NN)
+    back = exact_dot(top, g_grow, TN) + dot(low, late, TN)
     dgram = dot(late, early, NT).astype(BF16)
     dc_ref[0] = dci_ref[0] + dot(dgram, b_early, NN)
     db_ref[0] = dbi_ref[0] + dot(dgram, c_late, TN)

time: 158 us -> 158 us (level)
  transfers between devices with their start and end apart: 7 -> 7, of which waited for: 3 -> 4; matrix products, arithmetic and copies ran while one was open for 1% -> 1% of each run, Pallas kernels for 32% -> 31%
where the time goes in v7:
time: 158 us; the launch traced here: 157 us
  Pallas kernels  67 us (42%)
  blocking collectives  58.7 us (37%)
  starting transfers between devices  21.9 us (14%)
  waiting for transfers between devices  6.04 us (4%)
    all_to_all x1, blocking collectives, exchange(): return lax.all_to_all(value, 'context', 0, 0, axis_index_groups=[order])  58.7 us
    pallas_call x1, Pallas kernels, on_device(): pl.pallas_call(intra_kernel, grid=(seqs, blocks), in_specs=[smem, tok_spe...  17.9 us
    all_to_all x3, starting transfers between devices, exchange(): return lax.all_to_all(value, 'context', 0, 0, axis_index_groups=[order])  16.6 us
    pallas_call x2, Pallas kernels, final(): pl.pallas_call(lambda *refs: final_kernel(unit, heads, *refs), grid=(numb...  13.2 us
    pallas_call x2, Pallas kernels, groups(): pl.pallas_call(lambda *refs: groups_kernel(seq, *refs), grid=(parts,), in...  10.5 us
    pallas_call x1, Pallas kernels, on_device(): pl.pallas_call(cross_kernel, grid=(seqs,), in_specs=[smem, early(width),...  9.67 us
    pallas_call x1, Pallas kernels, on_device(): pl.pallas_call(states_kernel, grid=(seqs + 1,), in_specs=[smem, of_either...  8.21 us
    pallas_call x2, Pallas kernels, chained(): pl.pallas_call(lambda *refs: chain_kernel(unit, heads, *refs), grid=(numb...  7.57 us
  transfers between devices with their start and end apart: 7, of which 4 were waited for; matrix products, arithmetic and copies ran while one was open for 1% of the time, Pallas kernels for 31%

profile of v7, /device:TPU:0, one launch (start us, length us, event | category | flops | bytes accessed | tf_op | source)
XLA Modules:
  0.0 157.0 jit_solution(6860144863100416028)
XLA Ops:
  0.6 8.2 %states.1 = f32[16,520,128]{2,1,0:T(8,128)} custom-call(s32[2]{0:T(128)} %refs_0_.3, bf16[2,512,1024]{2,1,0:T(8,128)(2,1)} %refs_2_.5, bf16[2,512,1024]{2,1,0:T(8,128)(2,1)} %refs_3_.3, bf16[2,512,256]{2,1,0:T(8,128)(2,1)} %refs_4_.3, bf16[2,512,256]{2,1,0:T(8,128)(2,1)} %refs_5_.3, f32[2,16,512]{2,1,0:T(8,128)} %dt_ref.2, f32[1,16]{1,0:T(1,128)} %bitcast.9, ...), custom_call_target="tpu_custom_call" | custom-call | tf_op jit(solution)/shard_map/states/pallas_call | solution.py:505
  8.8 58.7 %all_to_all.20.refs_0_.refs_1_ = f32[16,520,128]{2,1,0:T(8,128)} all-to-all(f32[16,520,128]{2,1,0:T(8,128)} %states.1), channel_id=1, replica_groups={{0,8,16,24,56,48,40,32,64,72,80,88,120,112,104,96},{1,9,17,25,57,49,41,..., dimensions={0} | all-to-all | bytes 8519680 | tf_op jit(solution)/shard_map/all_to_all | solution.py:468
  67.6 4.8 %chain.3 = (f32[16,384,128]{2,1,0:T(8,128)}, f32[8,128]{1,0:T(8,128)}) custom-call(f32[16,520,128]{2,1,0:T(8,128)} %all_to_all.20.refs_0_.refs_1_, f32[16,520,128]{2,1,0:T(8,128)} %all_to_all.20.refs_0_.refs_1_, bf16[2,128,1024]{2,1,0:T(8,128)(2,1)} %constant.16.clone.spread_ref.refs_2_.refs_8_.refs_12_), custom_call_target="tpu_custom_call" | custom-call | tf_op jit(solution)/shard_map/chain/pallas_call | solution.py:524
  72.4 3.9 %all-to-all-start.1 = ((f32[16,384,128]{2,1,0:T(8,128)}), f32[16,384,128]{2,1,0:T(8,128)S(1)}, u32[]{:S(2)}, u32[]{:S(2)}) async-start(f32[16,384,128]{2,1,0:T(8,128)} %get-tuple-element.64), calls=%async_computation.1 | async-start | bytes 6291456 | tf_op jit(solution)/shard_map/all_to_all | solution.py:468
  76.3 0.1 collective-permute-start
  76.4 1.1 collective-permute-done
  77.5 4.0 %collective-permute-start.3 = (f32[2,128]{1,0:T(2,128)S(1)}, f32[2,128]{1,0:T(2,128)S(1)}, u32[]{:S(2)}, u32[]{:S(2)}) collective-permute-start(f32[2,128]{1,0:T(2,128)S(1)} %slice_add_fusion), channel_id=1, source_target_pairs={{0,6},{1,7},{2,0},{3,1},{4,2},{5,3},{6,4},{7,5},{8,14},{9,15},{10,... | collective-permute-start | bytes 3080 | tf_op jit(solution)/shard_map/ppermute | solution.py:477
  81.6 1.3 collective-permute-start.1
  82.8 17.9 %intra.1 = (f32[2,512,1024]{2,1,0:T(8,128)}, f32[2,512,256]{2,1,0:T(8,128)}, f32[2,512,256]{2,1,0:T(8,128)}, f32[2,16,512]{2,1,0:T(8,128)}, f32[2,16,512]{2,1,0:...) custom-call(s32[2]{0:T(128)} %refs_0_.3, ...), custom_call_target="tpu_custom_call" | custom-call | tf_op jit(solution)/shard_map/intra/pallas_call | solution.py:549
  100.7 9.7 %cross.1 = (f32[2,16,512]{2,1,0:T(8,128)}, f32[2,16,512]{2,1,0:T(8,128)}, f32[2,512,1024]{2,1,0:T(8,128)}, f32[2,512,256]{2,1,0:T(8,128)}, f32[2,512,256]{2,1,0:T(8,128)}) custom-call(s32[2]{0:T(128)} %refs_0_.3, bf16[2,512,1024]{2,1,0:T(8,128)(2,1)} %refs_2_.5, ...), custom_call_target="tpu_custom_call", output_to_operand_aliasing={{2}: (10, {}), {3}: (11, {}), {4}: (12, {})} | custom-call | tf_op jit(solution)/shard_map/cross/pallas_call | solution.py:584
  110.4 2.7 %chain.2 = (f32[16,128,128]{2,1,0:T(8,128)}, f32[8,128]{1,0:T(8,128)}) custom-call(f32[16,520,128]{2,1,0:T(8,128)} %all_to_all.20.refs_0_.refs_1_, f32[16,520,128]{2,1,0:T(8,128)} %all_to_all.20.refs_0_.refs_1_, bf16[2,128,1024]{2,1,0:T(8,128)(2,1)} %constant.16.clone.spread_ref.refs_2_.refs_8_.refs_12_), custom_call_target="tpu_custom_call" | custom-call | tf_op jit(solution)/shard_map/chain/pallas_call | solution.py:524
  113.2 0.1 slice_reduce_fusion
  113.3 0.6 multiply_reduce_fusion
  114.6 0.5 fusion.refs_0_.refs_1_
  115.1 0.2 all-to-all-done.1.refs_9_.refs_6_
  115.4 7.8 %all-to-all-start.2 = ((f32[16,128,128]{2,1,0:T(8,128)}), f32[16,128,128]{2,1,0:T(8,128)}, u32[]{:S(2)}, u32[]{:S(2)}) async-start(f32[16,128,128]{2,1,0:T(8,128)} %get-tuple-element.65), calls=%async_computation.2 | async-start | bytes 2097152 | tf_op jit(solution)/shard_map/all_to_all | solution.py:468
  123.2 8.4 %final.2 = (f32[2,16,512]{2,1,0:T(8,128)}, f32[16,8,128]{2,1,0:T(8,128)}, f32[512,128]{1,0:T(8,128)}, f32[8,128]{1,0:T(8,128)}) custom-call(s32[2]{0:T(128)} %refs_0_.3, f32[2]{0:T(128)} %fusion.refs_0_.refs_1_, bf16[2,512,1024]{2,1,0:T(8,128)(2,1)} %refs_2_.5, bf16[2,512,1024]{2,1,0:T(8,128)(2,1)} %refs_3_.3, bf16[2,512,256]{2,1,0:T(8,128)(2,1)} %refs_4_.3, ...), custom_call_target="tpu_custom_call" | custom-call | tf_op jit(solution)/shard_map/final/pallas_call | solution.py:619
  131.7 5.2 %groups.2 = (bf16[2,512,1024]{2,1,0:T(8,128)(2,1)}, bf16[2,512,256]{2,1,0:T(8,128)(2,1)}, bf16[2,512,256]{2,1,0:T(8,128)(2,1)}) custom-call(f32[2]{0:T(128)} %fusion.refs_0_.refs_1_, bf16[2,512,256]{2,1,0:T(8,128)(2,1)} %refs_4_.3, bf16[2,512,128]{2,1,0:T(8,128)(2,1)} %get-tuple-element.58.refs_2_.refs_7_, bf16[2,512,1024]{2,1,0:T(8,128)(2,1)} %get-tuple-element.59.refs_3_, ...), custom_call_target="tpu_custom_call" | custom-call | tf_op jit(solution)/shard_map/groups/pallas_call | solution.py:654
  136.9 2.3 %all-to-all-done.2.refs_10_.refs_6_ = f32[16,128,128]{2,1,0:T(8,128)} async-done(((f32[16,128,128]{2,1,0:T(8,128)}), f32[16,128,128]{2,1,0:T(8,128)}, u32[]{:S(2)}, u32[]{:S(2)}) %all-to-all-start.2) | async-done | bytes 1048608 | tf_op jit(solution)/shard_map/all_to_all | solution.py:468
  139.2 4.8 %final.3 = (f32[2,16,512]{2,1,0:T(8,128)}, f32[16,8,128]{2,1,0:T(8,128)}, f32[512,128]{1,0:T(8,128)}, f32[8,128]{1,0:T(8,128)}) custom-call(s32[2]{0:T(128)} %refs_0_.3, f32[2]{0:T(128)} %fusion.refs_0_.refs_1_, bf16[2,512,1024]{2,1,0:T(8,128)(2,1)} %refs_2_.5, bf16[2,512,1024]{2,1,0:T(8,128)(2,1)} %refs_3_.3, ...), custom_call_target="tpu_custom_call", output_to_operand_aliasing={{0}: (17, {})} | custom-call | tf_op jit(solution)/shard_map/final/pallas_call | solution.py:619
  144.0 4.8 %all-to-all-start.3 = ((f32[16,8,128]{2,1,0:T(8,128)}), f32[16,8,128]{2,1,0:T(8,128)S(1)}, u32[]{:S(2)}, u32[]{:S(2)}) async-start(f32[16,8,128]{2,1,0:T(8,128)} %get-tuple-element.84), calls=%async_computation.3 | async-start | bytes 131072 | tf_op jit(solution)/shard_map/all_to_all | solution.py:468
  148.8 5.3 %groups.3 = (bf16[2,512,1024]{2,1,0:T(8,128)(2,1)}, bf16[2,512,256]{2,1,0:T(8,128)(2,1)}, bf16[2,512,256]{2,1,0:T(8,128)(2,1)}) custom-call(f32[2]{0:T(128)} %fusion.refs_0_.refs_1_, bf16[2,512,256]{2,1,0:T(8,128)(2,1)} %refs_4_.3, ...), custom_call_target="tpu_custom_call", output_to_operand_aliasing={{0}: (11, {}), {1}: (12, {}), {2}: (13, {})} | custom-call | tf_op jit(solution)/shard_map/groups/pallas_call | solution.py:654
  154.1 2.3 %all-to-all-done.3 = f32[16,8,128]{2,1,0:T(8,128)S(1)} async-done(((f32[16,8,128]{2,1,0:T(8,128)}), f32[16,8,128]{2,1,0:T(8,128)S(1)}, u32[]{:S(2)}, u32[]{:S(2)}) %all-to-all-start.3) | async-done | bytes 65568 | tf_op jit(solution)/shard_map/all_to_all | solution.py:468
  156.5 0.5 slice_bitcast_fusion
  (12 shorter events, 0.1 us)
Async XLA Ops:
  72.4 3.9 %copy-start.1 = (f32[8,128]{1,0:T(8,128)S(1)}, f32[8,128]{1,0:T(8,128)}, u32[]{:S(2)}) copy-start(f32[8,128]{1,0:T(8,128)} %get-tuple-element.47) | copy-start | bytes 12292
  72.4 43.0 %all-to-all-start.1 = ((f32[16,384,128]{2,1,0:T(8,128)}), f32[16,384,128]{2,1,0:T(8,128)S(1)}, u32[]{:S(2)}, u32[]{:S(2)}) async-start(f32[16,384,128]{2,1,0:T(8,128)} %get-tuple-element.64), calls=%async_computation.1 | async-start | bytes 6291456 | tf_op jit(solution)/shard_map/all_to_all | solution.py:468
  76.3 1.2 collective-permute-start
  77.5 35.6 %collective-permute-start.3 = (f32[2,128]{1,0:T(2,128)S(1)}, f32[2,128]{1,0:T(2,128)S(1)}, u32[]{:S(2)}, u32[]{:S(2)}) collective-permute-start(f32[2,128]{1,0:T(2,128)S(1)} %slice_add_fusion), channel_id=1, source_target_pairs={{0,6},{1,7},{2,0},{3,1},{4,2},{5,3},{6,4},{7,5},{8,14},{9,15},{10,... | collective-permute-start | bytes 3080 | tf_op jit(solution)/shard_map/ppermute | solution.py:477
  81.6 31.6 %collective-permute-start.2 = (f32[2,128]{1,0:T(2,128)S(1)}, f32[2,128]{1,0:T(2,128)S(1)}, u32[]{:S(2)}, u32[]{:S(2)}) collective-permute-start(f32[2,128]{1,0:T(2,128)S(1)} %slice_add_fusion), channel_id=1, source_target_pairs={{0,4},{1,5},{2,6},{3,7},{4,0},{5,1},{6,2},{7,3},{8,12},{9,13},{10,... | collective-permute-start | bytes 3080 | tf_op jit(solution)/shard_map/ppermute | solution.py:477
  81.6 31.6 %collective-permute-start.1 = (f32[2,128]{1,0:T(2,128)S(1)}, f32[2,128]{1,0:T(2,128)S(1)}, u32[]{:S(2)}, u32[]{:S(2)}) collective-permute-start(f32[2,128]{1,0:T(2,128)S(1)} %slice_add_fusion), channel_id=1, source_target_pairs={{0,2},{1,3},{2,4},{3,5},{4,6},{5,7},{6,0},{7,1},{8,10},{9,11},{10,... | collective-permute-start | bytes 3080 | tf_op jit(solution)/shard_map/ppermute | solution.py:477
  115.4 7.9 %copy-start = (f32[16,384,128]{2,1,0:T(8,128)}, f32[16,384,128]{2,1,0:T(8,128)S(1)}, u32[]{:S(2)}) copy-start(f32[16,384,128]{2,1,0:T(8,128)S(1)} %all-to-all-done.1.refs_9_.refs_6_) | copy-start | bytes 9437188
  115.4 23.8 %all-to-all-start.2 = ((f32[16,128,128]{2,1,0:T(8,128)}), f32[16,128,128]{2,1,0:T(8,128)}, u32[]{:S(2)}, u32[]{:S(2)}) async-start(f32[16,128,128]{2,1,0:T(8,128)} %get-tuple-element.65), calls=%async_computation.2 | async-start | bytes 2097152 | tf_op jit(solution)/shard_map/all_to_all | solution.py:468
  144.0 12.5 %all-to-all-start.3 = ((f32[16,8,128]{2,1,0:T(8,128)}), f32[16,8,128]{2,1,0:T(8,128)S(1)}, u32[]{:S(2)}, u32[]{:S(2)}) async-start(f32[16,8,128]{2,1,0:T(8,128)} %get-tuple-element.84), calls=%async_computation.3 | async-start | bytes 131072 | tf_op jit(solution)/shard_map/all_to_all | solution.py:468
